TPU v7x, 32 devices: a whole 2x2x4 slice. The times are simulated.
32 devices in a mesh: dp: 4 (over y, x), seq: 8 (over z, core).
Axes of the slice: x: 2, y: 2, z: 4, core: 2. Of those that a mesh axis runs over, the one named last changes fastest.
Arguments:
- hidden_in: bfloat16 [8, 4096, 2048], P('dp', 'seq'), may hold values from -6 to 6
- doc_lengths: int32 [8, 8], P('dp'), may hold values from 1 to 4089, as said below
- cotangent: bfloat16 [8, 4096, 2048], P('dp', 'seq'), may hold values from -6 to 6
- ln1_gain: bfloat16 [2048], P(('dp', 'seq')), may hold values from 0.099609375 to 1.8984375
- ln1_bias: bfloat16 [2048], P(('dp', 'seq')), may hold values from -1.5 to 1.5
- w_qkv: bfloat16 [2048, 2304], P(('dp', 'seq')), may hold values from -0.125 to 0.125
- b_qv: bfloat16 [2176], P(('dp', 'seq')), may hold values from -2.5 to 2.5
- w_out: bfloat16 [2048, 2048], P(None, ('dp', 'seq')), may hold values from -1 to 1
- b_out: bfloat16 [2048], P(('dp', 'seq')), may hold values from -2.5 to 2.5
- ln2_gain: bfloat16 [2048], P(('dp', 'seq')), may hold values from 0.099609375 to 1.8984375
- ln2_bias: bfloat16 [2048], P(('dp', 'seq')), may hold values from -1.5 to 1.5
- w_up: bfloat16 [2048, 8192], P(('dp', 'seq')), may hold values from -0.125 to 0.125
- b_up: bfloat16 [8192], P(('dp', 'seq')), may hold values from -2.5 to 2.5
- w_down: bfloat16 [8192, 2048], P(('dp', 'seq')), may hold values from -0.0625 to 0.0625
- b_down: bfloat16 [2048], P(('dp', 'seq')), may hold values from -2.5 to 2.5
Outputs:
- mixed_out: bfloat16 [8, 4096, 2048], P('dp', 'seq')
- grad_hidden: float32 [8, 4096, 2048], P('dp', 'seq')
- grad_ln1_gain: float32 [2048], P(('dp', 'seq'))
- grad_ln1_bias: float32 [2048], P(('dp', 'seq'))
- grad_w_qkv: float32 [2048, 2304], P(('dp', 'seq'))
- grad_b_query: float32 [2048], P(('dp', 'seq'))
- grad_b_value: float32 [128], P(('dp', 'seq'))
- grad_w_out: float32 [2048, 2048], P(None, ('dp', 'seq'))
- grad_b_out: float32 [2048], P(('dp', 'seq'))
- grad_ln2_gain: float32 [2048], P(('dp', 'seq'))
- grad_ln2_bias: float32 [2048], P(('dp', 'seq'))
- grad_w_up: float32 [2048, 8192], P(('dp', 'seq'))
- grad_b_up: float32 [8192], P(('dp', 'seq'))
- grad_w_down: float32 [8192, 2048], P(('dp', 'seq'))
- grad_b_down: float32 [2048], P(('dp', 'seq'))
Inputs may be any that keep to these rules, and one draw needn't show every extreme that they name: `doc_lengths`: the lengths of a window sum to at most 4096; the positions after its last document are padding. Some window holds a document of exactly 4089 tokens.
All inputs are finite; a program needn't handle non-finite values.
Results may differ from a plain program's by a relative error of at most 0.012.
Values may be sent and summed in bfloat16 or wider, within the bound.
No kernel may reach another device: no remote copies, remote signals or barrier semaphores. Data moves between devices by JAX's collectives and lax.ppermute only.
A program may use at most 448 MiB of HBM per device.

v0:
```python
import jax
import jax.numpy as jnp
from jax import lax
from jax.sharding import PartitionSpec as P

HEADS = 16
HD = 128
DOCS = 8


def layer_norm(values, gain_vec, offset):
    centre = jnp.mean(values, axis=-1, keepdims=True)
    centred = values - centre
    spread = jnp.mean(centred * centred, axis=-1, keepdims=True)
    return centred * lax.rsqrt(spread + 1e-05) * gain_vec + offset


def gelu_tanh(values):
    return jax.nn.gelu(values, approximate=True)


def row_sum(values):
    return jnp.sum(values.astype(jnp.float32), axis=0)


def contract_rows(left_op, right_op):
    return lax.dot_general(
        left_op, right_op, (((0,), (0,)), ((), ())), preferred_element_type=jnp.float32
    )


def contract_cols(left_op, right_op):
    return lax.dot_general(
        left_op, right_op, (((1,), (1,)), ((), ())), preferred_element_type=jnp.float32
    )


def key_blocks(keys_all, values_all, key_segs):
    length = keys_all.shape[0]
    block_width = min(512, length)
    blocks = length // block_width
    positions = jnp.arange(length, dtype=jnp.int32)
    return (
        keys_all.reshape(blocks, block_width, -1),
        values_all.reshape(blocks, block_width, -1),
        key_segs.reshape(blocks, block_width),
        positions.reshape(blocks, block_width),
    )


def block_scores(queries, key_block, seg_block, pos_block, query_pos, query_seg):
    scale_factor = queries.shape[1] ** (-0.5)
    scores = contract_cols(queries, key_block) * scale_factor
    allowed = (query_pos[:, None] >= pos_block[None, :]) & (
        query_seg[:, None] == seg_block[None, :]
    )
    return (scores, allowed)


def attend_forward(queries, keys_all, values_all, query_pos, query_seg, key_segs):
    blocks = key_blocks(keys_all, values_all, key_segs)
    row_count = queries.shape[0]

    def gather_stats(state_pair, pieces):
        running_max, running_sum = state_pair
        key_block, value_block, seg_block, pos_block = pieces
        scores, allowed = block_scores(
            queries, key_block, seg_block, pos_block, query_pos, query_seg
        )
        scores = jnp.where(allowed, scores, -1e30)
        new_max = jnp.maximum(running_max, jnp.max(scores, axis=1))
        exponent = jnp.where(allowed, jnp.exp(scores - new_max[:, None]), 0.0)
        running_sum = running_sum * jnp.exp(running_max - new_max) + jnp.sum(exponent, axis=1)
        return ((new_max, running_sum), None)

    initial = (jnp.full((row_count,), -1e30, jnp.float32), jnp.zeros((row_count,), jnp.float32))
    (row_max, row_sum_exp), _ = lax.scan(gather_stats, initial, blocks)
    log_total = row_max + jnp.log(row_sum_exp)

    def accumulate(running, pieces):
        key_block, value_block, seg_block, pos_block = pieces
        scores, allowed = block_scores(
            queries, key_block, seg_block, pos_block, query_pos, query_seg
        )
        block_probs = jnp.where(
            allowed, jnp.exp(jnp.where(allowed, scores, -1e30) - log_total[:, None]), 0.0
        ).astype(jnp.bfloat16)
        return (
            running + jnp.dot(block_probs, value_block, preferred_element_type=jnp.float32),
            None,
        )

    attended, _ = lax.scan(
        accumulate, jnp.zeros((row_count, values_all.shape[1]), jnp.float32), blocks
    )
    return (attended, log_total)


def attend_backward(
    queries,
    keys_all,
    values_all,
    query_pos,
    query_seg,
    key_segs,
    attended,
    log_total,
    grad_attended,
):
    blocks = key_blocks(keys_all, values_all, key_segs)
    row_delta = jnp.sum(grad_attended.astype(jnp.float32) * attended, axis=1)

    def step_back(grad_query, pieces):
        key_block, value_block, seg_block, pos_block = pieces
        scores, allowed = block_scores(
            queries, key_block, seg_block, pos_block, query_pos, query_seg
        )
        block_probs = jnp.where(
            allowed, jnp.exp(jnp.where(allowed, scores, -1e30) - log_total[:, None]), 0.0
        )
        grad_probs = contract_cols(grad_attended, value_block)
        grad_scores = (block_probs * (grad_probs - row_delta[:, None])).astype(jnp.bfloat16)
        grad_query = grad_query + jnp.dot(
            grad_scores, key_block, preferred_element_type=jnp.float32
        )
        grad_key = contract_rows(grad_scores, queries)
        grad_value = contract_rows(block_probs.astype(jnp.bfloat16), grad_attended)
        return (grad_query, (grad_key, grad_value))

    start_grad = jnp.zeros(queries.shape, jnp.float32)
    grad_query, (grad_key, grad_value) = lax.scan(step_back, start_grad, blocks)
    scale_factor = queries.shape[1] ** (-0.5)
    length = keys_all.shape[0]
    return (
        grad_query * scale_factor,
        grad_key.reshape(length, -1) * scale_factor,
        grad_value.reshape(length, -1),
    )


def project_attention(tokens, weights, windows, local_len):
    width_q = HEADS * HD
    normed = layer_norm(
        tokens, weights[0].astype(jnp.float32), weights[1].astype(jnp.float32)
    ).astype(jnp.bfloat16)
    projected = jnp.dot(normed, weights[2], preferred_element_type=jnp.float32)
    bias_all = weights[3].astype(jnp.float32)
    queries = (projected[:, :width_q] + bias_all[:width_q]).astype(jnp.bfloat16)
    own_keys = projected[:, width_q : width_q + HD].astype(jnp.bfloat16)
    own_values = (projected[:, width_q + HD :] + bias_all[width_q:]).astype(jnp.bfloat16)
    keys_all, values_all = (
        lax.all_gather(own_keys.reshape(windows, local_len, HD), "seq", axis=1, tiled=True),
        lax.all_gather(own_values.reshape(windows, local_len, HD), "seq", axis=1, tiled=True),
    )
    return (normed, queries.reshape(windows, local_len * HEADS, HD), keys_all, values_all)


def after_attention(tokens, attended, weights):
    residual = (
        tokens
        + jnp.dot(attended, weights[4], preferred_element_type=jnp.float32)
        + weights[5].astype(jnp.float32)
    )
    mixed_rows = layer_norm(
        residual, weights[6].astype(jnp.float32), weights[7].astype(jnp.float32)
    ).astype(jnp.bfloat16)
    upward = jnp.dot(mixed_rows, weights[8], preferred_element_type=jnp.float32) + weights[
        9
    ].astype(jnp.float32)
    active = gelu_tanh(upward).astype(jnp.bfloat16)
    return (residual, mixed_rows, upward, active)


def body(
    hidden_in,
    doc_lengths,
    cotangent,
    ln1_gain,
    ln1_bias,
    w_qkv,
    b_qv,
    w_out,
    b_out,
    ln2_gain,
    ln2_bias,
    w_up,
    b_up,
    w_down,
    b_down,
):
    windows, local_len, model_width = hidden_in.shape
    token_count = windows * local_len
    width_q = HEADS * HD
    length = local_len * lax.axis_size("seq")
    first_pos = lax.axis_index("seq") * local_len
    doc_ends = jnp.cumsum(doc_lengths, axis=1)
    positions = jnp.arange(length, dtype=jnp.int32)
    key_segs = jnp.sum((positions[None, :, None] >= doc_ends[:, None, :]).astype(jnp.int32), axis=2)
    local_segs = lax.dynamic_slice_in_dim(key_segs, first_pos, local_len, 1)
    query_pos = jnp.repeat(first_pos + jnp.arange(local_len, dtype=jnp.int32), HEADS)
    query_segs = jnp.repeat(local_segs, HEADS, axis=1)
    valid_rows = (local_segs < DOCS).astype(jnp.float32).reshape(token_count, 1)
    tokens = hidden_in.reshape(token_count, model_width).astype(jnp.float32)
    full_fwd = (
        lax.all_gather(ln1_gain, ("dp", "seq"), axis=0, tiled=True),
        lax.all_gather(ln1_bias, ("dp", "seq"), axis=0, tiled=True),
        lax.all_gather(w_qkv, ("dp", "seq"), axis=0, tiled=True),
        lax.all_gather(b_qv, ("dp", "seq"), axis=0, tiled=True),
        lax.all_gather(w_out, ("dp", "seq"), axis=1, tiled=True),
        lax.all_gather(b_out, ("dp", "seq"), axis=0, tiled=True),
        lax.all_gather(ln2_gain, ("dp", "seq"), axis=0, tiled=True),
        lax.all_gather(ln2_bias, ("dp", "seq"), axis=0, tiled=True),
        lax.all_gather(w_up, ("dp", "seq"), axis=0, tiled=True),
        lax.all_gather(b_up, ("dp", "seq"), axis=0, tiled=True),
        lax.all_gather(w_down, ("dp", "seq"), axis=0, tiled=True),
        lax.all_gather(b_down, ("dp", "seq"), axis=0, tiled=True),
    )
    normed_one, queries, keys_all, values_all = project_attention(
        tokens, full_fwd, windows, local_len
    )
    attended_full, log_total = lax.map(
        lambda pieces: attend_forward(
            pieces[0], pieces[1], pieces[2], query_pos, pieces[3], pieces[4]
        ),
        (queries, keys_all, values_all, query_segs, key_segs),
    )
    attended = attended_full.astype(jnp.bfloat16).reshape(token_count, width_q)
    residual, mixed_rows, upward, active = after_attention(tokens, attended, full_fwd)
    mixed_out = (
        (
            residual
            + jnp.dot(active, full_fwd[10], preferred_element_type=jnp.float32)
            + full_fwd[11].astype(jnp.float32)
        )
        .astype(jnp.bfloat16)
        .reshape(windows, local_len, model_width)
    )
    full_bwd = (
        lax.all_gather(ln1_gain, ("dp", "seq"), axis=0, tiled=True),
        lax.all_gather(ln1_bias, ("dp", "seq"), axis=0, tiled=True),
        lax.all_gather(w_qkv, ("dp", "seq"), axis=0, tiled=True),
        lax.all_gather(b_qv, ("dp", "seq"), axis=0, tiled=True),
        lax.all_gather(w_out, ("dp", "seq"), axis=1, tiled=True),
        lax.all_gather(b_out, ("dp", "seq"), axis=0, tiled=True),
        lax.all_gather(ln2_gain, ("dp", "seq"), axis=0, tiled=True),
        lax.all_gather(ln2_bias, ("dp", "seq"), axis=0, tiled=True),
        lax.all_gather(w_up, ("dp", "seq"), axis=0, tiled=True),
        lax.all_gather(b_up, ("dp", "seq"), axis=0, tiled=True),
        lax.all_gather(w_down, ("dp", "seq"), axis=0, tiled=True),
        lax.all_gather(b_down, ("dp", "seq"), axis=0, tiled=True),
    )
    normed_one, queries, keys_all, values_all = project_attention(
        tokens, full_bwd, windows, local_len
    )
    residual, mixed_rows, upward, active = after_attention(tokens, attended, full_bwd)
    upstream = cotangent.reshape(token_count, model_width).astype(jnp.float32) * valid_rows
    grad_down = upstream.astype(jnp.bfloat16)
    grad_b_down = row_sum(grad_down)
    grad_w_down = contract_rows(active, grad_down)
    grad_active = contract_cols(grad_down, full_bwd[10])
    _, gelu_pull = jax.vjp(gelu_tanh, upward)
    grad_up = gelu_pull(grad_active)[0].astype(jnp.bfloat16)
    grad_b_up = row_sum(grad_up)
    grad_w_up = contract_rows(mixed_rows, grad_up)
    grad_mixed = contract_cols(grad_up, full_bwd[8])
    _, norm_pull = jax.vjp(
        layer_norm, residual, full_bwd[6].astype(jnp.float32), full_bwd[7].astype(jnp.float32)
    )
    grad_res, grad_ln2_gain, grad_ln2_bias = norm_pull(grad_mixed)
    grad_res = grad_res + upstream
    grad_branch = grad_res.astype(jnp.bfloat16)
    grad_b_out = row_sum(grad_branch)
    grad_w_out = contract_rows(attended, grad_branch)
    grad_att = contract_cols(grad_branch, full_bwd[4]).astype(jnp.bfloat16)
    grad_query, grad_key, grad_value = lax.map(
        lambda pieces: attend_backward(
            pieces[0],
            pieces[1],
            pieces[2],
            query_pos,
            pieces[3],
            pieces[4],
            pieces[5],
            pieces[6],
            pieces[7],
        ),
        (
            queries,
            keys_all,
            values_all,
            query_segs,
            key_segs,
            attended_full,
            log_total,
            grad_att.reshape(windows, local_len * HEADS, HD),
        ),
    )
    own_key_grad, own_value_grad = (
        lax.psum_scatter(
            grad_key.astype(jnp.bfloat16), "seq", scatter_dimension=1, tiled=True
        ).astype(jnp.float32),
        lax.psum_scatter(
            grad_value.astype(jnp.bfloat16), "seq", scatter_dimension=1, tiled=True
        ).astype(jnp.float32),
    )
    grad_qkv = jnp.concatenate(
        [
            grad_query.reshape(token_count, width_q),
            own_key_grad.reshape(token_count, HD),
            own_value_grad.reshape(token_count, HD),
        ],
        axis=1,
    ).astype(jnp.bfloat16)
    grad_w_qkv = contract_rows(normed_one, grad_qkv)
    column_sums = row_sum(grad_qkv)
    grad_b_query = column_sums[:width_q]
    grad_b_value = column_sums[width_q + HD :]
    grad_normed = contract_cols(grad_qkv, full_bwd[2])
    _, first_pull = jax.vjp(
        layer_norm, tokens, full_bwd[0].astype(jnp.float32), full_bwd[1].astype(jnp.float32)
    )
    grad_tok, grad_ln1_gain, grad_ln1_bias = first_pull(grad_normed)
    grad_hidden = (grad_res + grad_tok).reshape(windows, local_len, model_width)
    result = (
        lax.psum_scatter(grad_ln1_gain, ("dp", "seq"), scatter_dimension=0, tiled=True),
        lax.psum_scatter(grad_ln1_bias, ("dp", "seq"), scatter_dimension=0, tiled=True),
        lax.psum_scatter(grad_w_qkv, ("dp", "seq"), scatter_dimension=0, tiled=True),
        lax.psum_scatter(grad_b_query, ("dp", "seq"), scatter_dimension=0, tiled=True),
        lax.psum_scatter(grad_b_value, ("dp", "seq"), scatter_dimension=0, tiled=True),
        lax.psum_scatter(grad_w_out, ("dp", "seq"), scatter_dimension=1, tiled=True),
        lax.psum_scatter(grad_b_out, ("dp", "seq"), scatter_dimension=0, tiled=True),
        lax.psum_scatter(grad_ln2_gain, ("dp", "seq"), scatter_dimension=0, tiled=True),
        lax.psum_scatter(grad_ln2_bias, ("dp", "seq"), scatter_dimension=0, tiled=True),
        lax.psum_scatter(grad_w_up, ("dp", "seq"), scatter_dimension=0, tiled=True),
        lax.psum_scatter(grad_b_up, ("dp", "seq"), scatter_dimension=0, tiled=True),
        lax.psum_scatter(grad_w_down, ("dp", "seq"), scatter_dimension=0, tiled=True),
        lax.psum_scatter(grad_b_down, ("dp", "seq"), scatter_dimension=0, tiled=True),
    )
    return (
        mixed_out,
        grad_hidden,
        result[0],
        result[1],
        result[2],
        result[3],
        result[4],
        result[5],
        result[6],
        result[7],
        result[8],
        result[9],
        result[10],
        result[11],
        result[12],
    )


def solution(mesh):
    placed = (
        P("dp", "seq", None),
        P("dp", None),
        P("dp", "seq", None),
        P(("dp", "seq")),
        P(("dp", "seq")),
        P(("dp", "seq"), None),
        P(("dp", "seq")),
        P(None, ("dp", "seq")),
        P(("dp", "seq")),
        P(("dp", "seq")),
        P(("dp", "seq")),
        P(("dp", "seq"), None),
        P(("dp", "seq")),
        P(("dp", "seq"), None),
        P(("dp", "seq")),
    )
    return jax.shard_map(
        body,
        mesh=mesh,
        in_specs=placed,
        out_specs=(
            P("dp", "seq", None),
            P("dp", "seq", None),
            P(("dp", "seq")),
            P(("dp", "seq")),
            P(("dp", "seq"), None),
            P(("dp", "seq")),
            P(("dp", "seq")),
            P(None, ("dp", "seq")),
            P(("dp", "seq")),
            P(("dp", "seq")),
            P(("dp", "seq")),
            P(("dp", "seq"), None),
            P(("dp", "seq")),
            P(("dp", "seq"), None),
            P(("dp", "seq")),
        ),
        check_vma=False,
    )
```

profile of v0, /device:TPU:0, one launch (start us, length us, event | category | flops | bytes accessed | tf_op | source)
XLA Modules:
  0.0 3671.5 jit_solution(8182547551401550134)
XLA Ops:
  13.9 43.2 %all-reduce.17 = (bf16[2048]{0:T(1024)(128)(2,1)S(1)}, bf16[2048]{0:T(1024)(128)(2,1)S(1)}, bf16[2048]{0:T(1024)(128)(2,1)S(1)}, bf16[2176]{0:T(1024)(128)(2,1)S...) all-reduce(bf16[2048]{0:T(1024)(128)(2,1)S(1)} %dynamic-update-slic, ...), channel_id=1, replica_groups=mesh['dp'=4,'seq'=8] {'dp','seq'}, use_global_device_ids=true, to_apply=%add.3 | all-reduce | flops 14464 | bytes 57856
  67.9 28.3 all-gather.8.cloned.1.call-done
  125.0 39.8 %all-gather = bf16[32,1,256]{2,1,0:T(2,128)(2,1)S(1)} all-gather(bf16[1,1,256]{2,1,0:T(2,128)(2,1)S(1)} %reshape.267), channel_id=1, replica_groups=mesh['dp'=4,'seq'=8] {'dp','seq'}, dimensions={0}, use_global_device_ids=true | all-gather | bytes 16896 | tf_op jit(solution)/shard_map/all_gather | solution.py:214
  185.0 541.1 %while.83 = (s32[]{:T(128)}, f32[2,8192,128]{2,1,0:T(8,128)}, f32[2,8192]{1,0:T(2,128)}, bf16[2,4096,128]{2,1,0:T(8,128)(2,1)}, bf16[2,4096,128]{2,1,0:T(8,128)(...) while((s32[]{:T(128)}, f32[2,8192,128]{2,1,0:T(8,128)}, ...), condition=%wide.region_11.12_spmd.clone.clone, body=%wide.region_4.11_spmd.clone.sunk.clone | while | flops 3315654656 | bytes 65126616 | solution.py:221
  191.9 146.1 %while.81 = (s32[]{:T(128)}, f32[8192]{0:T(1024)S(1)}, f32[8192]{0:T(1024)S(1)}, s32[512,16]{1,0:T(8,128)}, s32[8,512]{1,0:T(8,128)S(1)}, /*index=5*/s32[8192]{0...) while((s32[]{:T(128)}, f32[8192]{0:T(1024)S(1)}, ...), condition=%wide.wide.region_8.8_spmd.clone, body=%wide.wide.region_5.7_spmd.clone.sunk | while | flops 1132503040 | bytes 36356236 | solution.py:77
  339.0 109.5 %while.82 = (s32[]{:T(128)}, f32[8192,128]{1,0:T(8,128)}, s32[512,16]{1,0:T(8,128)}, s32[8,512]{1,0:T(8,128)S(1)}, s32[8192]{0:T(1024)S(1)}, /*index=5*/s32[8,51...) while((s32[]{:T(128)}, f32[8192,128]{1,0:T(8,128)}, ...), condition=%wide.wide.region_10.10_spmd.clone, body=%wide.wide.region_9.9_spmd.clone.sunk | while | flops 2183135232 | bytes 10860178 | solution.py:93
  461.9 149.8 %while.81 = (s32[]{:T(128)}, f32[8192]{0:T(1024)S(1)}, f32[8192]{0:T(1024)S(1)}, s32[512,16]{1,0:T(8,128)}, s32[8,512]{1,0:T(8,128)S(1)}, /*index=5*/s32[8192]{0...) while((s32[]{:T(128)}, f32[8192]{0:T(1024)S(1)}, ...), condition=%wide.wide.region_8.8_spmd.clone, body=%wide.wide.region_5.7_spmd.clone.sunk | while | flops 1132503040 | bytes 36356236 | solution.py:77
  612.8 107.1 %while.82 = (s32[]{:T(128)}, f32[8192,128]{1,0:T(8,128)}, s32[512,16]{1,0:T(8,128)}, s32[8,512]{1,0:T(8,128)S(1)}, s32[8192]{0:T(1024)S(1)}, /*index=5*/s32[8,51...) while((s32[]{:T(128)}, f32[8192,128]{1,0:T(8,128)}, ...), condition=%wide.wide.region_10.10_spmd.clone, body=%wide.wide.region_9.9_spmd.clone.sunk | while | flops 2183135232 | bytes 10860178 | solution.py:93
  757.8 43.1 %fusion.78 = f32[1024,8192]{1,0:T(8,128)} fusion(bf16[2048,8192]{1,0:T(8,128)(2,1)} %all-gather.16.cloned.1.call-done, f32[1024,2048]{1,0:T(8,128)} %copy-done.9, f32[2048]{0:T(1024)S(1)} %copy-done.55, f32[2048]{0:T(1024)S(1)} %copy-done.47, f32[1024]{0:T(1024)S(1)} %fusion.71, f32[1024]{0:T(1024)S(1)} %broadcast_multiply_fusion.1), kind=kOutput, calls=%fused_computation.147 | convolution fusion | flops 34370224128 | bytes 75522048 | tf_op jit(solution)/shard_map/dot_general | solution.py:167
  800.9 65.6 %convert_reduce_fusion = (f32[8192]{0:T(1024)}, bf16[1024,8192]{1,0:T(8,128)(2,1)}) fusion(f32[1024,8192]{1,0:T(8,128)} %fusion.78, f32[8192]{0:T(1024)S(1)} %bitcast.341, bf16[1024,2048]{1,0:T(8,128)(2,1)} %fusion.68, bf16[8192,2048]{1,0:T(8,128)(2,1)} %all-gather.18.cloned.1.call-done), kind=kOutput, calls=%fused_computation.86 | convolution fusion | flops 34552668160 | bytes 88145920 | tf_op jit(solution)/shard_map/dot_general | solution.py:33
  866.5 47.4 %multiply_reduce_fusion = (f32[2048]{0:T(1024)}, f32[1024]{0:T(1024)S(1)}, f32[2048]{0:T(1024)}, f32[1024,2048]{1,0:T(8,128)}) fusion(f32[1024,2048]{1,0:T(8,128)} %copy-done.9, f32[1024]{0:T(1024)S(1)} %fusion.71, f32[1024]{0:T(1024)S(1)} %broadcast_multiply_fusion.1, f32[2048]{0:T(1024)S(1)} %copy-done.47, bf16[1024,8192]{1,0:T(8,128)(2,1)} %get-tuple-element.644, ...), kind=kOutput, calls=%fused_computation.112 | convolution fusion | flops 34376515584 | bytes 67145728 | tf_op jit(solution)/shard_map/dot_general | solution.py:33
  944.9 676.5 %while.85 = (s32[]{:T(128)}, bf16[2,8192,128]{2,1,0:T(8,128)(2,1)}, bf16[2,4096,128]{2,1,0:T(8,128)(2,1)}, bf16[2,4096,128]{2,1,0:T(8,128)(2,1)}, bf16[2,4096,12...) while((s32[]{:T(128)}, bf16[2,8192,128]{2,1,0:T(8,128)(2,1)}, ...), condition=%wide.region_20.21_spmd.clone.clone, body=%wide.region_16.20_spmd.clone.sunk.clone | while | flops 5422186496 | bytes 291994400 | solution.py:275
  958.2 317.5 %while.84 = (s32[]{:T(128)}, f32[8192,128]{1,0:T(8,128)}, f32[8,512,128]{2,1,0:T(8,128)}, bf16[8,512,128]{2,1,0:T(8,128)(2,1)}, s32[512,16]{1,0:T(8,128)}, /*ind...) while((s32[]{:T(128)}, f32[8192,128]{1,0:T(8,128)}, ...), condition=%wide.wide.region_19.19_spmd.clone, body=%wide.wide.region_18.18_spmd.clone.sunk | while | flops 5416943616 | bytes 160444624 | solution.py:131
  1296.3 317.5 %while.84 = (s32[]{:T(128)}, f32[8192,128]{1,0:T(8,128)}, f32[8,512,128]{2,1,0:T(8,128)}, bf16[8,512,128]{2,1,0:T(8,128)(2,1)}, s32[512,16]{1,0:T(8,128)}, /*ind...) while((s32[]{:T(128)}, f32[8192,128]{1,0:T(8,128)}, ...), condition=%wide.wide.region_19.19_spmd.clone, body=%wide.wide.region_18.18_spmd.clone.sunk | while | flops 5416943616 | bytes 160444624 | solution.py:131
  1633.3 22.5 reduce-scatter.9.cloned.1.call-done
  1655.8 37.3 %reduce-scatter.7.cloned.1.call-done = bf16[2,512,128]{2,1,0:T(8,128)(2,1)} async-done(((bf16[2,4096,128]{2,1,0:T(8,128)(2,1)}), bf16[2,512,128]{2,1,0:T(8,128)(2,1)}) %reduce-scatter.7.cloned.1.call-update) | async-done | bytes 262160 | tf_op jit(solution)/shard_map/reduce_scatter | solution.py:299
  1717.6 17.2 fusion.74
  1751.0 48.0 %fusion.77 = f32[2048,8192]{1,0:T(8,128)} fusion(bf16[1024,8192]{1,0:T(8,128)(2,1)} %get-tuple-element.644, f32[1024,2048]{1,0:T(8,128)} %copy-done.9, f32[2048]{0:T(1024)S(1)} %copy-done.56, f32[2048]{0:T(1024)S(1)} %copy-done.48, f32[1024]{0:T(1024)S(1)} %copy-done.53, f32[1024]{0:T(1024)S(1)} %copy-done.38), kind=kOutput, calls=%fused_computation.146 | convolution fusion | flops 34370224128 | bytes 92299264 | tf_op jit(solution)/shard_map/dot_general | solution.py:27
  1799.7 54.0 %fusion.79 = f32[8192,2048]{1,0:T(8,128)} fusion(bf16[1024,2048]{1,0:T(8,128)(2,1)} %fusion.68, f32[1024,8192]{1,0:T(8,128)} %fusion.78, f32[8192]{0:T(1024)S(1)} %bitcast.342), kind=kOutput, calls=%fused_computation.148 | convolution fusion | flops 34443624448 | bytes 104890368 | tf_op jit(solution)/shard_map/dot_general | solution.py:27
  1854.4 58.9 %add_convert_fusion = bf16[1024,2048]{1,0:T(8,128)(2,1)} fusion(f32[1024,2048]{1,0:T(8,128)} %copy-done.9, f32[2048]{0:T(1024)S(1)} %convert_element_type.152, bf16[8192,2048]{1,0:T(8,128)(2,1)} %all-gather.18.cloned.1.call-done, f32[1024,8192]{1,0:T(8,128)} %fusion.78, f32[8192]{0:T(1024)S(1)} %bitcast.343), kind=kOutput, calls=%fused_computation.117 | convolution fusion | flops 34449915904 | bytes 79732736 | tf_op jit(solution)/shard_map/dot_general | solution.py:232
  1938.3 118.7 %reduce-scatter.11.cloned.1.call-done = f32[64,2304]{1,0:T(8,128)} async-done(((f32[2048,2304]{1,0:T(8,128)}), f32[64,2304]{1,0:T(8,128)}) %reduce-scatter.11.cloned.1.call-update) | async-done | bytes 589840 | tf_op jit(solution)/shard_map/reduce_scatter | solution.py:327
  2057.0 188.5 %reduce-scatter.13.cloned.1.call-done = f32[2048,64]{0,1:T(8,128)} async-done(((f32[2048,2048]{0,1:T(8,128)}), f32[2048,64]{0,1:T(8,128)}) %reduce-scatter.13.cloned.1.call-update) | async-done | bytes 524304 | tf_op jit(solution)/shard_map/reduce_scatter | solution.py:330
  2245.6 710.0 %reduce-scatter.15.cloned.1.call-done = f32[64,8192]{1,0:T(8,128)} async-done(((f32[2048,8192]{1,0:T(8,128)}), f32[64,8192]{1,0:T(8,128)}) %reduce-scatter.15.cloned.1.call-update) | async-done | bytes 2097168 | tf_op jit(solution)/shard_map/reduce_scatter | solution.py:334
  2955.6 709.0 %reduce-scatter.17.cloned.1.call-done = f32[256,2048]{1,0:T(8,128)} async-done(((f32[8192,2048]{1,0:T(8,128)}), f32[256,2048]{1,0:T(8,128)}) %reduce-scatter.17.cloned.1.call-update) | async-done | bytes 2097168 | tf_op jit(solution)/shard_map/reduce_scatter | solution.py:336
  (583 shorter events, 1423.0 us)
Async XLA Ops:
  7.2 89.0 %all-gather.8.cloned.1.call-start = ((), (), s32[]{:S(2)}) async-start(), calls=%async_computation.6 | async-start | bytes 9732096 | tf_op jit(solution)/shard_map/all_gather | solution.py:207
  7.9 177.1 %all-gather.10.cloned.1.call-start = ((), (), s32[]{:S(2)}) async-start(), calls=%async_computation.7 | async-start | bytes 2359296 | tf_op jit(solution)/shard_map/all_gather | solution.py:152
  114.0 71.0 %all-gather.12.cloned.1.call-start = ((), (), s32[]{:S(2)}) async-start(), calls=%async_computation.8 | async-start | bytes 2359296 | tf_op jit(solution)/shard_map/all_gather | solution.py:153
  115.9 623.5 %all-gather.14.cloned.1.call-start = ((), (), s32[]{:S(2)}) async-start(), calls=%async_computation.9 | async-start | bytes 8650752 | tf_op jit(solution)/shard_map/all_gather | solution.py:209
  116.4 641.3 %all-gather.16.cloned.1.call-start = ((), (), s32[]{:S(2)}) async-start(), calls=%async_computation.10 | async-start | bytes 34603008 | tf_op jit(solution)/shard_map/all_gather | solution.py:213
  117.0 683.9 %all-gather.18.cloned.1.call-start = ((), (), s32[]{:S(2)}) async-start(), calls=%async_computation.11 | async-start | bytes 34603008 | tf_op jit(solution)/shard_map/all_gather | solution.py:215
  117.6 1538.2 %reduce-scatter.9.cloned.1.call-start = ((), (), s32[]{:S(2)}) async-start(), calls=%async_computation.13 | async-start | bytes 2359296 | tf_op jit(solution)/shard_map/reduce_scatter | solution.py:302
  752.9 161.1 %copy-start.37 = (f32[1024]{0:T(1024)}, f32[1024]{0:T(1024)S(1)}, u32[]{:S(2)}) copy-start(f32[1024]{0:T(1024)S(1)} %broadcast_multiply_fusion.1) | copy-start | bytes 12292
  757.7 156.3 %copy-start.52 = (f32[1024]{0:T(1024)}, f32[1024]{0:T(1024)S(1)}, u32[]{:S(2)}) copy-start(f32[1024]{0:T(1024)S(1)} %fusion.71) | copy-start | bytes 12292
  944.9 677.4 %copy-start.51 = (f32[2,512]{1,0:T(2,128)S(1)}, f32[2,512]{1,0:T(2,128)}, u32[]{:S(2)}) copy-start(f32[2,512]{1,0:T(2,128)} %get-tuple-element.641) | copy-start | bytes 12292
  1621.5 71.6 %reduce-scatter.7.cloned.1.call-start = ((), (), s32[]{:S(2)}) async-start(), calls=%async_computation.12 | async-start | bytes 2359296 | tf_op jit(solution)/shard_map/reduce_scatter | solution.py:299
  1622.2 304.7 %all-reduce.20.cloned.1.call-start = ((), (), s32[]{:S(2)}) async-start(), calls=%async_computation.18 | async-start | bytes 181248
  1622.3 74.9 %copy-start.26 = (f32[2048]{0:T(1024)S(1)}, f32[2048]{0:T(1024)}, u32[]{:S(2)}) copy-start(f32[2048]{0:T(1024)} %copy-done.25) | copy-start | bytes 24580
  1622.3 74.9 %copy-start.32 = (f32[1,4,2,128]{3,1,2,0:T(4,128)S(1)}, f32[1,4,2,128]{3,1,2,0:T(4,128)}, u32[]{:S(2)}) copy-start(f32[1,4,2,128]{3,1,2,0:T(4,128)} %copy-done.31) | copy-start | bytes 12292
  1717.5 339.5 %reduce-scatter.11.cloned.1.call-start = ((), (), s32[]{:S(2)}) async-start(), calls=%async_computation.14 | async-start | bytes 19464192 | tf_op jit(solution)/shard_map/reduce_scatter | solution.py:327
  1734.8 510.7 %reduce-scatter.13.cloned.1.call-start = ((), (), s32[]{:S(2)}) async-start(), calls=%async_computation.15 | async-start | bytes 17301504 | tf_op jit(solution)/shard_map/reduce_scatter | solution.py:330
  1750.3 1205.3 %reduce-scatter.15.cloned.1.call-start = ((), (), s32[]{:S(2)}) async-start(), calls=%async_computation.16 | async-start | bytes 69206016 | tf_op jit(solution)/shard_map/reduce_scatter | solution.py:334
  1799.0 1865.5 %reduce-scatter.17.cloned.1.call-start = ((), (), s32[]{:S(2)}) async-start(), calls=%async_computation.17 | async-start | bytes 69206016 | tf_op jit(solution)/shard_map/reduce_scatter | solution.py:336
  1854.4 59.0 %copy-start.27 = (f32[2048]{0:T(1024)S(1)}, f32[2048]{0:T(1024)}, u32[]{:S(2)}) copy-start(f32[2048]{0:T(1024)} %copy-done.25) | copy-start | bytes 24580
  1854.4 59.0 %copy-start.30 = (f32[1024]{0:T(1024)S(1)}, f32[1024]{0:T(1024)}, u32[]{:S(2)}) copy-start(f32[1024]{0:T(1024)} %copy-done.28) | copy-start | bytes 12292
  1854.4 59.0 %copy-start.33 = (f32[1,4,2,128]{3,1,2,0:T(4,128)S(1)}, f32[1,4,2,128]{3,1,2,0:T(4,128)}, u32[]{:S(2)}) copy-start(f32[1,4,2,128]{3,1,2,0:T(4,128)} %copy-done.31) | copy-start | bytes 12292
  1854.4 59.0 %copy-start.36 = (f32[1,4,2,128]{3,1,2,0:T(4,128)S(1)}, f32[1,4,2,128]{3,1,2,0:T(4,128)}, u32[]{:S(2)}) copy-start(f32[1,4,2,128]{3,1,2,0:T(4,128)} %copy-done.34) | copy-start | bytes 12292
  1854.4 59.0 %copy-start.42 = (f32[1024]{0:T(1024)S(1)}, f32[1024]{0:T(1024)}, u32[]{:S(2)}) copy-start(f32[1024]{0:T(1024)} %copy-done.41) | copy-start | bytes 12292
  1854.4 59.0 %copy-start.44 = (f32[1024]{0:T(1024)S(1)}, f32[1024]{0:T(1024)}, u32[]{:S(2)}) copy-start(f32[1024]{0:T(1024)} %copy-done.43) | copy-start | bytes 12292
  (78 other events, 781.6 us)
Sparse Core Ops, SparseCore 0:
  11.0 85.1 all-gather.7
  114.1 27.8 all-gather.9
  144.2 28.5 all-gather.11
  175.7 76.8 all-gather.13
  255.4 193.3 all-gather.15
  451.6 192.9 all-gather.17
  1621.6 34.1 reduce-scatter.8
  1658.6 34.4 reduce-scatter.6
  1717.6 123.6 all-reduce.19
  1849.2 207.7 reduce-scatter.10
  2060.0 185.5 reduce-scatter.12
  2248.5 707.0 reduce-scatter.14
  2958.6 705.8 reduce-scatter.16
where the time goes:
time: 3680 us; the launch traced here: 3670 us
  waiting for transfers between devices  1820 us (49%)
  matrix products  1380 us (38%)
  other arithmetic  225 us (6%)
  local copies, waits for them, and re-layouts  148 us (4%)
  blocking collectives  83.1 us (2%)
    reduce_scatter x1, waiting for transfers between devices, body(): lax.psum_scatter(grad_w_up, ('dp', 'seq'), scatter_dimension=0, tiled=True)  710 us
    reduce_scatter x1, waiting for transfers between devices, body(): lax.psum_scatter(grad_w_down, ('dp', 'seq'), scatter_dimension=0, tiled=T...  709 us
    dot_general x52, matrix products, contract_cols(): lax.dot_general(left_op, right_op, (((1,), (1,)), ((), ())), preferred_el...  597 us
    dot_general x36, matrix products, contract_rows(): lax.dot_general(left_op, right_op, (((0,), (0,)), ((), ())), preferred_el...  305 us
    dot_general x16, matrix products, accumulate(): jnp.dot(block_probs, value_block, preferred_element_type=jnp.float32)  205 us
    reduce_scatter x1, waiting for transfers between devices, body(): lax.psum_scatter(grad_w_out, ('dp', 'seq'), scatter_dimension=1, tiled=True)  189 us
    dot_general x16, matrix products, step_back(): jnp.dot(grad_scores, key_block, preferred_element_type=jnp.float32)  146 us
    reduce_sum x16, other arithmetic, gather_stats(): jnp.sum(exponent, axis=1)  144 us
  transfers between devices with their start and end apart: 13, of which 7 were waited for; matrix products, arithmetic and copies ran while one was open for 24% of the time, Pallas kernels for 0%

commit v1 on v0

v1 whole, which is shorter than its diff:
```python
import functools

import jax
import jax.numpy as jnp
from jax import lax
from jax.experimental import pallas as pl
from jax.experimental.pallas import tpu as pltpu
from jax.sharding import Mesh
from jax.sharding import PartitionSpec as P

HEADS = 16
HD = 128
DOCS = 8
LOG2E = 1.4426950408889634
CHIPS = ("y", "x", "z")
EVERY = ("y", "x", "z", "core")
PAIR = [(0, 1), (1, 0)]
BF16 = jnp.bfloat16
F32 = jnp.float32


def key_place(j, tk, nums, w, i, chips_z, chip_len):
    first = j * tk
    owner = first // chip_len
    slot = lax.rem(nums[w, i, 5] - owner + chips_z, chips_z)
    return slot, pl.multiple_of(first - owner * chip_len, tk), first


def forward_kernel(tq, tk, heads, deps, nums, q_ref, k_ref, v_ref, start_ref, *refs):
    o_ref, lse_ref, acc, top, bias = refs[deps:]
    w, i = pl.program_id(0), pl.program_id(1)
    t0, lo, hi, full_lo, full_hi = (nums[w, i, n] for n in range(5))
    factor = HD**-0.5 * LOG2E
    acc[...] = jnp.zeros_like(acc)
    top[...] = jnp.full_like(top, -1e20)
    ones = jnp.ones((tk, HD), BF16)

    def tile(j, masked):
        slot, row, k0 = key_place(j, tk, nums, w, i, k_ref.shape[0], k_ref.shape[2])
        keys = k_ref[slot, 0, pl.ds(row, tk), :]
        values = jnp.concatenate([v_ref[slot, 0, pl.ds(row, tk), :], ones], axis=1)
        if masked:
            key_pos = k0 + lax.broadcasted_iota(jnp.int32, (tq, tk), 1)
            query_pos = t0 + lax.broadcasted_iota(jnp.int32, (tq, tk), 0)
            allowed = (key_pos <= query_pos) & (key_pos >= start_ref[...][:, :1])
            bias[...] = jnp.where(allowed, 0.0, -1e30)
        for h in range(heads):
            queries = q_ref[:, h * HD : (h + 1) * HD]
            scores = contract_cols(queries, keys) * factor
            if masked:
                scores = scores + bias[...]
            old = top[h]
            new = jnp.maximum(old, jnp.max(scores, axis=1, keepdims=True))
            probs = jnp.exp2(scores - jnp.concatenate([new] * (tk // HD), axis=1)).astype(BF16)
            fade = jnp.exp2(old - new)
            top[h] = new
            acc[h] = acc[h] * jnp.concatenate([fade, fade], axis=1) + plain_dot(probs, values)

    def step(j, carry):
        partial = (j < full_lo) | (j >= full_hi)

        @pl.when(partial)
        def _():
            tile(j, True)

        @pl.when(jnp.logical_not(partial))
        def _():
            tile(j, False)

        return carry

    lax.fori_loop(lo, hi, step, 0)
    lane = lax.broadcasted_iota(jnp.int32, (tq, HD), 1)
    stats = jnp.zeros((tq, HD), F32)
    for h in range(heads):
        total = acc[h, :, HD:]
        o_ref[:, h * HD : (h + 1) * HD] = (acc[h, :, :HD] / total).astype(BF16)
        stats = jnp.where(lane == h, top[h] + jnp.log2(total), stats)
    lse_ref[...] = jnp.transpose(stats)[:heads]


def attend_forward(queries, keys, values, starts, nums, tq, tk, deps=()):
    chips_z, windows, chip_len, _ = keys.shape
    rows, width = queries.shape
    heads = width // HD
    tiles = rows // windows // tq

    def block(w, i):
        return w * tiles + i

    spread = jnp.broadcast_to(starts.reshape(rows, 1), (rows, HD))
    key_spec = pl.BlockSpec((chips_z, 1, chip_len, HD), lambda w, i, n: (0, w, 0, 0))
    return pl.pallas_call(
        functools.partial(forward_kernel, tq, tk, heads, len(deps)),
        grid_spec=pltpu.PrefetchScalarGridSpec(
            num_scalar_prefetch=1,
            grid=(windows, tiles),
            in_specs=[
                pl.BlockSpec((tq, width), lambda w, i, n: (block(w, i), 0)),
                key_spec,
                key_spec,
                pl.BlockSpec((tq, HD), lambda w, i, n: (block(w, i), 0)),
            ]
            + [pl.BlockSpec(memory_space=pl.ANY)] * len(deps),
            out_specs=[
                pl.BlockSpec((tq, width), lambda w, i, n: (block(w, i), 0)),
                pl.BlockSpec((heads, tq), lambda w, i, n: (0, block(w, i))),
            ],
            scratch_shapes=[
                pltpu.VMEM((heads, tq, 2 * HD), F32),
                pltpu.VMEM((heads, tq, HD), F32),
                pltpu.VMEM((tq, tk), F32),
            ],
        ),
        out_shape=[
            jax.ShapeDtypeStruct((rows, width), BF16),
            jax.ShapeDtypeStruct((heads, rows), F32),
        ],
        compiler_params=pltpu.CompilerParams(vmem_limit_bytes=40 * 2**20),
        cost_estimate=pl.CostEstimate(
            flops=2 * rows * width * chip_len * chips_z, bytes_accessed=4 * rows * width,
            transcendentals=rows * heads * chip_len * chips_z // 4,
        ),
        name="attention_forward",
    )(nums, queries, keys, values, spread, *deps)


def backward_kernel(tq, tk, heads, deps, nums, q_ref, g_ref, o_ref, lse_ref, k_ref, v_ref, start_ref, *refs):
    (dq_ref, dk_ref, dv_ref, dq_acc, dk_acc, dv_acc, bias, delta, probs_all, grads_all, q_all, g_all, turned) = refs[deps:]
    w, i = pl.program_id(0), pl.program_id(1)
    t0, lo, hi, full_lo, full_hi = (nums[w, i, n] for n in range(5))
    scale = HD**-0.5
    factor = scale * LOG2E
    chips_z, chip_len = k_ref.shape[0], k_ref.shape[2]

    @pl.when(i == 0)
    def _():
        dk_acc[...] = jnp.zeros_like(dk_acc)
        dv_acc[...] = jnp.zeros_like(dv_acc)
        for s in range(chips_z):
            turned[s] = jnp.transpose(k_ref[s, 0])

    dq_acc[...] = jnp.zeros_like(dq_acc)
    ones = jnp.ones((8, HD), F32)
    for h in range(heads):
        cols = slice(h * HD, (h + 1) * HD)
        rows = slice(h * tq, (h + 1) * tq)
        product = g_ref[:, cols].astype(F32) * o_ref[:, cols].astype(F32)
        delta[h] = lax.dot_general(
            ones, product, (((1,), (1,)), ((), ())), precision=lax.Precision.HIGHEST, preferred_element_type=F32
        )
        q_all[rows, :] = q_ref[:, cols]
        g_all[rows, :] = g_ref[:, cols]

    def tile(j, masked):
        slot, row, k0 = key_place(j, tk, nums, w, i, chips_z, chip_len)
        keys = k_ref[slot, 0, pl.ds(row, tk), :]
        values = v_ref[slot, 0, pl.ds(row, tk), :]
        if masked:
            key_pos = k0 + lax.broadcasted_iota(jnp.int32, (tk, tq), 0)
            query_pos = t0 + lax.broadcasted_iota(jnp.int32, (tk, tq), 1)
            allowed = (key_pos <= query_pos) & (key_pos >= start_ref[:1, :])
            bias[...] = jnp.where(allowed, 0.0, -1e30)
        for h in range(heads):
            rows = slice(h * tq, (h + 1) * tq)
            scores = contract_cols(keys, q_all[rows, :]) * factor
            if masked:
                scores = scores + bias[...]
            probs = jnp.exp2(scores - lse_ref[h : h + 1, :])
            grad_probs = contract_cols(values, g_all[rows, :])
            probs_all[:, rows] = probs.astype(BF16)
            grads_all[:, rows] = (probs * (grad_probs - delta[h, :1, :])).astype(BF16)
        dk_acc[slot, pl.ds(row, tk), :] += plain_dot(grads_all[...], q_all[...])
        dv_acc[slot, pl.ds(row, tk), :] += plain_dot(probs_all[...], g_all[...])
        dq_acc[...] += plain_dot(turned[slot, :, pl.ds(row, tk)], grads_all[...])

    def step(j, carry):
        partial = (j < full_lo) | (j >= full_hi)

        @pl.when(partial)
        def _():
            tile(j, True)

        @pl.when(jnp.logical_not(partial))
        def _():
            tile(j, False)

        return carry

    lax.fori_loop(lo, hi, step, 0)
    for h in range(heads):
        rows = slice(h * tq, (h + 1) * tq)
        dq_ref[:, h * HD : (h + 1) * HD] = (jnp.transpose(dq_acc[:, rows]) * scale).astype(BF16)

    @pl.when(i == pl.num_programs(1) - 1)
    def _():
        dk_ref[:, 0] = (dk_acc[...] * scale).astype(BF16)
        dv_ref[:, 0] = dv_acc[...].astype(BF16)


def attend_backward(queries, grad_attended, first_row, attended, lse, keys, values, starts, nums, tq, tk, deps=()):
    chips_z, windows, chip_len, _ = keys.shape
    rows, width = queries.shape
    heads = width // HD
    tiles = rows // windows // tq
    skip = first_row // tq

    def block(w, i):
        return w * tiles + i

    spread = jnp.broadcast_to(starts.reshape(1, rows), (8, rows))
    row_spec = pl.BlockSpec((tq, width), lambda w, i, n: (block(w, i), 0))
    key_spec = pl.BlockSpec((chips_z, 1, chip_len, HD), lambda w, i, n: (0, w, 0, 0))
    key_shape = jax.ShapeDtypeStruct(keys.shape, BF16)
    return pl.pallas_call(
        functools.partial(backward_kernel, tq, tk, heads, len(deps)),
        grid_spec=pltpu.PrefetchScalarGridSpec(
            num_scalar_prefetch=1,
            grid=(windows, tiles),
            in_specs=[
                row_spec,
                pl.BlockSpec((tq, width), lambda w, i, n: (block(w, i) + skip, 0)),
                row_spec,
                pl.BlockSpec((heads, tq), lambda w, i, n: (0, block(w, i))),
                key_spec,
                key_spec,
                pl.BlockSpec((8, tq), lambda w, i, n: (0, block(w, i))),
            ]
            + [pl.BlockSpec(memory_space=pl.ANY)] * len(deps),
            out_specs=[row_spec, key_spec, key_spec],
            scratch_shapes=[
                pltpu.VMEM((HD, heads * tq), F32),
                pltpu.VMEM((chips_z, chip_len, HD), F32),
                pltpu.VMEM((chips_z, chip_len, HD), F32),
                pltpu.VMEM((tk, tq), F32),
                pltpu.VMEM((heads, 8, tq), F32),
                pltpu.VMEM((tk, heads * tq), BF16),
                pltpu.VMEM((tk, heads * tq), BF16),
                pltpu.VMEM((heads * tq, HD), BF16),
                pltpu.VMEM((heads * tq, HD), BF16),
                pltpu.VMEM((chips_z, HD, chip_len), BF16),
            ],
        ),
        out_shape=[jax.ShapeDtypeStruct((rows, width), BF16), key_shape, key_shape],
        compiler_params=pltpu.CompilerParams(vmem_limit_bytes=40 * 2**20),
        cost_estimate=pl.CostEstimate(
            flops=4 * rows * width * chip_len * chips_z, bytes_accessed=8 * rows * width,
            transcendentals=rows * heads * chip_len * chips_z // 4,
        ),
        name="attention_backward",
    )(nums, queries, grad_attended, attended, lse, keys, values, spread, *deps)


def tile_numbers(starts, positions, z, tq, tk):
    windows, local = starts.shape
    tiled = starts.reshape(windows, local // tq, tq)
    t0 = jnp.broadcast_to(positions.reshape(local // tq, tq)[None, :, 0], (windows, local // tq))
    first, last = tiled[:, :, 0], tiled[:, :, -1]
    return jnp.stack(
        [t0, first // tk, (t0 + tq - 1) // tk + 1, (last + tk - 1) // tk, (t0 + 1) // tk, jnp.broadcast_to(z, t0.shape)],
        axis=2,
    ).astype(jnp.int32)


def matmul_kernel(kind, chunk, n_extra, n_out, n_deps, finish, *refs):
    a_ref, b_ref = refs[0], refs[1]
    extras = refs[2:2+n_extra]
    outs = refs[2+n_extra+n_deps:2+n_extra+n_deps+n_out]
    scratch = refs[2+n_extra+n_deps+n_out:]
    if kind == "tn":
        turned = scratch[0]
        @pl.when(pl.program_id(1) == 0)
        def _():
            turned[...] = jnp.transpose(a_ref[...])
        left = turned
    else:
        left = a_ref
    rows = left.shape[0]
    for r in range(0, rows, chunk):
        part = pl.ds(r, chunk)
        if kind == "nt":
            total = lax.dot_general(left[part, :], b_ref[...], (((1,), (1,)), ((), ())), preferred_element_type=F32)
        else:
            total = jnp.dot(left[part, :], b_ref[...], preferred_element_type=F32)
        finish(part, total, extras, outs)


def store(part, total, extras, outs):
    outs[0][part, :] = total.astype(outs[0].dtype)


def matmul(kind, a, b, outs, finish=store, extras=(), tm=1024, tn=512, chunk=256, deps=(), a_rows=None, name="matmul"):
    if kind == "tn":
        k, m = a.shape; n = b.shape[1]
    elif kind == "nt":
        m, k = a.shape; n = b.shape[0]
    else:
        m, k = a.shape; n = b.shape[1]
    first = 0
    if a_rows is not None:
        first, m = a_rows
    tm = min(tm, m); tn = min(tn, n); chunk = min(chunk, tm)
    f0 = first // tm
    a_spec = pl.BlockSpec((k, tm), lambda i, j: (0, i)) if kind == "tn" else pl.BlockSpec((tm, k), lambda i, j: (i + f0, 0))
    b_spec = pl.BlockSpec((tn, k), lambda i, j: (j, 0)) if kind == "nt" else pl.BlockSpec((k, tn), lambda i, j: (0, j))
    tile = pl.BlockSpec((tm, tn), lambda i, j: (i, j))
    row = pl.BlockSpec((1, tn), lambda i, j: (0, j))
    spec = {"tile": tile, "row": row, "part": pl.BlockSpec((1, 8, tn), lambda i, j: (i, 0, j))}
    shape = {"tile": (m, n), "row": (1, n), "part": (m // tm, 8, n)}
    out_shape = [jax.ShapeDtypeStruct(shape[w], d) for d, w in outs]
    res = pl.pallas_call(
        functools.partial(matmul_kernel, kind, chunk, len(extras), len(outs), len(deps), finish),
        grid=(m // tm, n // tn),
        in_specs=[a_spec, b_spec] + [spec[w] for _, w in extras] + [pl.BlockSpec(memory_space=pl.ANY)] * len(deps),
        out_specs=[spec[w] for _, w in outs],
        scratch_shapes=[pltpu.VMEM((tm, k), BF16)] if kind == "tn" else [],
        out_shape=out_shape,
        compiler_params=pltpu.CompilerParams(vmem_limit_bytes=52 * 2**20),
        cost_estimate=pl.CostEstimate(flops=2*m*n*k, bytes_accessed=2*(m*k+n*k+m*n), transcendentals=0),
        name=name,
    )(a, b, *[e for e, _ in extras], *deps)
    return res[0] if len(outs) == 1 else res


def slope_finish(part, total, extras, outs):
    g = (total * extras[0][part, :].astype(F32)).astype(BF16)
    outs[0][part, :] = g
    sums = jnp.sum(g.astype(F32).reshape(-1, 8, g.shape[1]), axis=0)
    if part.start == 0:
        outs[1][0] = sums
    else:
        outs[1][0] += sums


def contract_rows(left_op, right_op):
    return lax.dot_general(left_op, right_op, (((0,), (0,)), ((), ())), preferred_element_type=F32)


def contract_cols(left_op, right_op):
    return lax.dot_general(left_op, right_op, (((1,), (1,)), ((), ())), preferred_element_type=F32)


def plain_dot(left_op, right_op):
    return jnp.dot(left_op, right_op, preferred_element_type=F32)


def normalise(values):
    centred = values - jnp.mean(values, axis=-1, keepdims=True)
    spread = jnp.mean(centred * centred, axis=-1, keepdims=True)
    inverse = lax.rsqrt(spread + 1e-05)
    return centred * inverse, inverse


def norm_backward(unit, inverse, gain, grad):
    scaled = grad * gain
    inner = jnp.mean(scaled * unit, axis=-1, keepdims=True)
    return (scaled - jnp.mean(scaled, axis=-1, keepdims=True) - unit * inner) * inverse


def gelu_parts(u):
    inner = 0.7978845608028654 * (u + 0.044715 * u * u * u)
    t = jnp.tanh(inner)
    slope = 0.5 * (1.0 + t) + 0.5 * u * (1.0 - t * t) * 0.7978845608028654 * (1.0 + 3 * 0.044715 * u * u)
    return 0.5 * u * (1.0 + t), slope


def swap(values, axis):
    return lax.ppermute(values, axis, PAIR)


def in_order(index, own, other):
    return jnp.where(index == 0, jnp.stack([own, other]), jnp.stack([other, own]))


def pick(values, index, axis):
    return lax.dynamic_index_in_dim(values, index, axis, keepdims=False)


def exchange_add(values, index, axis_name, dim):
    arrived = swap(pick(values, 1 - index, dim), axis_name)
    return pick(values, index, dim).astype(F32) + arrived.astype(F32)


def core_rows(core, first, second):
    own = jnp.where(core == 0, first, second)
    other = swap(jnp.where(core == 0, second, first), "core")
    return in_order(core, own, other).reshape(2 * own.shape[0], own.shape[1])


def place_kernel(steps, half, spot, *refs):
    pieces, out, held, arrive, leave = refs[: 4 * steps], *refs[4 * steps :]
    y, x, z = spot[0], spot[1], spot[2]
    moves = []
    for s in range(steps):
        from_z = lax.rem(z - s + steps, steps)
        for i in range(2):
            for k, to in enumerate(((i, x, 0), (i, 1 - x, 0), (y, i, 1), (1 - y, i, 1))):
                row = (((to[0] * 2 + to[1]) * steps + from_z) * 2 + to[2]) * half
                moves.append((4 * s + k, i, pl.multiple_of(row, half)))
    inward = [
        pltpu.make_async_copy(pieces[p].at[i], held.at[n], arrive.at[n]) for n, (p, i, _) in enumerate(moves)
    ]
    outward = [
        pltpu.make_async_copy(held.at[n], out.at[pl.ds(row, half), :], leave.at[n])
        for n, (_, _, row) in enumerate(moves)
    ]
    for copy in inward:
        copy.start()
    for n, copy in enumerate(inward):
        copy.wait()
        outward[n].start()
    for copy in outward:
        copy.wait()


def place(pieces, spot):
    steps = len(pieces) // 4
    _, half, cols = pieces[0].shape
    return pl.pallas_call(
        functools.partial(place_kernel, steps, half),
        grid_spec=pltpu.PrefetchScalarGridSpec(
            num_scalar_prefetch=1,
            grid=(1,),
            in_specs=[pl.BlockSpec(memory_space=pl.ANY)] * len(pieces),
            out_specs=pl.BlockSpec(memory_space=pl.ANY),
            scratch_shapes=[
                pltpu.VMEM((8 * steps, half, cols), BF16),
                pltpu.SemaphoreType.DMA((8 * steps,)),
                pltpu.SemaphoreType.DMA((8 * steps,)),
            ],
        ),
        out_shape=jax.ShapeDtypeStruct((8 * steps * half, cols), BF16),
        compiler_params=pltpu.CompilerParams(vmem_limit_bytes=32 * 2**20),
        name="place_weight",
    )(spot, *pieces)


def gather_pieces(block, y, x, chips_z):
    half = block.shape[0] // 2
    ring = [(i, (i + 1) % chips_z) for i in range(chips_z)]
    one, two = block[:half], block[half:]
    got_one, got_two = lax.ppermute(one, "y", PAIR), lax.ppermute(two, "x", PAIR)
    one, two = in_order(y, one, got_one), in_order(x, two, got_two)
    pieces = []
    for s in range(chips_z):
        last = s == chips_z - 1
        next_one = None if last else lax.ppermute(one, "z", ring)
        next_two = None if last else lax.ppermute(two, "z", ring)
        pieces += [one, lax.ppermute(one, "x", PAIR), two, lax.ppermute(two, "y", PAIR)]
        one, two = next_one, next_two
    return pieces


class Sum:
    def __init__(self, total, y, x, chips_z):
        self.cols = total.shape[1]
        self.half = total.shape[0] // (8 * chips_z)
        self.total, self.y, self.x, self.chips_z = total.reshape(2, 2, chips_z, 2, self.half, self.cols), y, x, chips_z
        self.sent = (self.cut(0, 1 - y, 0), self.cut(1, 1 - x, 1))

    def cut(self, dim, index, part):
        at, size = [0, 0, 0, part, 0, 0], [2, 2, self.chips_z, 1, self.half, self.cols]
        at[dim], size[dim] = index, 1
        return lax.dynamic_slice(self.total, at, size).reshape(2, self.chips_z, self.half, self.cols)

    def first(self):
        one, two = swap(self.sent[0], "y"), swap(self.sent[1], "x")
        self.one = (self.cut(0, self.y, 0).astype(F32) + one.astype(F32)).astype(BF16)
        self.two = (self.cut(1, self.x, 1).astype(F32) + two.astype(F32)).astype(BF16)
        self.sent = (pick(self.one, 1 - self.x, 0), pick(self.two, 1 - self.y, 0))

    def second(self):
        one, two = swap(self.sent[0], "x"), swap(self.sent[1], "y")
        one = (pick(self.one, self.x, 0).astype(F32) + one.astype(F32)).astype(BF16)
        two = (pick(self.two, self.y, 0).astype(F32) + two.astype(F32)).astype(BF16)
        self.both = jnp.stack([one, two], axis=1).reshape(-1, self.cols)

    def over_z(self):
        self.result = lax.psum_scatter(self.both, "z", scatter_dimension=0, tiled=True)
        return self.result.astype(F32)


def doubling(axis):
    size = lax.axis_size(axis)
    step = 1
    while step < size:
        yield step, [(i, i ^ step) for i in range(size)]
        step *= 2


def gather_small(vector):
    for axis in reversed(EVERY):
        index = lax.axis_index(axis)
        for step, pairs in doubling(axis):
            vector = in_order((index // step) % 2, vector, lax.ppermute(vector, axis, pairs))
    return vector.reshape(-1, vector.shape[-1])


def sum_small(vector):
    for axis in reversed(EVERY):
        for _, pairs in doubling(axis):
            vector = vector + lax.ppermute(vector, axis, pairs)
    return vector


def own_rows(core, rows):
    pair = rows.reshape(2, rows.shape[0] // 2, rows.shape[1])
    own = pick(pair, core, 0)
    other = swap(pick(pair, 1 - core, 0), "core")
    return in_order(core, own, other)


def body(
    hidden_in, doc_lengths, cotangent, ln1_gain, ln1_bias, w_qkv, b_qv, w_out, b_out,
    ln2_gain, ln2_bias, w_up, b_up, w_down, b_down,
):
    windows, local_len, width = hidden_in.shape
    own_count = windows * local_len
    count = 2 * own_count
    chips_z = lax.axis_size("z")
    chips = 2 * lax.axis_size("y") * chips_z
    y, x, z, core = (lax.axis_index(name) for name in EVERY)
    width_q = HEADS * HD
    half_q = width_q // 2
    chip_len = 2 * local_len
    length = chip_len * chips_z
    hidden_units = w_up.shape[1]
    unit_block = hidden_units // (2 * chips)

    doc_ends = jnp.cumsum(doc_lengths, axis=1)
    cores = jnp.stack([core, 1 - core])
    positions = (z * chip_len + cores[:, None] * local_len + jnp.arange(local_len, dtype=jnp.int32)[None, :]).astype(jnp.int32)
    ended = positions[:, None, :, None] >= doc_ends[None, :, None, :]
    starts = jnp.max(jnp.where(ended, doc_ends[None, :, None, :], 0), axis=3)
    valid = (jnp.sum(ended[0].astype(jnp.int32), axis=2) < DOCS).reshape(own_count, 1)

    vectors = (ln1_gain, ln1_bias, b_qv, b_out, ln2_gain, ln2_bias, b_up, b_down)
    sizes = [v.shape[0] for v in vectors]
    packed = gather_small(jnp.concatenate(vectors)).astype(F32)
    full = []
    at = 0
    for size in sizes:
        full.append(packed[:, at : at + size].reshape(-1))
        at += size
    gain1, bias1, bias_qv, bias_out, gain2, bias2, bias_up, bias_down = full
    bias_up = pick(bias_up.reshape(chips, 2, unit_block), core, 1).reshape(-1)
    bias_qkv = jnp.where(
        core == 0,
        jnp.concatenate([bias_qv[:half_q], jnp.zeros((HD,), F32)]),
        jnp.concatenate([bias_qv[half_q:width_q], bias_qv[width_q:]]),
    )
    qkv_block = core_rows(
        core,
        jnp.concatenate([w_qkv[:, :half_q], w_qkv[:, width_q : width_q + HD]], axis=1),
        jnp.concatenate([w_qkv[:, half_q:width_q], w_qkv[:, width_q + HD :]], axis=1),
    )
    w_out_t = w_out.T
    out_block = core_rows(core, w_out_t[:, :half_q], w_out_t[:, half_q:])
    up_parts = w_up.reshape(w_up.shape[0], chips, 2, unit_block)
    up_block = core_rows(
        core,
        up_parts[:, :, 0].reshape(w_up.shape[0], -1),
        up_parts[:, :, 1].reshape(w_up.shape[0], -1),
    )
    spot = jnp.stack([y, x, z]).astype(jnp.int32)
    by_hand = lax.axis_size("y") == 2

    def gather(block):
        return lax.all_gather(block, CHIPS, axis=0, tiled=True)

    if by_hand:
        w_qkv_all = place(gather_pieces(qkv_block, y, x, chips_z), spot)
        w_out_all = place(gather_pieces(out_block, y, x, chips_z), spot)
    else:
        w_qkv_all, w_out_all = gather(qkv_block), gather(out_block)
    w_up_all, w_down_all = gather(up_block), gather(w_down)

    tokens = hidden_in.reshape(own_count, width).astype(F32)
    unit1, inverse1 = normalise(tokens)
    normed1_own = (unit1 * gain1 + bias1).astype(BF16)
    normed1 = jnp.concatenate([normed1_own, swap(normed1_own, "core")], axis=0)
    own_kv = (plain_dot(normed1, w_qkv_all[:, half_q:]) + bias_qkv[half_q:]).astype(BF16)
    own_kv = own_kv.reshape(2, windows, local_len, HD)
    own_kv = jnp.swapaxes(in_order(core, own_kv[0], own_kv[1]), 0, 1).reshape(windows, chip_len, HD)
    ring = [(i, (i + 1) % chips_z) for i in range(chips_z)]
    keys, values = [], []
    for s in range(chips_z):
        other_kv = swap(own_kv, "core")
        keys.append(jnp.where(core == 0, own_kv, other_kv))
        values.append(jnp.where(core == 0, other_kv, own_kv))
        if s < chips_z - 1:
            own_kv = lax.ppermute(own_kv, "z", ring)
    keys, values = jnp.stack(keys), jnp.stack(values)
    projected = (plain_dot(normed1, w_qkv_all[:, :half_q]) + bias_qkv[:half_q]).astype(BF16)
    queries = (projected[:own_count], projected[own_count:])
    tq_forward, tk_forward = min(512, local_len), min(512, chip_len)
    tq, tk = min(256, local_len), min(256, chip_len)
    attended, lse = [None, None], [None, None]
    for n in (1, 0):
        attended[n], lse[n] = attend_forward(
            queries[n], keys, values, starts[n],
            tile_numbers(starts[n], positions[n], z, tq_forward, tk_forward), tq_forward, tk_forward,
        )
        if n == 1:
            out_other = swap(plain_dot(attended[1], w_out_all.T).astype(BF16), "core")
    residual = tokens + bias_out + plain_dot(attended[0], w_out_all.T) + out_other.astype(F32)
    attended_all = jnp.concatenate(attended, axis=0)

    unit2, inverse2 = normalise(residual)
    normed2_own = (unit2 * gain2 + bias2).astype(BF16)
    normed2 = jnp.concatenate([normed2_own, swap(normed2_own, "core")], axis=0)
    upward = plain_dot(normed2, w_up_all) + bias_up
    active, slope = gelu_parts(upward)
    active = active.astype(BF16)
    upstream = jnp.where(valid, cotangent.reshape(own_count, width), 0)
    grad_down = jnp.concatenate([upstream, swap(upstream, "core")], axis=0)
    grad_b_down = jnp.sum(upstream.astype(F32), axis=0)
    down_total = contract_rows(active, grad_down).astype(BF16)

    if by_hand:
        down_sum = Sum(down_total, y, x, chips_z)
    grad_up, unit_sums = matmul(
        "nt", grad_down, w_down_all, [(BF16, "tile"), (F32, "part")], slope_finish, [(slope, "tile")],
        deps=down_sum.sent if by_hand else (), name="grad_up",
    )
    grad_b_up = jnp.sum(unit_sums, axis=(0, 1))
    up_total = matmul("tn", normed2, grad_up, [(BF16, "tile")], name="grad_w_up")
    if by_hand:
        down_sum.first()
        up_sum = Sum(up_total, y, x, chips_z)
    grad_other = matmul(
        "nt", grad_up, w_up_all, [(BF16, "tile")], a_rows=(own_count, own_count),
        deps=down_sum.sent + up_sum.sent if by_hand else (), name="grad_normed2",
    )
    grad_mixed = contract_cols(grad_up[:own_count], w_up_all) + swap(grad_other, "core").astype(F32)
    grad_gain2 = jnp.sum(grad_mixed * unit2, axis=0)
    grad_bias2 = jnp.sum(grad_mixed, axis=0)
    grad_residual = upstream.astype(F32) + norm_backward(unit2, inverse2, gain2, grad_mixed)
    branch_own = grad_residual.astype(BF16)
    grad_b_out = jnp.sum(branch_own.astype(F32), axis=0)
    branch = jnp.concatenate([branch_own, swap(branch_own, "core")], axis=0)
    if by_hand:
        down_sum.second()
        grad_w_down = down_sum.over_z()
    down_other = matmul(
        "nn", active, w_down_all, [(BF16, "tile")], a_rows=(own_count, own_count),
        deps=(branch_own, down_sum.both) if by_hand else (branch_own,), name="mixed_out",
    )
    mixed_out = (
        residual + bias_down + plain_dot(active[:own_count], w_down_all) + swap(down_other, "core").astype(F32)
    ).astype(BF16)
    if by_hand:
        up_sum.first()

    grad_attended = matmul(
        "nn", branch, w_out_all, [(BF16, "tile")], deps=up_sum.sent if by_hand else (), name="grad_attended"
    )
    out_total = matmul("tn", branch, attended_all, [(BF16, "tile")], name="grad_w_out")
    if by_hand:
        out_sum = Sum(out_total, y, x, chips_z)
        up_sum.second()
        grad_w_up = up_sum.over_z()
    grad_query, grad_keys, grad_values = [None, None], [None, None], [None, None]
    for n in (0, 1):
        deps = ()
        if by_hand:
            if n == 0:
                deps = out_sum.sent + (up_sum.both, mixed_out)
            else:
                out_sum.first()
                deps = out_sum.sent + (grad_keys[0], down_sum.result)
        grad_query[n], grad_keys[n], grad_values[n] = attend_backward(
            queries[n], grad_attended, n * own_count, attended[n], lse[n], keys, values, starts[n],
            tile_numbers(starts[n], positions[n], z, tq, tk), tq, tk, deps,
        )
    grad_keys = grad_keys[0].astype(F32) + grad_keys[1].astype(F32)
    grad_values = grad_values[0].astype(F32) + grad_values[1].astype(F32)
    arrived = swap(jnp.where(core == 0, grad_values, grad_keys).astype(BF16), "core")
    grad_kv = (jnp.where(core == 0, grad_keys, grad_values) + arrived.astype(F32)).astype(BF16)
    running = grad_kv[1 % chips_z]
    for s in range(2, chips_z + 1):
        running = (grad_kv[s % chips_z].astype(F32) + lax.ppermute(running, "z", ring).astype(F32)).astype(BF16)
    grad_kv = jnp.swapaxes(running.reshape(windows, 2, local_len, HD), 0, 1)
    grad_kv = in_order(core, grad_kv[0], grad_kv[1]).reshape(count, HD)
    grad_qkv = jnp.concatenate([jnp.concatenate(grad_query, axis=0), grad_kv], axis=1)
    grad_b_qkv = jnp.sum(grad_qkv.astype(F32), axis=0)
    qkv_total = contract_rows(normed1, grad_qkv).astype(BF16)
    grad_other = contract_cols(grad_qkv[own_count:], w_qkv_all).astype(BF16)
    grad_normed = contract_cols(grad_qkv[:own_count], w_qkv_all) + swap(grad_other, "core").astype(F32)
    grad_gain1 = jnp.sum(grad_normed * unit1, axis=0)
    grad_bias1 = jnp.sum(grad_normed, axis=0)
    grad_hidden = grad_residual + norm_backward(unit1, inverse1, gain1, grad_normed)

    if by_hand:
        qkv_sum = Sum(qkv_total, y, x, chips_z)
        out_sum.second()
        grad_w_out = out_sum.over_z()
        qkv_sum.first()
        qkv_sum.second()
        grad_w_qkv = qkv_sum.over_z()
    else:
        grad_w_down, grad_w_up, grad_w_out, grad_w_qkv = (
            lax.psum_scatter(total, CHIPS, scatter_dimension=0, tiled=True).astype(F32)
            for total in (down_total, up_total, out_total, qkv_total)
        )
    zero = jnp.zeros_like(grad_b_qkv[:half_q])
    query_bias = jnp.where(
        core == 0, jnp.concatenate([grad_b_qkv[:half_q], zero]), jnp.concatenate([zero, grad_b_qkv[:half_q]])
    )
    value_bias = jnp.where(core == 0, 0.0, grad_b_qkv[half_q:])
    unit_bias = in_order(core, grad_b_up.reshape(chips, unit_block), jnp.zeros((chips, unit_block), F32))
    unit_bias = jnp.swapaxes(unit_bias, 0, 1).reshape(-1)
    device = ((y * 2 + x) * chips_z + z) * 2 + core
    mine = []
    for group in ((grad_b_out, grad_gain2, grad_bias2, unit_bias, grad_b_down), (grad_gain1, grad_bias1, query_bias, value_bias)):
        sums = sum_small(jnp.concatenate(group))
        at = 0
        for part in group:
            size = part.shape[0] // (2 * chips)
            mine.append(lax.dynamic_slice_in_dim(sums, at + device * size, size, 0))
            at += part.shape[0]
    own_qkv = own_rows(core, grad_w_qkv)
    own_qkv = jnp.concatenate(
        [own_qkv[0, :, :half_q], own_qkv[1, :, :half_q], own_qkv[0, :, half_q:], own_qkv[1, :, half_q:]], axis=1
    )
    own_out = own_rows(core, grad_w_out)
    own_out = jnp.concatenate([own_out[0], own_out[1]], axis=1).T
    own_up = own_rows(core, grad_w_up)
    own_up = jnp.moveaxis(own_up.reshape(2, own_up.shape[1], chips, unit_block), 0, 2).reshape(own_up.shape[1], -1)
    return (
        mixed_out.reshape(windows, local_len, width),
        grad_hidden.reshape(windows, local_len, width),
        mine[5], mine[6], own_qkv, mine[7], mine[8], own_out, mine[0], mine[1], mine[2],
        own_up, mine[3], grad_w_down, mine[4],
    )


def solution(mesh):
    split = Mesh(mesh.devices.reshape(mesh.shape["dp"] // 2, 2, mesh.shape["seq"] // 2, 2), EVERY)
    rows = ("y", "x")
    cols = ("z", "core")
    vector, matrix = P(EVERY), P(EVERY, None)
    tokens = P(rows, cols, None)
    return jax.shard_map(
        body,
        mesh=split,
        in_specs=(
            tokens, P(rows, None), tokens, vector, vector, matrix, vector, P(None, EVERY), vector,
            vector, vector, matrix, vector, matrix, vector,
        ),
        out_specs=(
            tokens, tokens, vector, vector, matrix, vector, vector, P(None, EVERY), vector, vector, vector,
            matrix, vector, matrix, vector,
        ),
        check_vma=False,
    )
```

time: 3680 us -> 1330 us (0.36)
  waiting for transfers between devices: 1820 us -> 410 us
  matrix products: 1380 us -> 229 us
  Pallas kernels: 0 us -> 266 us
  starting transfers between devices: 0.52 us -> 155 us
  blocking collectives: 83.1 us -> 0 us
  other arithmetic: 225 us -> 152 us
  local copies, waits for them, and re-layouts: 148 us -> 85.1 us
    reduce_scatter x6 -> x4, waiting for transfers between devices: 1790 us -> 11.5 us  [over_z(): lax.psum_scatter(self.both, 'z', scatter_dimension=0, tiled=True)]
    dot_general x52 -> x3, matrix products: 597 us -> 50.2 us  [contract_cols(): lax.dot_general(left_op, right_op, (((1,), (1,)), ((), ())), preferred_el...]
    ppermute x0 -> x88, waiting for transfers between devices: none -> 375 us  [the longest x35 106 us: swap(): return lax.ppermute(values, axis, PAIR)]
    dot_general x36 -> x6, matrix products: 479 us -> 122 us  [plain_dot(): return jnp.dot(left_op, right_op, preferred_element_type=F32)]
    pallas_call x0 -> x12, Pallas kernels: none -> 266 us  [the longest x6 171 us: matmul(): pl.pallas_call(functools.partial(matmul_kernel, kind, chunk, len(extras),...]
    dot_general x36 -> x2, matrix products: 305 us -> 56.7 us  [contract_rows(): lax.dot_general(left_op, right_op, (((0,), (0,)), ((), ())), preferred_el...]
    ppermute x0 -> x88, starting transfers between devices: none -> 154 us  [the longest x6 30.4 us: gather_pieces(): next_one = None if last else lax.ppermute(one, 'z', ring)]
    reduce_sum x27 -> x8, other arithmetic: 173 us -> 25.1 us  [the longest x1 13.7 us: body(): grad_b_out = jnp.sum(branch_own.astype(F32), axis=0)]
  transfers between devices with their start and end apart: 13 -> 94, of which waited for: 7 -> 42; matrix products, arithmetic and copies ran while one was open for 24% -> 33% of each run, Pallas kernels for 0% -> 20%
where the time goes in v1:
time: 1330 us; the launch traced here: 1320 us
  waiting for transfers between devices  410 us (31%)
  Pallas kernels  266 us (20%)
  matrix products  229 us (17%)
  starting transfers between devices  155 us (12%)
  other arithmetic  152 us (11%)
  local copies, waits for them, and re-layouts  85.1 us (6%)
  between operations  19.2 us (1%)
    pallas_call x6, Pallas kernels, matmul(): pl.pallas_call(functools.partial(matmul_kernel, kind, chunk, len(extras),...  171 us
    dot_general x6, matrix products, plain_dot(): return jnp.dot(left_op, right_op, preferred_element_type=F32)  122 us
    ppermute x35, waiting for transfers between devices, swap(): return lax.ppermute(values, axis, PAIR)  106 us
    ppermute x3, waiting for transfers between devices, body(): lax.ppermute(running, 'z', ring).astype(F32)  101 us
    dot_general x2, matrix products, contract_rows(): lax.dot_general(left_op, right_op, (((0,), (0,)), ((), ())), preferred_el...  56.7 us
    dot_general x3, matrix products, contract_cols(): lax.dot_general(left_op, right_op, (((1,), (1,)), ((), ())), preferred_el...  50.2 us
    ppermute x6, waiting for transfers between devices, gather_pieces(): next_one = None if last else lax.ppermute(one, 'z', ring)  48.3 us
    pallas_call x2, Pallas kernels, attend_backward(): pl.pallas_call(functools.partial(backward_kernel, tq, tk, heads, len(deps...  46.4 us
  transfers between devices with their start and end apart: 94, of which 42 were waited for; matrix products, arithmetic and copies ran while one was open for 33% of the time, Pallas kernels for 20%

profile of v1, /device:TPU:0, one launch (start us, length us, event | category | flops | bytes accessed | tf_op | source)
XLA Modules:
  0.0 1316.6 jit_solution(13230133374058219650)
XLA Ops:
  70.3 27.9 %collective-permute-done.35.refs_4_ = bf16[2,64,1024]{2,1,0:T(8,128)(2,1)} collective-permute-done((bf16[2,64,1024]{2,1,0:T(8,128)(2,1)S(1)}, bf16[2,64,1024]{2,1,0:T(8,128)(2,1)}, u32[]{:S(2)}, u32[]{:S(2)}) %collective-permute-start.35) | collective-permute-done | bytes 262176 | tf_op jit(solution)/shard_map/ppermute | solution.py:447
  100.1 17.2 %collective-permute-start.15 = (bf16[2,64,1152]{2,1,0:T(8,128)(2,1)S(1)}, bf16[2,64,1152]{2,1,0:T(8,128)(2,1)S(1)}, u32[]{:S(2)}, u32[]{:S(2)}) collective-permute-start(bf16[2,64,1152]{2,1,0:T(8,128)(2,1)S(1)} %collective-permute-done.11.refs_4_), channel_id=1, source_target_pairs={{0,2},{2,4},{4,6},{6,0},{1,3},{3,5},{5,7},{7,1},{8,10},{10,12},{12... | collective-permute-start | bytes 884744 | tf_op jit(solution)/shard_map/ppermute | solution.py:447
  320.1 15.8 %attention_forward.3 = (bf16[1024,1024]{1,0:T(8,128)(2,1)S(1)}, f32[8,1024]{1,0:T(8,128)S(1)}) custom-call(s32[2,1,6]{2,1,0:T(1,128)S(1)} %stack.420.nums, bf16[1024,1024]{1,0:T(8,128)(2,1)S(1)} %get-tuple-element.73.q_ref, bf16[4,2,1024,128]{3,2,1,0:T(8,128)(2,1)S(1)} %get-tuple-element.182.k_ref, bf16[4,2,1024,128]{3,2,1,0:T(8,128)(2,1)S(1)} %get-tuple-element.183.v_ref, ...), custom_call_target="tpu_custom_call" | custom-call | flops 8589934592 | bytes 4194304 | tf_op jit(solution)/shard_map/attention_forward/pallas_call | solution.py:93
  408.0 65.9 %fusion.4 = (f32[2048,4096]{1,0:T(8,128)}, bf16[2048,4096]{1,0:T(8,128)(2,1)}) fusion(f32[4096]{0:T(1024)S(1)} %bitcast.402, bf16[2048,4096]{1,0:T(8,128)(2,1)} %all-gather.3.cloned.1.call-done.refs_1_, bf16[1024,2048]{1,0:T(8,128)(2,1)} %collective-permute-done.48, bf16[1024,2048]{1,0:T(8,128)(2,1)} %add_convert_fusion.1), kind=kOutput, calls=%fused_computation.6 | convolution fusion | flops 34544287744 | bytes 75513856 | tf_op jit(solution)/shard_map/dot_general | solution.py:344
  473.9 41.1 %convolution_convert_fusion = bf16[4096,2048]{1,0:T(8,128)(2,1)S(1)} fusion(bf16[2048,4096]{1,0:T(8,128)(2,1)} %get-tuple-element.63.refs_0_, bf16[1024,2048]{1,0:T(8,128)(2,1)} %collective-permute-done.50, bf16[1024,2048]{1,0:T(8,128)(2,1)} %bitcast_select_fusion), kind=kOutput, calls=%fused_computation.8 | convolution fusion | flops 34384904192 | bytes 41943040 | tf_op jit(solution)/shard_map/dot_general | solution.py:336
  526.4 23.8 %all-gather.5.cloned.1.call-done.refs_1_ = bf16[4096,2048]{1,0:T(8,128)(2,1)} async-done(((bf16[256,2048]{1,0:T(8,128)(2,1)}), bf16[4096,2048]{1,0:T(8,128)(2,1)}) %all-gather.5.cloned.1.call-update) | async-done | bytes 16777232 | tf_op jit(solution)/shard_map/all_gather | solution.py:569
  550.2 46.1 %grad_up.1 = (bf16[2048,4096]{1,0:T(8,128)(2,1)}, f32[2,8,4096]{2,1,0:T(8,128)S(1)}) custom-call(bf16[2048,2048]{1,0:T(8,128)(2,1)} %pad_maximum_fusion.2.refs_0_, bf16[4096,2048]{1,0:T(8,128)(2,1)} %all-gather.5.cloned.1.call-done.refs_1_, f32[2048,4096]{1,0:T(8,128)} %get-tuple-element.62.refs_2_, ...), custom_call_target="tpu_custom_call" | custom-call | flops 34359738368 | bytes 41943040 | tf_op jit(solution)/shard_map/grad_up/pallas_call | solution.py:311
  596.4 45.0 %grad_w_up.1 = bf16[2048,4096]{1,0:T(8,128)(2,1)} custom-call(bf16[2048,2048]{1,0:T(8,128)(2,1)} %pad_maximum_fusion.1.refs_0_, bf16[2048,4096]{1,0:T(8,128)(2,1)} %get-tuple-element.29.refs_1_.refs_0_), custom_call_target="tpu_custom_call" | custom-call | flops 34359738368 | bytes 41943040 | tf_op jit(solution)/shard_map/grad_w_up/pallas_call | solution.py:311
  664.5 23.8 %grad_normed2.1 = bf16[1024,2048]{1,0:T(8,128)(2,1)} custom-call(bf16[2048,4096]{1,0:T(8,128)(2,1)} %get-tuple-element.29.refs_1_.refs_0_, bf16[2048,4096]{1,0:T(8,128)(2,1)} %all-gather.3.cloned.1.call-done.refs_1_, bf16[4,128,2048]{2,1,0:T(8,128)(2,1)} %copy-done.47, bf16[4,128,2048]{2,1,0:T(8,128)(2,1)} %dynamic-slice_bitcast_fusion.6.refs_3_, ...), custom_call_target="tpu_custom_call" | custom-call | flops 17179869184 | bytes 29360128 | tf_op jit(solution)/shard_map/grad_normed2/pallas_call | solution.py:311
  688.3 24.2 %fusion.5 = f32[1024,2048]{1,0:T(8,128)} fusion(bf16[4096,2048]{1,0:T(8,128)(2,1)} %all-gather.5.cloned.1.call-done.refs_1_, bf16[2048,4096]{1,0:T(8,128)(2,1)} %get-tuple-element.63.refs_0_), kind=kOutput, calls=%fused_computation.10 | convolution fusion | flops 17179869184 | bytes 33554432 | tf_op jit(solution)/shard_map/dot_general | solution.py:344
  713.7 26.1 %collective-permute-done.59 = bf16[2,4,64,4096]{3,2,1,0:T(8,128)(2,1)} collective-permute-done((bf16[2,4,64,4096]{3,2,1,0:T(8,128)(2,1)}, bf16[2,4,64,4096]{3,2,1,0:T(8,128)(2,1)}, u32[]{:S(2)}, u32[]{:S(2)}) %collective-permute-start.59) | collective-permute-done | bytes 4194336 | tf_op jit(solution)/shard_map/ppermute | solution.py:368
  757.4 27.4 %collective-permute-done.54 = bf16[4,128,2048]{2,1,0:T(8,128)(2,1)} collective-permute-done((bf16[4,128,2048]{2,1,0:T(8,128)(2,1)S(1)}, bf16[4,128,2048]{2,1,0:T(8,128)(2,1)}, u32[]{:S(2)}, u32[]{:S(2)}) %collective-permute-start.54) | collective-permute-done | bytes 2097184 | tf_op jit(solution)/shard_map/ppermute | solution.py:368
  793.3 28.7 %multiply_reduce_fusion = (f32[2048]{0:T(1024)S(1)}, f32[1024]{0:T(1024)S(1)}, f32[1024]{0:T(1024)S(1)}, f32[2048]{0:T(1024)S(1)}, f32[1024,2048]{1,0:T(8,128)}) fusion(f32[1024,2048]{1,0:T(8,128)} %copy-done.28, f32[1024]{0:T(1024)S(1)} %copy-done.66, f32[1024]{0:T(1024)S(1)} %copy-done.58, f32[2048]{0:T(1024)S(1)} %copy-done.56, ...), kind=kOutput, calls=%fused_computation.45 | convolution fusion | flops 17202931712 | bytes 46178304 | tf_op jit(solution)/shard_map/dot_general | solution.py:340
  838.0 24.1 %mixed_out.1 = bf16[1024,2048]{1,0:T(8,128)(2,1)} custom-call(bf16[2048,4096]{1,0:T(8,128)(2,1)} %get-tuple-element.63.refs_0_, bf16[4096,2048]{1,0:T(8,128)(2,1)} %all-gather.5.cloned.1.call-done.refs_1_, bf16[1024,2048]{1,0:T(8,128)(2,1)} %get-tuple-element.50.refs_2_, bf16[1024,2048]{1,0:T(8,128)(2,1)} %bitcast.348), custom_call_target="tpu_custom_call" | custom-call | flops 17179869184 | bytes 29360128 | tf_op jit(solution)/shard_map/mixed_out/pallas_call | solution.py:311
  864.6 21.2 %collective-permute-done.61 = bf16[4,64,4096]{2,1,0:T(8,128)(2,1)} collective-permute-done((bf16[4,64,4096]{2,1,0:T(8,128)(2,1)}, bf16[4,64,4096]{2,1,0:T(8,128)(2,1)}, u32[]{:S(2)}, u32[]{:S(2)}) %collective-permute-start.61) | collective-permute-done | bytes 2097184 | tf_op jit(solution)/shard_map/ppermute | solution.py:368
  899.4 17.8 %grad_w_out.1 = bf16[2048,1024]{1,0:T(8,128)(2,1)} custom-call(bf16[2048,2048]{1,0:T(8,128)(2,1)} %pad_maximum_fusion.3.refs_0_, bf16[2048,1024]{1,0:T(8,128)(2,1)} %pad_maximum_fusion.6.refs_1_), custom_call_target="tpu_custom_call" | custom-call | flops 8589934592 | bytes 16777216 | tf_op jit(solution)/shard_map/grad_w_out/pallas_call | solution.py:311
  921.9 14.4 %grad_attended.1.g_ref = bf16[2048,1024]{1,0:T(8,128)(2,1)} custom-call(bf16[2048,2048]{1,0:T(8,128)(2,1)} %pad_maximum_fusion.3.refs_0_, bf16[2048,1024]{1,0:T(8,128)(2,1)} %copy-done.3, bf16[4,64,4096]{2,1,0:T(8,128)(2,1)} %dynamic-slice_bitcast_fusion.5.refs_2_, bf16[4,64,4096]{2,1,0:T(8,128)(2,1)} %dynamic-slice_bitcast_fusion.4.refs_3_), custom_call_target="tpu_custom_call" | custom-call | flops 8589934592 | bytes 16777216 | tf_op jit(solution)/shard_map/grad_attended/pallas_call | solution.py:311
  951.2 19.2 %attention_backward.2 = (bf16[1024,1024]{1,0:T(8,128)(2,1)S(1)}, bf16[4,2,1024,128]{3,2,1,0:T(8,128)(2,1)S(1)}, bf16[4,2,1024,128]{3,2,1,0:T(8,128)(2,1)S(1)}) custom-call(s32[2,2,6]{2,1,0:T(2,128)S(1)} %stack.427.nums, bf16[1024,1024]{1,0:T(8,128)(2,1)S(1)} %copy-done.8, bf16[2048,1024]{1,0:T(8,128)(2,1)} %grad_attended.1.g_ref, ...), custom_call_target="tpu_custom_call" | custom-call | flops 17179869184 | bytes 8388608 | tf_op jit(solution)/shard_map/attention_backward/pallas_call | solution.py:215
  981.5 27.2 %attention_backward.3 = (bf16[1024,1024]{1,0:T(8,128)(2,1)S(1)}, bf16[4,2,1024,128]{3,2,1,0:T(8,128)(2,1)S(1)}, bf16[4,2,1024,128]{3,2,1,0:T(8,128)(2,1)S(1)}) custom-call(s32[2,2,6]{2,1,0:T(2,128)S(1)} %stack.431.nums, bf16[1024,1024]{1,0:T(8,128)(2,1)S(1)} %copy-done.6, bf16[2048,1024]{1,0:T(8,128)(2,1)} %grad_attended.1.g_ref, ...), custom_call_target="tpu_custom_call" | custom-call | flops 17179869184 | bytes 8388608 | tf_op jit(solution)/shard_map/attention_backward/pallas_call | solution.py:215
  1017.7 26.0 %collective-permute-start.65 = (bf16[2,1024,128]{2,1,0:T(8,128)(2,1)}, bf16[2,1024,128]{2,1,0:T(8,128)(2,1)}, u32[]{:S(2)}, u32[]{:S(2)}) collective-permute-start(bf16[2,1024,128]{2,1,0:T(8,128)(2,1)} %slice_bitcast_fusion), channel_id=1, source_target_pairs={{0,2},{2,4},{4,6},{6,0},{1,3},{3,5},{5,7},{7,1},{8,10},{10,12},{12... | collective-permute-start | bytes 1572872 | tf_op jit(solution)/shard_map/ppermute | solution.py:682
  1046.9 72.1 %collective-permute-done.65 = bf16[2,1024,128]{2,1,0:T(8,128)(2,1)} collective-permute-done((bf16[2,1024,128]{2,1,0:T(8,128)(2,1)}, bf16[2,1024,128]{2,1,0:T(8,128)(2,1)}, u32[]{:S(2)}, u32[]{:S(2)}) %collective-permute-start.65) | collective-permute-done | bytes 524320 | tf_op jit(solution)/shard_map/ppermute | solution.py:682
  1140.9 16.3 %collective-permute-done.67 = bf16[2,1024,128]{2,1,0:T(8,128)(2,1)} collective-permute-done((bf16[2,1024,128]{2,1,0:T(8,128)(2,1)}, bf16[2,1024,128]{2,1,0:T(8,128)(2,1)}, u32[]{:S(2)}, u32[]{:S(2)}) %collective-permute-start.67) | collective-permute-done | bytes 524320 | tf_op jit(solution)/shard_map/ppermute | solution.py:682
  1163.9 15.6 %convolution_convert_fusion.1 = bf16[2048,1152]{1,0:T(8,128)(2,1)S(1)} fusion(bf16[2048,1152]{1,0:T(8,128)(2,1)S(1)} %get-tuple-element.53, bf16[1024,2048]{1,0:T(8,128)(2,1)} %collective-permute-done.5, bf16[1024,2048]{1,0:T(8,128)(2,1)} %fusion.21), kind=kOutput, calls=%fused_computation.58 | convolution fusion | flops 9682812928 | bytes 17825792 | tf_op jit(solution)/shard_map/dot_general | solution.py:336
  1254.6 14.1 %fusion.26 = (f32[2048]{0:T(1024)S(1)}, f32[1024]{0:T(1024)S(1)}, f32[1024]{0:T(1024)S(1)}, f32[2048]{0:T(1024)S(1)}, f32[1024,2048]{1,0:T(8,128)}) fusion(bf16[2,512,2048]{2,1,0:T(8,128)(2,1)} %param.15, f32[1024]{0:T(1024)S(1)} %bitcast.393, f32[1024]{0:T(1024)S(1)} %bitcast.396, f32[2048]{0:T(1024)S(1)} %copy-done.54, ...), kind=kOutput, calls=%fused_computation.43 | convolution fusion | flops 4856997888 | bytes 23896064 | tf_op jit(solution)/shard_map/dot_general | solution.py:340
  (605 shorter events, 616.5 us)
Async XLA Ops:
  7.2 400.8 %all-gather.3.cloned.1.call-start = ((), (), s32[]{:S(2)}) async-start(), calls=%async_computation.4 | async-start | bytes 17825792 | tf_op jit(solution)/shard_map/all_gather | solution.py:569
  15.2 535.1 %all-gather.5.cloned.1.call-start = ((), (), s32[]{:S(2)}) async-start(), calls=%async_computation.5 | async-start | bytes 17825792 | tf_op jit(solution)/shard_map/all_gather | solution.py:569
  43.5 157.8 %collective-permute-start.5 = (bf16[1024,2048]{1,0:T(8,128)(2,1)}, bf16[1024,2048]{1,0:T(8,128)(2,1)}, u32[]{:S(2)}, u32[]{:S(2)}) collective-permute-start(bf16[1024,2048]{1,0:T(8,128)(2,1)} %fusion.21), channel_id=1, source_target_pairs={{0,1},{1,0},{2,3},{3,2},{4,5},{5,4},{6,7},{7,6},{8,9},{9,8},{10,11... | collective-permute-start | bytes 12582920 | tf_op jit(solution)/shard_map/ppermute | solution.py:368
  57.1 60.2 %collective-permute-start.13 = (bf16[2,64,1152]{2,1,0:T(8,128)(2,1)S(1)}, bf16[2,64,1152]{2,1,0:T(8,128)(2,1)S(1)}, u32[]{:S(2)}, u32[]{:S(2)}) collective-permute-start(bf16[2,64,1152]{2,1,0:T(8,128)(2,1)S(1)} %maximum_select_fusion.8.refs_2_), channel_id=1, source_target_pairs={{0,2},{2,4},{4,6},{6,0},{1,3},{3,5},{5,7},{7,1},{8,10},{10,12},{12... | collective-permute-start | bytes 884744 | tf_op jit(solution)/shard_map/ppermute | solution.py:448
  64.6 55.3 %collective-permute-start.10 = (bf16[2,64,1152]{2,1,0:T(8,128)(2,1)S(1)}, bf16[2,64,1152]{2,1,0:T(8,128)(2,1)S(1)}, u32[]{:S(2)}, u32[]{:S(2)}) collective-permute-start(bf16[2,64,1152]{2,1,0:T(8,128)(2,1)S(1)} %maximum_select_fusion.8.refs_2_), channel_id=1, source_target_pairs={{0,16},{16,0},{1,17},{17,1},{2,18},{18,2},{3,19},{19,3},{4,20},{20... | collective-permute-start | bytes 884744 | tf_op jit(solution)/shard_map/ppermute | solution.py:449
  141.8 58.4 %collective-permute-start.37 = (bf16[2,64,1024]{2,1,0:T(8,128)(2,1)S(1)}, bf16[2,64,1024]{2,1,0:T(8,128)(2,1)}, u32[]{:S(2)}, u32[]{:S(2)}) collective-permute-start(bf16[2,64,1024]{2,1,0:T(8,128)(2,1)S(1)} %maximum_select_fusion.11.refs_2_), channel_id=1, source_target_pairs={{0,2},{2,4},{4,6},{6,0},{1,3},{3,5},{5,7},{7,1},{8,10},{10,12},{12... | collective-permute-start | bytes 786440 | tf_op jit(solution)/shard_map/ppermute | solution.py:448
  342.1 635.0 %reduce-scatter.5.cloned.1.call-start = ((), (), s32[]{:S(2)}) async-start(), calls=%async_computation.6 | async-start | bytes 5242880 | tf_op jit(solution)/shard_map/reduce_scatter | solution.py:479
  517.6 135.2 %collective-permute-start.51 = (bf16[2,4,128,2048]{3,2,1,0:T(8,128)(2,1)}, bf16[2,4,128,2048]{3,2,1,0:T(8,128)(2,1)}, u32[]{:S(2)}, u32[]{:S(2)}) collective-permute-start(bf16[2,4,128,2048]{3,2,1,0:T(8,128)(2,1)} %dynamic-slice_bitcast_fusion.3.refs_3_), channel_id=1, source_target_pairs={{0,16},{16,0},{1,17},{17,1},{2,18},{18,2},{3,19},{19,3},{4,20},{20... | collective-permute-start | bytes 12582920 | tf_op jit(solution)/shard_map/ppermute | solution.py:368
  524.5 128.2 %collective-permute-start.52 = (bf16[2,4,128,2048]{3,2,1,0:T(8,128)(2,1)}, bf16[2,4,128,2048]{3,2,1,0:T(8,128)(2,1)}, u32[]{:S(2)}, u32[]{:S(2)}) collective-permute-start(bf16[2,4,128,2048]{3,2,1,0:T(8,128)(2,1)} %dynamic-slice_bitcast_fusion.2.refs_4_), channel_id=1, source_target_pairs={{0,8},{8,0},{1,9},{9,1},{2,10},{10,2},{3,11},{11,3},{4,12},{12,4},... | collective-permute-start | bytes 12582920 | tf_op jit(solution)/shard_map/ppermute | solution.py:368
  646.0 93.8 %collective-permute-start.59 = (bf16[2,4,64,4096]{3,2,1,0:T(8,128)(2,1)}, bf16[2,4,64,4096]{3,2,1,0:T(8,128)(2,1)}, u32[]{:S(2)}, u32[]{:S(2)}) collective-permute-start(bf16[2,4,64,4096]{3,2,1,0:T(8,128)(2,1)} %dynamic-slice_bitcast_fusion.refs_5_), channel_id=1, source_target_pairs={{0,8},{8,0},{1,9},{9,1},{2,10},{10,2},{3,11},{11,3},{4,12},{12,4},... | collective-permute-start | bytes 12582920 | tf_op jit(solution)/shard_map/ppermute | solution.py:368
  652.2 93.8 %collective-permute-start.58 = (bf16[2,4,64,4096]{3,2,1,0:T(8,128)(2,1)}, bf16[2,4,64,4096]{3,2,1,0:T(8,128)(2,1)}, u32[]{:S(2)}, u32[]{:S(2)}) collective-permute-start(bf16[2,4,64,4096]{3,2,1,0:T(8,128)(2,1)} %dynamic-slice_bitcast_fusion.1.refs_4_), channel_id=1, source_target_pairs={{0,16},{16,0},{1,17},{17,1},{2,18},{18,2},{3,19},{19,3},{4,20},{20... | collective-permute-start | bytes 12582920 | tf_op jit(solution)/shard_map/ppermute | solution.py:368
  663.0 121.8 %collective-permute-start.54 = (bf16[4,128,2048]{2,1,0:T(8,128)(2,1)S(1)}, bf16[4,128,2048]{2,1,0:T(8,128)(2,1)}, u32[]{:S(2)}, u32[]{:S(2)}) collective-permute-start(bf16[4,128,2048]{2,1,0:T(8,128)(2,1)S(1)} %dynamic-slice_bitcast_fusion.7.refs_2_), channel_id=1, source_target_pairs={{0,8},{8,0},{1,9},{9,1},{2,10},{10,2},{3,11},{11,3},{4,12},{12,4},... | collective-permute-start | bytes 6291464 | tf_op jit(solution)/shard_map/ppermute | solution.py:368
  688.3 104.4 %collective-permute-start.53 = (bf16[1024,2048]{1,0:T(8,128)(2,1)}, bf16[1024,2048]{1,0:T(8,128)(2,1)}, u32[]{:S(2)}, u32[]{:S(2)}) collective-permute-start(bf16[1024,2048]{1,0:T(8,128)(2,1)} %grad_normed2.1), channel_id=1, source_target_pairs={{0,1},{1,0},{2,3},{3,2},{4,5},{5,4},{6,7},{7,6},{8,9},{9,8},{10,11... | collective-permute-start | bytes 12582920 | tf_op jit(solution)/shard_map/ppermute | solution.py:368
  712.4 76.5 %collective-permute-start.55 = (bf16[4,128,2048]{2,1,0:T(8,128)(2,1)S(1)}, bf16[4,128,2048]{2,1,0:T(8,128)(2,1)S(1)}, u32[]{:S(2)}, u32[]{:S(2)}) collective-permute-start(bf16[4,128,2048]{2,1,0:T(8,128)(2,1)S(1)} %copy-done.46), channel_id=1, source_target_pairs={{0,16},{16,0},{1,17},{17,1},{2,18},{18,2},{3,19},{19,3},{4,20},{20... | collective-permute-start | bytes 6291464 | tf_op jit(solution)/shard_map/ppermute | solution.py:368
  756.8 105.4 %collective-permute-start.60 = (bf16[4,64,4096]{2,1,0:T(8,128)(2,1)}, bf16[4,64,4096]{2,1,0:T(8,128)(2,1)}, u32[]{:S(2)}, u32[]{:S(2)}) collective-permute-start(bf16[4,64,4096]{2,1,0:T(8,128)(2,1)} %dynamic-slice_bitcast_fusion.5.refs_2_), channel_id=1, source_target_pairs={{0,8},{8,0},{1,9},{9,1},{2,10},{10,2},{3,11},{11,3},{4,12},{12,4},... | collective-permute-start | bytes 6291464 | tf_op jit(solution)/shard_map/ppermute | solution.py:368
  792.6 345.6 %reduce-scatter.11.cloned.1.call-start = ((), (), s32[]{:S(2)}) async-start(), calls=%async_computation.9 | async-start | bytes 5242880 | tf_op jit(solution)/shard_map/reduce_scatter | solution.py:479
  862.1 74.2 %collective-permute-start.56 = (bf16[1024,2048]{1,0:T(8,128)(2,1)}, bf16[1024,2048]{1,0:T(8,128)(2,1)}, u32[]{:S(2)}, u32[]{:S(2)}) collective-permute-start(bf16[1024,2048]{1,0:T(8,128)(2,1)} %mixed_out.1), channel_id=1, source_target_pairs={{0,1},{1,0},{2,3},{3,2},{4,5},{5,4},{6,7},{7,6},{8,9},{9,8},{10,11... | collective-permute-start | bytes 12582920 | tf_op jit(solution)/shard_map/ppermute | solution.py:368
  890.8 332.8 %reduce-scatter.9.cloned.1.call-start = ((), (), s32[]{:S(2)}) async-start(), calls=%async_computation.8 | async-start | bytes 1310720 | tf_op jit(solution)/shard_map/reduce_scatter | solution.py:479
  1017.7 101.3 %collective-permute-start.65 = (bf16[2,1024,128]{2,1,0:T(8,128)(2,1)}, bf16[2,1024,128]{2,1,0:T(8,128)(2,1)}, u32[]{:S(2)}, u32[]{:S(2)}) collective-permute-start(bf16[2,1024,128]{2,1,0:T(8,128)(2,1)} %slice_bitcast_fusion), channel_id=1, source_target_pairs={{0,2},{2,4},{4,6},{6,0},{1,3},{3,5},{5,7},{7,1},{8,10},{10,12},{12... | collective-permute-start | bytes 1572872 | tf_op jit(solution)/shard_map/ppermute | solution.py:682
  1044.8 75.5 %collective-permute-start.79 = (bf16[4,64,1024]{2,1,0:T(8,128)(2,1)S(1)}, bf16[4,64,1024]{2,1,0:T(8,128)(2,1)S(1)}, u32[]{:S(2)}, u32[]{:S(2)}) collective-permute-start(bf16[4,64,1024]{2,1,0:T(8,128)(2,1)S(1)} %dynamic-slice_bitcast_fusion.16.refs_0_), channel_id=1, source_target_pairs={{0,8},{8,0},{1,9},{9,1},{2,10},{10,2},{3,11},{11,3},{4,12},{12,4},... | collective-permute-start | bytes 1572872 | tf_op jit(solution)/shard_map/ppermute | solution.py:368
  1045.4 76.1 %collective-permute-start.80 = (bf16[4,64,1024]{2,1,0:T(8,128)(2,1)S(1)}, bf16[4,64,1024]{2,1,0:T(8,128)(2,1)S(1)}, u32[]{:S(2)}, u32[]{:S(2)}) collective-permute-start(bf16[4,64,1024]{2,1,0:T(8,128)(2,1)S(1)} %dynamic-slice_bitcast_fusion.15.refs_1_), channel_id=1, source_target_pairs={{0,16},{16,0},{1,17},{17,1},{2,18},{18,2},{3,19},{19,3},{4,20},{20... | collective-permute-start | bytes 1572872 | tf_op jit(solution)/shard_map/ppermute | solution.py:368
  1137.7 143.4 %reduce-scatter.7.cloned.1.call-start = ((), (), s32[]{:S(2)}) async-start(), calls=%async_computation.7 | async-start | bytes 1474560 | tf_op jit(solution)/shard_map/reduce_scatter | solution.py:479
  1140.9 79.2 %collective-permute-start.87 = (f32[64,4096]{1,0:T(8,128)}, f32[64,4096]{1,0:T(8,128)}, u32[]{:S(2)}, u32[]{:S(2)}) collective-permute-start(f32[64,4096]{1,0:T(8,128)} %get-tuple-element.75), channel_id=1, source_target_pairs={{0,1},{1,0},{2,3},{3,2},{4,5},{5,4},{6,7},{7,6},{8,9},{9,8},{10,11... | collective-permute-start | bytes 3145736 | tf_op jit(solution)/shard_map/ppermute | solution.py:368
  1189.8 64.8 %collective-permute-start.68 = (bf16[1024,2048]{1,0:T(8,128)(2,1)}, bf16[1024,2048]{1,0:T(8,128)(2,1)}, u32[]{:S(2)}, u32[]{:S(2)}) collective-permute-start(bf16[1024,2048]{1,0:T(8,128)(2,1)} %convolution_convert_fusion.2), channel_id=1, source_target_pairs={{0,1},{1,0},{2,3},{3,2},{4,5},{5,4},{6,7},{7,6},{8,9},{9,8},{10,11... | collective-permute-start | bytes 12582920 | tf_op jit(solution)/shard_map/ppermute | solution.py:368
  (166 other events, 3157.7 us)
Sparse Core Ops, SparseCore 0:
  15.3 265.1 all-gather.2
  342.3 207.9 all-gather.4
  792.7 87.3 reduce-scatter.4
  890.9 87.9 reduce-scatter.10
  1137.8 30.9 reduce-scatter.8
  1254.6 26.3 reduce-scatter.6

commit v2 on v1

--- a/solution.py
+++ b/solution.py
@@ -262,74 +262,103 @@
     ).astype(jnp.int32)
 
 
-def matmul_kernel(kind, chunk, n_extra, n_out, n_deps, finish, *refs):
-    a_ref, b_ref = refs[0], refs[1]
-    extras = refs[2:2+n_extra]
-    outs = refs[2+n_extra+n_deps:2+n_extra+n_deps+n_out]
-    scratch = refs[2+n_extra+n_deps+n_out:]
-    if kind == "tn":
-        turned = scratch[0]
-        @pl.when(pl.program_id(1) == 0)
-        def _():
-            turned[...] = jnp.transpose(a_ref[...])
-        left = turned
-    else:
-        left = a_ref
-    rows = left.shape[0]
-    for r in range(0, rows, chunk):
-        part = pl.ds(r, chunk)
-        if kind == "nt":
-            total = lax.dot_general(left[part, :], b_ref[...], (((1,), (1,)), ((), ())), preferred_element_type=F32)
-        else:
-            total = jnp.dot(left[part, :], b_ref[...], preferred_element_type=F32)
-        finish(part, total, extras, outs)
-
-
 def store(part, total, extras, outs):
     outs[0][part, :] = total.astype(outs[0].dtype)
 
 
-def matmul(kind, a, b, outs, finish=store, extras=(), tm=1024, tn=512, chunk=256, deps=(), a_rows=None, name="matmul"):
-    if kind == "tn":
-        k, m = a.shape; n = b.shape[1]
-    elif kind == "nt":
-        m, k = a.shape; n = b.shape[0]
+def sum_finish(part, total, extras, outs):
+    total = total + extras[0][part, :] + extras[1][...] + extras[2][part, :].astype(F32)
+    outs[0][part, :] = total.astype(BF16)
+
+
+def slope_finish(part, total, extras, outs):
+    grad = (total * extras[0][part, :].astype(F32)).astype(BF16)
+    outs[0][part, :] = grad
+    sums = jnp.sum(grad.astype(F32).reshape(-1, 8, grad.shape[1]), axis=0)
+    if part.start == 0:
+        outs[1][...] = sums
     else:
-        m, k = a.shape; n = b.shape[1]
-    first = 0
-    if a_rows is not None:
-        first, m = a_rows
-    tm = min(tm, m); tn = min(tn, n); chunk = min(chunk, tm)
-    f0 = first // tm
-    a_spec = pl.BlockSpec((k, tm), lambda i, j: (0, i)) if kind == "tn" else pl.BlockSpec((tm, k), lambda i, j: (i + f0, 0))
-    b_spec = pl.BlockSpec((tn, k), lambda i, j: (j, 0)) if kind == "nt" else pl.BlockSpec((k, tn), lambda i, j: (0, j))
-    tile = pl.BlockSpec((tm, tn), lambda i, j: (i, j))
-    row = pl.BlockSpec((1, tn), lambda i, j: (0, j))
-    spec = {"tile": tile, "row": row, "part": pl.BlockSpec((1, 8, tn), lambda i, j: (i, 0, j))}
-    shape = {"tile": (m, n), "row": (1, n), "part": (m // tm, 8, n)}
-    out_shape = [jax.ShapeDtypeStruct(shape[w], d) for d, w in outs]
+        outs[1][...] += sums
+
+
+def gelu_finish(part, total, extras, outs):
+    u = total + extras[0][...]
+    square = u * u
+    s = 0.5 * jnp.tanh(u * (0.7978845608028654 + (0.7978845608028654 * 0.044715) * square)) + 0.5
+    value = u * s
+    outs[0][part, :] = value.astype(BF16)
+    rate = 2 * 0.7978845608028654 + (6 * 0.7978845608028654 * 0.044715) * square
+    outs[1][part, :] = (s + value * (1.0 - s) * rate).astype(BF16)
+
+
+def rows_kernel(kind, chunk, extra_count, dep_count, finish, a_ref, b_ref, *refs):
+    extras, outs = refs[:extra_count], refs[extra_count + dep_count :]
+    dot = contract_cols if kind == "nt" else plain_dot
+    for r in range(0, a_ref.shape[0], chunk):
+        part = pl.ds(r, chunk)
+        finish(part, dot(a_ref[part, :], b_ref[...]), extras, outs)
+
+
+def matmul(kind, a, b, outs, finish=store, extras=(), tn=512, chunk=256, deps=(), name="matmul"):
+    m, k = a.shape
+    n = b.shape[0] if kind == "nt" else b.shape[1]
+    tn, chunk = min(tn, n), min(chunk, m)
+    tile = pl.BlockSpec((m, tn), lambda j: (0, j))
+    spec = {
+        "tile": tile,
+        "row": pl.BlockSpec((1, tn), lambda j: (0, j)),
+        "sums": pl.BlockSpec((8, tn), lambda j: (0, j)),
+    }
+    shape = {"tile": (m, n), "sums": (8, n)}
     res = pl.pallas_call(
-        functools.partial(matmul_kernel, kind, chunk, len(extras), len(outs), len(deps), finish),
+        functools.partial(rows_kernel, kind, chunk, len(extras), len(deps), finish),
+        grid=(n // tn,),
+        in_specs=[
+            pl.BlockSpec((m, k), lambda j: (0, 0)),
+            pl.BlockSpec((tn, k), lambda j: (j, 0)) if kind == "nt" else pl.BlockSpec((k, tn), lambda j: (0, j)),
+        ]
+        + [spec[kind_of] for _, kind_of in extras]
+        + [pl.BlockSpec(memory_space=pl.ANY)] * len(deps),
+        out_specs=[spec[w] for _, w in outs],
+        out_shape=[jax.ShapeDtypeStruct(shape[w], d) for d, w in outs],
+        compiler_params=pltpu.CompilerParams(vmem_limit_bytes=52 * 2**20),
+        cost_estimate=pl.CostEstimate(flops=2 * m * n * k, bytes_accessed=2 * (m * k + n * k + m * n), transcendentals=0),
+        name=name,
+    )(a, b, *[array for array, _ in extras], *deps)
+    return res[0] if len(outs) == 1 else res
+
+
+def tokens_kernel(chunk, dep_count, a0_ref, a1_ref, b0_ref, b1_ref, *refs):
+    out, left = refs[dep_count:]
+
+    @pl.when(pl.program_id(1) == 0)
+    def _():
+        left[0] = jnp.transpose(a0_ref[...])
+        left[1] = jnp.transpose(a1_ref[...])
+
+    for r in range(0, left.shape[1], chunk):
+        part = pl.ds(r, chunk)
+        out[part, :] = (plain_dot(left[0, part, :], b0_ref[...]) + plain_dot(left[1, part, :], b1_ref[...])).astype(BF16)
+
+
+def over_tokens(a, b, tm=2048, tn=512, chunk=256, deps=(), b_cols=None, name="weight_gradient"):
+    k, m = a[0].shape
+    first, n = b_cols or (0, b[0].shape[1])
+    tm, tn, chunk = min(tm, m), min(tn, n), min(chunk, m)
+    skip = first // tn
+    a_spec = pl.BlockSpec((k, tm), lambda i, j: (0, i))
+    b_spec = pl.BlockSpec((k, tn), lambda i, j: (0, j + skip))
+    return pl.pallas_call(
+        functools.partial(tokens_kernel, chunk, len(deps)),
         grid=(m // tm, n // tn),
-        in_specs=[a_spec, b_spec] + [spec[w] for _, w in extras] + [pl.BlockSpec(memory_space=pl.ANY)] * len(deps),
-        out_specs=[spec[w] for _, w in outs],
-        scratch_shapes=[pltpu.VMEM((tm, k), BF16)] if kind == "tn" else [],
-        out_shape=out_shape,
+        in_specs=[a_spec, a_spec, b_spec, b_spec] + [pl.BlockSpec(memory_space=pl.ANY)] * len(deps),
+        out_specs=pl.BlockSpec((tm, tn), lambda i, j: (i, j)),
+        scratch_shapes=[pltpu.VMEM((2, tm, k), BF16)],
+        out_shape=jax.ShapeDtypeStruct((m, n), BF16),
         compiler_params=pltpu.CompilerParams(vmem_limit_bytes=52 * 2**20),
-        cost_estimate=pl.CostEstimate(flops=2*m*n*k, bytes_accessed=2*(m*k+n*k+m*n), transcendentals=0),
+        cost_estimate=pl.CostEstimate(flops=4 * m * n * k, bytes_accessed=4 * (m * k + n * k + m * n), transcendentals=0),
         name=name,
-    )(a, b, *[e for e, _ in extras], *deps)
-    return res[0] if len(outs) == 1 else res
-
-
-def slope_finish(part, total, extras, outs):
-    g = (total * extras[0][part, :].astype(F32)).astype(BF16)
-    outs[0][part, :] = g
-    sums = jnp.sum(g.astype(F32).reshape(-1, 8, g.shape[1]), axis=0)
-    if part.start == 0:
-        outs[1][0] = sums
-    else:
-        outs[1][0] += sums
+    )(*a, *b, *deps)
 
 
 def contract_rows(left_op, right_op):
@@ -351,17 +380,55 @@
     return centred * inverse, inverse
 
 
-def norm_backward(unit, inverse, gain, grad):
-    scaled = grad * gain
+def norm_kernel(rounded, dep_count, own_ref, got_ref, unit_ref, inverse_ref, gain_ref, base_ref, *refs):
+    outs = refs[dep_count:]
+    grad = own_ref[...] + got_ref[...].astype(F32)
+    unit = unit_ref[...]
+    scaled = grad * gain_ref[...]
     inner = jnp.mean(scaled * unit, axis=-1, keepdims=True)
-    return (scaled - jnp.mean(scaled, axis=-1, keepdims=True) - unit * inner) * inverse
-
-
-def gelu_parts(u):
-    inner = 0.7978845608028654 * (u + 0.044715 * u * u * u)
-    t = jnp.tanh(inner)
-    slope = 0.5 * (1.0 + t) + 0.5 * u * (1.0 - t * t) * 0.7978845608028654 * (1.0 + 3 * 0.044715 * u * u)
-    return 0.5 * u * (1.0 + t), slope
+    level = jnp.mean(scaled, axis=-1, keepdims=True)
+    result = base_ref[...].astype(F32) + (scaled - level - unit * inner) * inverse_ref[...][:, :1]
+    outs[0][...] = result
+    terms = [grad * unit, grad]
+    if rounded:
+        low = result.astype(BF16)
+        outs[3][...] = low
+        terms.append(low.astype(F32))
+    first = pl.program_id(0) == 0
+    for term, out in zip(terms, (outs[1], outs[2], outs[-1])):
+        sums = jnp.sum(term.reshape(-1, 8, term.shape[1]), axis=0)
+
+        @pl.when(first)
+        def _(out=out, sums=sums):
+            out[...] = sums
+
+        @pl.when(jnp.logical_not(first))
+        def _(out=out, sums=sums):
+            out[...] += sums
+
+
+def norm_backward(own, got, unit, inverse, gain, base, rounded, deps=()):
+    rows, cols = own.shape
+    tile = min(128, rows)
+    block = pl.BlockSpec((tile, cols), lambda i: (i, 0))
+    sums = pl.BlockSpec((8, cols), lambda i: (0, 0))
+    sums_shape = jax.ShapeDtypeStruct((8, cols), F32)
+    out_specs, out_shape = [block, sums, sums], [jax.ShapeDtypeStruct((rows, cols), F32), sums_shape, sums_shape]
+    if rounded:
+        out_specs += [block, sums]
+        out_shape += [jax.ShapeDtypeStruct((rows, cols), BF16), sums_shape]
+    return pl.pallas_call(
+        functools.partial(norm_kernel, rounded, len(deps)),
+        grid=(rows // tile,),
+        in_specs=[
+            block, block, block, pl.BlockSpec((tile, HD), lambda i: (i, 0)), pl.BlockSpec((1, cols), lambda i: (0, 0)), block,
+        ]
+        + [pl.BlockSpec(memory_space=pl.ANY)] * len(deps),
+        out_specs=out_specs,
+        out_shape=out_shape,
+        compiler_params=pltpu.CompilerParams(vmem_limit_bytes=40 * 2**20),
+        name="norm_backward",
+    )(own, got, unit, jnp.broadcast_to(inverse, (rows, HD)), gain.reshape(1, cols), base, *deps)
 
 
 def swap(values, axis):
@@ -387,23 +454,46 @@
     return in_order(core, own, other).reshape(2 * own.shape[0], own.shape[1])
 
 
-def place_kernel(steps, half, spot, *refs):
-    pieces, out, held, arrive, leave = refs[: 4 * steps], *refs[4 * steps :]
+def hold_kernel(dep_count, value_ref, *refs):
+    refs[dep_count][...] = value_ref[...]
+
+
+def hold(value, *deps):
+    whole = pl.BlockSpec(value.shape, lambda: (0,) * value.ndim)
+    return pl.pallas_call(
+        functools.partial(hold_kernel, len(deps)),
+        in_specs=[whole] + [pl.BlockSpec(memory_space=pl.ANY)] * len(deps),
+        out_specs=whole,
+        out_shape=jax.ShapeDtypeStruct(value.shape, value.dtype),
+        name="hold",
+    )(value, *deps)
+
+
+def place_kernel(moves_of, whole_count, half, dep_count, spot, *refs):
+    count = len(moves_of)
+    pieces = refs[:count]
+    whole = refs[count : count + whole_count]
+    out, held, arrive, leave = refs[count + whole_count + dep_count :]
     y, x, z = spot[0], spot[1], spot[2]
+    steps = count // 4
+    parts = 2 + whole_count * 2
     moves = []
-    for s in range(steps):
+    for n, move in enumerate(moves_of):
+        s, k = move
         from_z = lax.rem(z - s + steps, steps)
         for i in range(2):
-            for k, to in enumerate(((i, x, 0), (i, 1 - x, 0), (y, i, 1), (1 - y, i, 1))):
-                row = (((to[0] * 2 + to[1]) * steps + from_z) * 2 + to[2]) * half
-                moves.append((4 * s + k, i, pl.multiple_of(row, half)))
-    inward = [
-        pltpu.make_async_copy(pieces[p].at[i], held.at[n], arrive.at[n]) for n, (p, i, _) in enumerate(moves)
-    ]
-    outward = [
-        pltpu.make_async_copy(held.at[n], out.at[pl.ds(row, half), :], leave.at[n])
-        for n, (_, _, row) in enumerate(moves)
-    ]
+            to = ((i, x, 0), (i, 1 - x, 0), (y, i, 1), (1 - y, i, 1))[k]
+            row = (((to[0] * 2 + to[1]) * steps + from_z) * parts + whole_count * 2 + to[2]) * half
+            moves.append((pieces[n].at[i], pl.multiple_of(row, half), half))
+    for array in whole:
+        for chip in range(4 * steps):
+            moves.append((array.at[pl.ds(chip * 2 * half, 2 * half), :], chip * parts * half, 2 * half))
+    inward, outward, at = [], [], 0
+    for n, (source, row, rows) in enumerate(moves):
+        here = held.at[pl.ds(at, rows), :]
+        inward.append(pltpu.make_async_copy(source, here, arrive.at[n]))
+        outward.append(pltpu.make_async_copy(here, out.at[pl.ds(row, rows), :], leave.at[n]))
+        at += rows
     for copy in inward:
         copy.start()
     for n, copy in enumerate(inward):
@@ -413,71 +503,170 @@
         copy.wait()
 
 
-def place(pieces, spot):
+def place(pieces, spot, whole=(), deps=()):
     steps = len(pieces) // 4
     _, half, cols = pieces[0].shape
+    count = 8 * steps + 4 * steps * len(whole)
+    rows = 8 * steps * half * (1 + len(whole))
+    moves_of = [(s, k) for s in range(steps) for k in range(4)]
     return pl.pallas_call(
-        functools.partial(place_kernel, steps, half),
+        functools.partial(place_kernel, moves_of, len(whole), half, len(deps)),
         grid_spec=pltpu.PrefetchScalarGridSpec(
             num_scalar_prefetch=1,
             grid=(1,),
-            in_specs=[pl.BlockSpec(memory_space=pl.ANY)] * len(pieces),
+            in_specs=[pl.BlockSpec(memory_space=pl.ANY)] * (len(pieces) + len(whole) + len(deps)),
             out_specs=pl.BlockSpec(memory_space=pl.ANY),
             scratch_shapes=[
-                pltpu.VMEM((8 * steps, half, cols), BF16),
-                pltpu.SemaphoreType.DMA((8 * steps,)),
-                pltpu.SemaphoreType.DMA((8 * steps,)),
+                pltpu.VMEM((rows, cols), BF16),
+                pltpu.SemaphoreType.DMA((count,)),
+                pltpu.SemaphoreType.DMA((count,)),
             ],
         ),
-        out_shape=jax.ShapeDtypeStruct((8 * steps * half, cols), BF16),
+        out_shape=jax.ShapeDtypeStruct((rows, cols), BF16),
         compiler_params=pltpu.CompilerParams(vmem_limit_bytes=32 * 2**20),
         name="place_weight",
-    )(spot, *pieces)
+    )(spot, *pieces, *whole, *deps)
 
 
 def gather_pieces(block, y, x, chips_z):
     half = block.shape[0] // 2
     ring = [(i, (i + 1) % chips_z) for i in range(chips_z)]
     one, two = block[:half], block[half:]
-    got_one, got_two = lax.ppermute(one, "y", PAIR), lax.ppermute(two, "x", PAIR)
+    got_one, got_two = swap(one, "y"), swap(two, "x")
     one, two = in_order(y, one, got_one), in_order(x, two, got_two)
-    pieces = []
+    pieces, stages = [], []
     for s in range(chips_z):
-        last = s == chips_z - 1
-        next_one = None if last else lax.ppermute(one, "z", ring)
-        next_two = None if last else lax.ppermute(two, "z", ring)
-        pieces += [one, lax.ppermute(one, "x", PAIR), two, lax.ppermute(two, "y", PAIR)]
-        one, two = next_one, next_two
-    return pieces
+        stages.append((one, two))
+        pieces += [one, swap(one, "x"), two, swap(two, "y")]
+        if s < chips_z - 1:
+            one, two = lax.ppermute(one, "z", ring), lax.ppermute(two, "z", ring)
+    return pieces, stages
+
+
+def fold_kernel(spot, own_one, own_two, got_one, got_two, *refs):
+    keep_one, send_one, keep_two, send_two = refs[-4:]
+    y, x = spot[0], spot[1]
+    for mine, own, got, keep, send in ((x, own_one, got_one, keep_one, send_one), (y, own_two, got_two, keep_two, send_two)):
+        for index, out in ((mine, keep), (1 - mine, send)):
+            total = own[own_at(own, index)].astype(F32) + got[index, 0].astype(F32)
+            out[0] = total.astype(BF16)
+
+
+def own_at(ref, index):
+    return (index, 0, 0, 0) if ref.shape[0] == 2 else (0, index, 0, 0)
+
+
+def fold_again_kernel(count, *refs):
+    out = refs[-1]
+    cols = out.shape[-1] // count
+    for n in range(count):
+        keep_one, keep_two, got_one, got_two = refs[4 * n : 4 * n + 4]
+        here = pl.ds(n * cols, cols)
+        out[0, 0, :, here] = (keep_one[0].astype(F32) + got_one[0].astype(F32)).astype(BF16)
+        out[0, 1, :, here] = (keep_two[0].astype(F32) + got_two[0].astype(F32)).astype(BF16)
 
 
 class Sum:
-    def __init__(self, total, y, x, chips_z):
+    def __init__(self, total, spot, chips_z):
         self.cols = total.shape[1]
         self.half = total.shape[0] // (8 * chips_z)
-        self.total, self.y, self.x, self.chips_z = total.reshape(2, 2, chips_z, 2, self.half, self.cols), y, x, chips_z
-        self.sent = (self.cut(0, 1 - y, 0), self.cut(1, 1 - x, 1))
+        self.total, self.spot, self.chips_z = total.reshape(2, 2, chips_z, 2, self.half, self.cols), spot, chips_z
+        self.sent = (self.cut(0, 1 - spot[0], 0), self.cut(1, 1 - spot[1], 1))
 
     def cut(self, dim, index, part):
         at, size = [0, 0, 0, part, 0, 0], [2, 2, self.chips_z, 1, self.half, self.cols]
         at[dim], size[dim] = index, 1
         return lax.dynamic_slice(self.total, at, size).reshape(2, self.chips_z, self.half, self.cols)
 
-    def first(self):
-        one, two = swap(self.sent[0], "y"), swap(self.sent[1], "x")
-        self.one = (self.cut(0, self.y, 0).astype(F32) + one.astype(F32)).astype(BF16)
-        self.two = (self.cut(1, self.x, 1).astype(F32) + two.astype(F32)).astype(BF16)
-        self.sent = (pick(self.one, 1 - self.x, 0), pick(self.two, 1 - self.y, 0))
-
-    def second(self):
-        one, two = swap(self.sent[0], "x"), swap(self.sent[1], "y")
-        one = (pick(self.one, self.x, 0).astype(F32) + one.astype(F32)).astype(BF16)
-        two = (pick(self.two, self.y, 0).astype(F32) + two.astype(F32)).astype(BF16)
-        self.both = jnp.stack([one, two], axis=1).reshape(-1, self.cols)
+    def first(self, *deps):
+        got = (swap(self.sent[0], "y"), swap(self.sent[1], "x"))
+        block = (self.half, self.cols)
+        got_spec = pl.BlockSpec((2, 1, *block), lambda z, spot: (0, z, 0, 0))
+        out_spec = pl.BlockSpec((1, *block), lambda z, spot: (z, 0, 0))
+        keep_one, send_one, keep_two, send_two = pl.pallas_call(
+            fold_kernel,
+            grid_spec=pltpu.PrefetchScalarGridSpec(
+                num_scalar_prefetch=1,
+                grid=(self.chips_z,),
+                in_specs=[
+                    pl.BlockSpec((1, 2, 1, 1, *block), lambda z, spot: (spot[0], 0, z, 0, 0, 0)),
+                    pl.BlockSpec((2, 1, 1, 1, *block), lambda z, spot: (0, spot[1], z, 1, 0, 0)),
+                    got_spec,
+                    got_spec,
+                ]
+                + [pl.BlockSpec(memory_space=pl.ANY)] * len(deps),
+                out_specs=[out_spec] * 4,
+            ),
+            out_shape=[jax.ShapeDtypeStruct((self.chips_z, *block), BF16)] * 4,
+            compiler_params=pltpu.CompilerParams(vmem_limit_bytes=32 * 2**20),
+            name="fold",
+        )(self.spot, self.total, self.total, *got, *deps)
+        self.keep, self.sent = (keep_one, keep_two), (send_one, send_two)
+
+    def second(self, *deps, beside=()):
+        sums = (self, *beside)
+        arrays = []
+        for one in sums:
+            arrays += [*one.keep, swap(one.sent[0], "x"), swap(one.sent[1], "y")]
+        self.cols *= len(sums)
+        self.both = pl.pallas_call(
+            functools.partial(fold_again_kernel, len(sums)),
+            grid=(self.chips_z,),
+            in_specs=[pl.BlockSpec((1, *array.shape[1:]), lambda z: (z, 0, 0)) for array in arrays]
+            + [pl.BlockSpec(memory_space=pl.ANY)] * len(deps),
+            out_specs=pl.BlockSpec((1, 2, self.half, self.cols), lambda z: (z, 0, 0, 0)),
+            out_shape=jax.ShapeDtypeStruct((self.chips_z, 2, self.half, self.cols), BF16),
+            compiler_params=pltpu.CompilerParams(vmem_limit_bytes=32 * 2**20),
+            name="fold_again",
+        )(*arrays, *deps).reshape(-1, self.cols)
+
+    def round_z(self, ring):
+        z = self.spot[2]
+        both = self.both.reshape(self.chips_z, -1, self.cols)
+        running = pick(both, (z + self.chips_z - 1) % self.chips_z, 0)
+        for s in range(2, self.chips_z + 1):
+            mine = pick(both, (z + self.chips_z - s) % self.chips_z, 0)
+            total = mine.astype(F32) + lax.ppermute(running, "z", ring).astype(F32)
+            running = total.astype(BF16)
+        return total
 
     def over_z(self):
         self.result = lax.psum_scatter(self.both, "z", scatter_dimension=0, tiled=True)
         return self.result.astype(F32)
+
+
+def pack_kernel(spot, gain1, bias1, query0, query1, out_bias, gain2, bias2, up0, up1, down_bias, packed):
+    width = packed.shape[1]
+    core = spot[0]
+    packed[...] = jnp.zeros_like(packed)
+    for n, ref in enumerate((gain1, bias1, out_bias, gain2, bias2, down_bias)):
+        packed[n : n + 1, :] = jnp.sum(ref[...], axis=0, keepdims=True)
+    units = jnp.sum(up0[...] + up1[...], axis=0, keepdims=True)
+    count = units.shape[1] // width
+    for n in range(count):
+        packed[pl.ds(8 + core * count + n, 1), :] = units[:, n * width : (n + 1) * width]
+    columns = jnp.sum(query0[...], axis=0, keepdims=True) + jnp.sum(query1[...], axis=0, keepdims=True)
+    half = width // 2
+    for n in range(2):
+        packed[6:7, n * half : (n + 1) * half] = jnp.where(core == n, columns[:, :half], 0.0)
+    packed[7:8, :HD] = jnp.where(core == 0, 0.0, columns[:, half:])
+
+
+def pack(core, *arrays):
+    width = arrays[0].shape[1]
+    units = arrays[7].shape[1] // width
+    return pl.pallas_call(
+        pack_kernel,
+        grid_spec=pltpu.PrefetchScalarGridSpec(
+            num_scalar_prefetch=1,
+            grid=(1,),
+            in_specs=[pl.BlockSpec(a.shape, lambda i, spot: (0, 0)) for a in arrays],
+            out_specs=pl.BlockSpec((8 + 2 * units, width), lambda i, spot: (0, 0)),
+        ),
+        out_shape=jax.ShapeDtypeStruct((8 + 2 * units, width), F32),
+        compiler_params=pltpu.CompilerParams(vmem_limit_bytes=32 * 2**20),
+        name="pack_small",
+    )(core.reshape(1).astype(jnp.int32), *arrays)
 
 
 def doubling(axis):
@@ -501,6 +690,34 @@
         for _, pairs in doubling(axis):
             vector = vector + lax.ppermute(vector, axis, pairs)
     return vector
+
+
+def join_kernel(cut, core, own, other, out):
+    cols = own.shape[1]
+    rest = cols - cut
+    for n in range(2):
+        for index, ref in ((n, own), (1 - n, other)):
+
+            @pl.when(core[0] == n)
+            def _(index=index, ref=ref):
+                out[:, index * cut : (index + 1) * cut] = ref[:, :cut]
+                out[:, 2 * cut + index * rest : 2 * cut + (index + 1) * rest] = ref[:, cut:]
+
+
+def join_columns(core, own, other, cut):
+    rows, cols = own.shape
+    whole = pl.BlockSpec((rows, cols), lambda i, spot: (0, 0))
+    return pl.pallas_call(
+        functools.partial(join_kernel, cut),
+        grid_spec=pltpu.PrefetchScalarGridSpec(
+            num_scalar_prefetch=1,
+            grid=(1,),
+            in_specs=[whole, whole],
+            out_specs=pl.BlockSpec((rows, 2 * cols), lambda i, spot: (0, 0)),
+        ),
+        out_shape=jax.ShapeDtypeStruct((rows, 2 * cols), F32),
+        name="join_columns",
+    )(core.reshape(1).astype(jnp.int32), own, other)
 
 
 def own_rows(core, rows):
@@ -549,13 +766,12 @@
         jnp.concatenate([bias_qv[:half_q], jnp.zeros((HD,), F32)]),
         jnp.concatenate([bias_qv[half_q:width_q], bias_qv[width_q:]]),
     )
-    qkv_block = core_rows(
+    w_out_t = w_out.T
+    near_block = core_rows(
         core,
-        jnp.concatenate([w_qkv[:, :half_q], w_qkv[:, width_q : width_q + HD]], axis=1),
-        jnp.concatenate([w_qkv[:, half_q:width_q], w_qkv[:, width_q + HD :]], axis=1),
-    )
-    w_out_t = w_out.T
-    out_block = core_rows(core, w_out_t[:, :half_q], w_out_t[:, half_q:])
+        jnp.concatenate([w_qkv[:, :half_q], w_qkv[:, width_q : width_q + HD], w_out_t[:, :half_q]], axis=1),
+        jnp.concatenate([w_qkv[:, half_q:width_q], w_qkv[:, width_q + HD :], w_out_t[:, half_q:]], axis=1),
+    )
     up_parts = w_up.reshape(w_up.shape[0], chips, 2, unit_block)
     up_block = core_rows(
         core,
@@ -564,25 +780,24 @@
     )
     spot = jnp.stack([y, x, z]).astype(jnp.int32)
     by_hand = lax.axis_size("y") == 2
+    ring = [(i, (i + 1) % chips_z) for i in range(chips_z)]
 
     def gather(block):
         return lax.all_gather(block, CHIPS, axis=0, tiled=True)
 
-    if by_hand:
-        w_qkv_all = place(gather_pieces(qkv_block, y, x, chips_z), spot)
-        w_out_all = place(gather_pieces(out_block, y, x, chips_z), spot)
-    else:
-        w_qkv_all, w_out_all = gather(qkv_block), gather(out_block)
-    w_up_all, w_down_all = gather(up_block), gather(w_down)
+    def both_cores(own):
+        return (own, swap(own, "core"))
+
+    near_all, w_up_all = gather(near_block), gather(up_block)
+    w_out_all = near_all[:, half_q + HD :]
 
     tokens = hidden_in.reshape(own_count, width).astype(F32)
     unit1, inverse1 = normalise(tokens)
-    normed1_own = (unit1 * gain1 + bias1).astype(BF16)
-    normed1 = jnp.concatenate([normed1_own, swap(normed1_own, "core")], axis=0)
-    own_kv = (plain_dot(normed1, w_qkv_all[:, half_q:]) + bias_qkv[half_q:]).astype(BF16)
-    own_kv = own_kv.reshape(2, windows, local_len, HD)
-    own_kv = jnp.swapaxes(in_order(core, own_kv[0], own_kv[1]), 0, 1).reshape(windows, chip_len, HD)
-    ring = [(i, (i + 1) % chips_z) for i in range(chips_z)]
+    normed1 = both_cores((unit1 * gain1 + bias1).astype(BF16))
+    w_query, w_kv = near_all[:, :half_q], near_all[:, half_q : half_q + HD]
+    own_kv = [(plain_dot(rows, w_kv) + bias_qkv[half_q:]).astype(BF16) for rows in normed1]
+    own_kv = [rows.reshape(windows, local_len, HD) for rows in own_kv]
+    own_kv = jnp.swapaxes(in_order(core, *own_kv), 0, 1).reshape(windows, chip_len, HD)
     keys, values = [], []
     for s in range(chips_z):
         other_kv = swap(own_kv, "core")
@@ -590,9 +805,9 @@
         values.append(jnp.where(core == 0, other_kv, own_kv))
         if s < chips_z - 1:
             own_kv = lax.ppermute(own_kv, "z", ring)
+    w_down_all = gather(w_down)
     keys, values = jnp.stack(keys), jnp.stack(values)
-    projected = (plain_dot(normed1, w_qkv_all[:, :half_q]) + bias_qkv[:half_q]).astype(BF16)
-    queries = (projected[:own_count], projected[own_count:])
+    queries = [(plain_dot(rows, w_query) + bias_qkv[:half_q]).astype(BF16) for rows in normed1]
     tq_forward, tk_forward = min(512, local_len), min(512, chip_len)
     tq, tk = min(256, local_len), min(256, chip_len)
     attended, lse = [None, None], [None, None]
@@ -600,129 +815,132 @@
         attended[n], lse[n] = attend_forward(
             queries[n], keys, values, starts[n],
             tile_numbers(starts[n], positions[n], z, tq_forward, tk_forward), tq_forward, tk_forward,
+            () if n == 1 else (attended[1],),
         )
         if n == 1:
-            out_other = swap(plain_dot(attended[1], w_out_all.T).astype(BF16), "core")
-    residual = tokens + bias_out + plain_dot(attended[0], w_out_all.T) + out_other.astype(F32)
-    attended_all = jnp.concatenate(attended, axis=0)
+            out_other = swap(matmul("nt", attended[1], w_out_all, [(BF16, "tile")], name="attention_out"), "core")
+    residual = tokens + bias_out + contract_cols(attended[0], w_out_all) + out_other.astype(F32)
 
     unit2, inverse2 = normalise(residual)
-    normed2_own = (unit2 * gain2 + bias2).astype(BF16)
-    normed2 = jnp.concatenate([normed2_own, swap(normed2_own, "core")], axis=0)
-    upward = plain_dot(normed2, w_up_all) + bias_up
-    active, slope = gelu_parts(upward)
-    active = active.astype(BF16)
+    normed2 = both_cores((unit2 * gain2 + bias2).astype(BF16))
+    active, slope = [None, None], [None, None]
+    for n in (0, 1):
+        active[n], slope[n] = matmul(
+            "nn", normed2[n], w_up_all, [(BF16, "tile"), (BF16, "tile")], gelu_finish, [(bias_up.reshape(1, -1), "row")],
+            name="upward",
+        )
     upstream = jnp.where(valid, cotangent.reshape(own_count, width), 0)
-    grad_down = jnp.concatenate([upstream, swap(upstream, "core")], axis=0)
-    grad_b_down = jnp.sum(upstream.astype(F32), axis=0)
-    down_total = contract_rows(active, grad_down).astype(BF16)
-
+    grad_down = both_cores(upstream)
+    down_total = over_tokens(active, grad_down, name="grad_w_down")
+
+    deps = ()
     if by_hand:
-        down_sum = Sum(down_total, y, x, chips_z)
-    grad_up, unit_sums = matmul(
-        "nt", grad_down, w_down_all, [(BF16, "tile"), (F32, "part")], slope_finish, [(slope, "tile")],
-        deps=down_sum.sent if by_hand else (), name="grad_up",
-    )
-    grad_b_up = jnp.sum(unit_sums, axis=(0, 1))
-    up_total = matmul("tn", normed2, grad_up, [(BF16, "tile")], name="grad_w_up")
+        down_sum = Sum(down_total, spot, chips_z)
+        deps = down_sum.sent
+    grad_up, unit_sums = [None, None], [None, None]
+    for n in (0, 1):
+        grad_up[n], unit_sums[n] = matmul(
+            "nt", grad_down[n], w_down_all, [(BF16, "tile"), (F32, "sums")], slope_finish, [(slope[n], "tile")],
+            deps=deps, name="grad_up",
+        )
+    cols = grad_up[0].shape[1] // 2
+    up_totals = [over_tokens(normed2, grad_up, b_cols=(n * cols, cols), name="grad_w_up") for n in (0, 1)]
     if by_hand:
-        down_sum.first()
-        up_sum = Sum(up_total, y, x, chips_z)
-    grad_other = matmul(
-        "nt", grad_up, w_up_all, [(BF16, "tile")], a_rows=(own_count, own_count),
-        deps=down_sum.sent + up_sum.sent if by_hand else (), name="grad_normed2",
-    )
-    grad_mixed = contract_cols(grad_up[:own_count], w_up_all) + swap(grad_other, "core").astype(F32)
-    grad_gain2 = jnp.sum(grad_mixed * unit2, axis=0)
-    grad_bias2 = jnp.sum(grad_mixed, axis=0)
-    grad_residual = upstream.astype(F32) + norm_backward(unit2, inverse2, gain2, grad_mixed)
-    branch_own = grad_residual.astype(BF16)
-    grad_b_out = jnp.sum(branch_own.astype(F32), axis=0)
-    branch = jnp.concatenate([branch_own, swap(branch_own, "core")], axis=0)
+        down_sum.first(up_totals[1])
+        up_sums = [Sum(total, spot, chips_z) for total in up_totals]
+        deps = down_sum.sent + up_sums[0].sent + up_sums[1].sent
+    mixed_other = matmul("nt", grad_up[1], w_up_all, [(BF16, "tile")], deps=deps, name="grad_normed2")
+    mixed_own = matmul("nt", grad_up[0], w_up_all, [(F32, "tile")], deps=(mixed_other,), name="grad_normed2")
+    down_other = matmul("nn", active[1], w_down_all, [(BF16, "tile")], deps=(mixed_own,), name="mixed_out")
+    deps = (down_other,)
     if by_hand:
-        down_sum.second()
+        down_sum.second(down_other)
+        up_sums[0].first(down_other)
         grad_w_down = down_sum.over_z()
-    down_other = matmul(
-        "nn", active, w_down_all, [(BF16, "tile")], a_rows=(own_count, own_count),
-        deps=(branch_own, down_sum.both) if by_hand else (branch_own,), name="mixed_out",
-    )
-    mixed_out = (
-        residual + bias_down + plain_dot(active[:own_count], w_down_all) + swap(down_other, "core").astype(F32)
-    ).astype(BF16)
+        deps += (down_sum.both,) + up_sums[0].sent
+    grad_residual, gain2_sums, bias2_sums, branch_own, out_sums = norm_backward(
+        mixed_own, swap(mixed_other, "core"), unit2, inverse2, gain2, upstream, True, deps
+    )
+    branch = both_cores(branch_own)
+
+    grad_attended = [matmul("nn", branch[n], w_out_all, [(BF16, "tile")], name="grad_attended") for n in (0, 1)]
+    out_total = over_tokens(branch, attended, deps=(grad_attended[1],), name="grad_w_out")
     if by_hand:
-        up_sum.first()
-
-    grad_attended = matmul(
-        "nn", branch, w_out_all, [(BF16, "tile")], deps=up_sum.sent if by_hand else (), name="grad_attended"
-    )
-    out_total = matmul("tn", branch, attended_all, [(BF16, "tile")], name="grad_w_out")
-    if by_hand:
-        out_sum = Sum(out_total, y, x, chips_z)
-        up_sum.second()
-        grad_w_up = up_sum.over_z()
+        out_sum = Sum(out_total, spot, chips_z)
+        up_sums[1].first(out_total)
     grad_query, grad_keys, grad_values = [None, None], [None, None], [None, None]
     for n in (0, 1):
         deps = ()
         if by_hand:
             if n == 0:
-                deps = out_sum.sent + (up_sum.both, mixed_out)
+                deps = out_sum.sent + up_sums[1].sent
             else:
-                out_sum.first()
-                deps = out_sum.sent + (grad_keys[0], down_sum.result)
+                up_sums[0].second(grad_keys[0], beside=up_sums[1:])
+                grad_w_up = up_sums[0].over_z()
+                deps = (up_sums[0].both, down_sum.result)
         grad_query[n], grad_keys[n], grad_values[n] = attend_backward(
-            queries[n], grad_attended, n * own_count, attended[n], lse[n], keys, values, starts[n],
+            queries[n], grad_attended[n], 0, attended[n], lse[n], keys, values, starts[n],
             tile_numbers(starts[n], positions[n], z, tq, tk), tq, tk, deps,
         )
+    if by_hand:
+        out_sum.first(grad_keys[1])
     grad_keys = grad_keys[0].astype(F32) + grad_keys[1].astype(F32)
     grad_values = grad_values[0].astype(F32) + grad_values[1].astype(F32)
-    arrived = swap(jnp.where(core == 0, grad_values, grad_keys).astype(BF16), "core")
-    grad_kv = (jnp.where(core == 0, grad_keys, grad_values) + arrived.astype(F32)).astype(BF16)
-    running = grad_kv[1 % chips_z]
+    kv_sent = jnp.where(core == 0, grad_values, grad_keys).astype(BF16)
+    query_total = over_tokens(
+        normed1, grad_query, deps=(kv_sent,), name="grad_w_query"
+    )
+    grad_kv = (jnp.where(core == 0, grad_keys, grad_values) + swap(kv_sent, "core").astype(F32)).astype(BF16)
+    running = hold(grad_kv[1 % chips_z], query_total, *((up_sums[0].result,) if by_hand else ()))
     for s in range(2, chips_z + 1):
         running = (grad_kv[s % chips_z].astype(F32) + lax.ppermute(running, "z", ring).astype(F32)).astype(BF16)
     grad_kv = jnp.swapaxes(running.reshape(windows, 2, local_len, HD), 0, 1)
-    grad_kv = in_order(core, grad_kv[0], grad_kv[1]).reshape(count, HD)
-    grad_qkv = jnp.concatenate([jnp.concatenate(grad_query, axis=0), grad_kv], axis=1)
-    grad_b_qkv = jnp.sum(grad_qkv.astype(F32), axis=0)
-    qkv_total = contract_rows(normed1, grad_qkv).astype(BF16)
-    grad_other = contract_cols(grad_qkv[own_count:], w_qkv_all).astype(BF16)
-    grad_normed = contract_cols(grad_qkv[:own_count], w_qkv_all) + swap(grad_other, "core").astype(F32)
-    grad_gain1 = jnp.sum(grad_normed * unit1, axis=0)
-    grad_bias1 = jnp.sum(grad_normed, axis=0)
-    grad_hidden = grad_residual + norm_backward(unit1, inverse1, gain1, grad_normed)
-
+    grad_kv = in_order(core, grad_kv[0], grad_kv[1]).reshape(2, own_count, HD)
+    kv_total = (contract_rows(normed1[0], grad_kv[0]) + contract_rows(normed1[1], grad_kv[1])).astype(BF16)
+    qkv_total = jnp.concatenate([query_total, kv_total], axis=1)
+    mixed_out = matmul(
+        "nn", active[0], w_down_all, [(BF16, "tile")], sum_finish,
+        [(residual, "tile"), (bias_down.reshape(1, -1), "row"), (swap(down_other, "core"), "tile")], deps=(query_total,), name="mixed_out",
+    )
+    grad_qkv = [jnp.concatenate([grad_query[n], grad_kv[n]], axis=1) for n in (0, 1)]
+    deps = (mixed_out,)
     if by_hand:
-        qkv_sum = Sum(qkv_total, y, x, chips_z)
-        out_sum.second()
+        out_sum.second(mixed_out)
         grad_w_out = out_sum.over_z()
-        qkv_sum.first()
+        qkv_sum = Sum(qkv_total, spot, chips_z)
+        deps += qkv_sum.sent + (out_sum.both,)
+    first_other = matmul("nt", grad_qkv[1], near_all, [(BF16, "tile")], deps=deps, name="grad_normed1")
+    first_own = matmul("nt", grad_qkv[0], near_all, [(F32, "tile")], deps=(first_other,), name="grad_normed1")
+    grad_hidden, gain1_sums, bias1_sums = norm_backward(
+        first_own, swap(first_other, "core"), unit1, inverse1, gain1, grad_residual, False
+    )
+    if by_hand:
+        qkv_sum.first(gain1_sums)
         qkv_sum.second()
-        grad_w_qkv = qkv_sum.over_z()
-    else:
+        grad_w_qkv = qkv_sum.round_z(ring)
+    qkv_sums = [jnp.sum(rows.astype(F32).reshape(-1, 8, rows.shape[1]), axis=0) for rows in grad_qkv]
+    down_sums = jnp.sum(upstream.astype(F32).reshape(-1, 8, width), axis=0)
+
+    if not by_hand:
         grad_w_down, grad_w_up, grad_w_out, grad_w_qkv = (
             lax.psum_scatter(total, CHIPS, scatter_dimension=0, tiled=True).astype(F32)
-            for total in (down_total, up_total, out_total, qkv_total)
+            for total in (down_total, jnp.concatenate(up_totals, axis=1), out_total, qkv_total)
         )
-    zero = jnp.zeros_like(grad_b_qkv[:half_q])
-    query_bias = jnp.where(
-        core == 0, jnp.concatenate([grad_b_qkv[:half_q], zero]), jnp.concatenate([zero, grad_b_qkv[:half_q]])
-    )
-    value_bias = jnp.where(core == 0, 0.0, grad_b_qkv[half_q:])
-    unit_bias = in_order(core, grad_b_up.reshape(chips, unit_block), jnp.zeros((chips, unit_block), F32))
-    unit_bias = jnp.swapaxes(unit_bias, 0, 1).reshape(-1)
     device = ((y * 2 + x) * chips_z + z) * 2 + core
-    mine = []
-    for group in ((grad_b_out, grad_gain2, grad_bias2, unit_bias, grad_b_down), (grad_gain1, grad_bias1, query_bias, value_bias)):
-        sums = sum_small(jnp.concatenate(group))
-        at = 0
-        for part in group:
-            size = part.shape[0] // (2 * chips)
-            mine.append(lax.dynamic_slice_in_dim(sums, at + device * size, size, 0))
-            at += part.shape[0]
-    own_qkv = own_rows(core, grad_w_qkv)
-    own_qkv = jnp.concatenate(
-        [own_qkv[0, :, :half_q], own_qkv[1, :, :half_q], own_qkv[0, :, half_q:], own_qkv[1, :, half_q:]], axis=1
-    )
+    share = width // (2 * chips)
+    sums = sum_small(
+        pack(
+            core, gain1_sums, bias1_sums, *qkv_sums, out_sums, gain2_sums, bias2_sums, *unit_sums, down_sums,
+        )
+    )
+    vectors = lax.dynamic_slice(sums, (0, device * share), (7, share))
+    value_bias = lax.dynamic_slice(sums, (7, device * (HD // (2 * chips))), (1, HD // (2 * chips)))[0]
+    unit_bias = lax.dynamic_slice_in_dim(
+        sums[8:].reshape(2, -1), ((y * 2 + x) * chips_z + z) * unit_block, unit_block, 1
+    )
+    unit_bias = pick(unit_bias, core, 0)
+    pair = grad_w_qkv.reshape(2, -1, half_q + HD)
+    own_qkv = join_columns(core, pick(pair, core, 0), swap(pick(pair, 1 - core, 0), "core"), half_q)
     own_out = own_rows(core, grad_w_out)
     own_out = jnp.concatenate([own_out[0], own_out[1]], axis=1).T
     own_up = own_rows(core, grad_w_up)
@@ -730,8 +948,8 @@
     return (
         mixed_out.reshape(windows, local_len, width),
         grad_hidden.reshape(windows, local_len, width),
-        mine[5], mine[6], own_qkv, mine[7], mine[8], own_out, mine[0], mine[1], mine[2],
-        own_up, mine[3], grad_w_down, mine[4],
+        vectors[0], vectors[1], own_qkv, vectors[6], value_bias, own_out, vectors[2], vectors[3], vectors[4],
+        own_up, unit_bias, grad_w_down, vectors[5],
     )
 
 

time: 1330 us -> 1250 us (0.940)
  Pallas kernels: 266 us -> 524 us
  matrix products: 229 us -> 37.2 us
  other arithmetic: 152 us -> 62 us
  starting transfers between devices: 155 us -> 70.4 us
  waiting for transfers between devices: 410 us -> 435 us
    pallas_call x8 -> x32, Pallas kernels: 194 us -> 452 us  [the longest x13 254 us: matmul(): pl.pallas_call(functools.partial(rows_kernel, kind, chunk, len(extras), l...]
    all_gather x2 -> x3, waiting for transfers between devices: 23.8 us -> 243 us  [gather(): return lax.all_gather(block, CHIPS, axis=0, tiled=True)]
    ppermute x32 -> x3, waiting for transfers between devices: 105 us -> 0.68 us  [round_z(): total = mine.astype(F32) + lax.ppermute(running, 'z', ring).astype(F32)]
    dot_general x6 -> x4, matrix products: 122 us -> 23.2 us  [plain_dot(): return jnp.dot(left_op, right_op, preferred_element_type=F32)]
    ppermute x35 -> x38, waiting for transfers between devices: 106 us -> 34 us  [swap(): return lax.ppermute(values, axis, PAIR)]
    ppermute x3, waiting for transfers between devices: 101 us -> 30.4 us  [body(): lax.ppermute(running, 'z', ring).astype(F32)]
    ppermute x32 -> x3, starting transfers between devices: 69.4 us -> 2.4 us  [round_z(): total = mine.astype(F32) + lax.ppermute(running, 'z', ring).astype(F32)]
    dot_general x2, matrix products: 56.7 us -> 4.94 us  [contract_rows(): lax.dot_general(left_op, right_op, (((0,), (0,)), ((), ())), preferred_el...]
  transfers between devices with their start and end apart: 94 -> 63, of which waited for: 42 -> 25; matrix products, arithmetic and copies ran while one was open for 33% -> 11% of each run, Pallas kernels for 20% -> 41%
where the time goes in v2:
time: 1250 us; the launch traced here: 1240 us
  Pallas kernels  524 us (42%)
  waiting for transfers between devices  435 us (35%)
  local copies, waits for them, and re-layouts  94.3 us (8%)
  starting transfers between devices  70.4 us (6%)
  other arithmetic  62 us (5%)
  matrix products  37.2 us (3%)
  between operations  19 us (2%)
    pallas_call x13, Pallas kernels, matmul(): pl.pallas_call(functools.partial(rows_kernel, kind, chunk, len(extras), l...  254 us
    all_gather x3, waiting for transfers between devices, gather(): return lax.all_gather(block, CHIPS, axis=0, tiled=True)  243 us
    pallas_call x5, Pallas kernels, over_tokens(): pl.pallas_call(functools.partial(tokens_kernel, chunk, len(deps)), grid=(...  133 us
    ppermute x3, waiting for transfers between devices, body(): own_kv = lax.ppermute(own_kv, 'z', ring)  51.5 us
    pallas_call x2, Pallas kernels, attend_backward(): pl.pallas_call(functools.partial(backward_kernel, tq, tk, heads, len(deps...  46.6 us
    reduce_scatter x3, waiting for transfers between devices, over_z(): lax.psum_scatter(self.both, 'z', scatter_dimension=0, tiled=True)  43.7 us
    unnamed x233, local copies, waits for them, and re-layouts  39.7 us
    ppermute x38, starting transfers between devices, swap(): return lax.ppermute(values, axis, PAIR)  35.9 us
  transfers between devices with their start and end apart: 63, of which 25 were waited for; matrix products, arithmetic and copies ran while one was open for 11% of the time, Pallas kernels for 41%

profile of v2, /device:TPU:0, one launch (start us, length us, event | category | flops | bytes accessed | tf_op | source)
XLA Modules:
  0.0 1241.7 jit_solution(7241954100243988633)
XLA Ops:
  51.9 80.7 %all-gather.4.cloned.1.call-done.b_ref = bf16[2048,2176]{1,0:T(8,128)(2,1)} async-done(((bf16[128,2176]{1,0:T(8,128)(2,1)}), bf16[2048,2176]{1,0:T(8,128)(2,1)}) %all-gather.4.cloned.1.call-update) | async-done | bytes 8912912 | tf_op jit(solution)/shard_map/all_gather | solution.py:786
  142.3 21.4 %collective-permute-done.8 = bf16[2,1024,128]{2,1,0:T(8,128)(2,1)S(1)} collective-permute-done((bf16[2,1024,128]{2,1,0:T(8,128)(2,1)S(1)}, bf16[2,1024,128]{2,1,0:T(8,128)(2,1)S(1)}, u32[]{:S(2)}, u32[]{:S(2)}) %collective-permute-start.8) | collective-permute-done | bytes 524320 | tf_op jit(solution)/shard_map/ppermute | solution.py:807
  171.9 16.6 %collective-permute-done.10 = bf16[2,1024,128]{2,1,0:T(8,128)(2,1)S(1)} collective-permute-done((bf16[2,1024,128]{2,1,0:T(8,128)(2,1)S(1)}, bf16[2,1024,128]{2,1,0:T(8,128)(2,1)S(1)}, u32[]{:S(2)}, u32[]{:S(2)}) %collective-permute-start.10) | collective-permute-done | bytes 524320 | tf_op jit(solution)/shard_map/ppermute | solution.py:807
  229.5 15.8 %attention_forward.2 = (bf16[1024,1024]{1,0:T(8,128)(2,1)S(1)}, f32[8,1024]{1,0:T(8,128)S(1)}) custom-call(s32[2,1,6]{2,1,0:T(1,128)S(1)} %stack.284.nums, bf16[1024,1024]{1,0:T(8,128)(2,1)S(1)} %add_convert_fusion.3.q_ref, bf16[4,2,1024,128]{3,2,1,0:T(8,128)(2,1)S(1)} %pad_maximum_fusion.3.k_ref, bf16[4,2,1024,128]{3,2,1,0:T(8,128)(2,1)S(1)} %pad_maximum_fusion.4.v_ref, ...), custom_call_target="tpu_custom_call" | custom-call | flops 8589934592 | bytes 4194304 | tf_op jit(solution)/shard_map/attention_forward/pallas_call | solution.py:93
  305.7 45.1 %all-gather.6.cloned.1.call-done.b_ref = bf16[2048,4096]{1,0:T(8,128)(2,1)} async-done(((bf16[128,4096]{1,0:T(8,128)(2,1)}), bf16[2048,4096]{1,0:T(8,128)(2,1)}) %all-gather.6.cloned.1.call-update) | async-done | bytes 16777232 | tf_op jit(solution)/shard_map/all_gather | solution.py:786
  350.9 30.2 %upward.2 = (bf16[1024,4096]{1,0:T(8,128)(2,1)}, bf16[1024,4096]{1,0:T(8,128)(2,1)}) custom-call(bf16[1024,2048]{1,0:T(8,128)(2,1)} %get-tuple-element.117.a_ref.a0_ref, bf16[2048,4096]{1,0:T(8,128)(2,1)} %all-gather.6.cloned.1.call-done.b_ref, f32[1,4096]{1,0:T(1,128)S(1)} %bitcast.262), custom_call_target="tpu_custom_call" | custom-call | flops 17179869184 | bytes 29360128 | tf_op jit(solution)/shard_map/upward/pallas_call | solution.py:313
  381.0 30.3 %upward.3 = (bf16[1024,4096]{1,0:T(8,128)(2,1)}, bf16[1024,4096]{1,0:T(8,128)(2,1)}) custom-call(bf16[1024,2048]{1,0:T(8,128)(2,1)} %collective-permute-done.16.a_ref.a1_ref, bf16[2048,4096]{1,0:T(8,128)(2,1)} %all-gather.6.cloned.1.call-done.b_ref, f32[1,4096]{1,0:T(1,128)S(1)} %bitcast.263), custom_call_target="tpu_custom_call" | custom-call | flops 17179869184 | bytes 29360128 | tf_op jit(solution)/shard_map/upward/pallas_call | solution.py:313
  411.3 46.9 %grad_w_down.1 = bf16[4096,2048]{1,0:T(8,128)(2,1)} custom-call(bf16[1024,4096]{1,0:T(8,128)(2,1)} %get-tuple-element.63.a0_ref.a_ref, bf16[1024,4096]{1,0:T(8,128)(2,1)} %get-tuple-element.64.a1_ref.a_ref, bf16[1024,2048]{1,0:T(8,128)(2,1)} %bitcast_select_fusion.b0_ref.a_ref.base_ref, bf16[1024,2048]{1,0:T(8,128)(2,1)} %collective-permute-done.17.b1_ref.a_ref), custom_call_target="tpu_custom_call" | custom-call | flops 34359738368 | bytes 58720256 | tf_op jit(solution)/shard_map/grad_w_down/pallas_call | solution.py:351
  469.8 117.6 %all-gather.8.cloned.1.call-done.b_ref = bf16[4096,2048]{1,0:T(8,128)(2,1)} async-done(((bf16[256,2048]{1,0:T(8,128)(2,1)}), bf16[4096,2048]{1,0:T(8,128)(2,1)}) %all-gather.8.cloned.1.call-update) | async-done | bytes 16777232 | tf_op jit(solution)/shard_map/all_gather | solution.py:786
  587.5 25.0 %grad_up.2 = (bf16[1024,4096]{1,0:T(8,128)(2,1)}, f32[8,4096]{1,0:T(8,128)S(1)}) custom-call(bf16[1024,2048]{1,0:T(8,128)(2,1)} %bitcast_select_fusion.b0_ref.a_ref.base_ref, bf16[4096,2048]{1,0:T(8,128)(2,1)} %all-gather.8.cloned.1.call-done.b_ref, bf16[1024,4096]{1,0:T(8,128)(2,1)} %get-tuple-element.65.refs_0_, ...), custom_call_target="tpu_custom_call" | custom-call | flops 17179869184 | bytes 29360128 | tf_op jit(solution)/shard_map/grad_up/pallas_call | solution.py:313
  612.5 24.9 %grad_up.3 = (bf16[1024,4096]{1,0:T(8,128)(2,1)}, f32[8,4096]{1,0:T(8,128)S(1)}) custom-call(bf16[1024,2048]{1,0:T(8,128)(2,1)} %collective-permute-done.17.b1_ref.a_ref, bf16[4096,2048]{1,0:T(8,128)(2,1)} %all-gather.8.cloned.1.call-done.b_ref, bf16[1024,4096]{1,0:T(8,128)(2,1)} %get-tuple-element.67.refs_0_, ...), custom_call_target="tpu_custom_call" | custom-call | flops 17179869184 | bytes 29360128 | tf_op jit(solution)/shard_map/grad_up/pallas_call | solution.py:313
  637.4 26.0 %grad_w_up.3 = bf16[2048,2048]{1,0:T(8,128)(2,1)} custom-call(bf16[1024,2048]{1,0:T(8,128)(2,1)} %get-tuple-element.117.a_ref.a0_ref, bf16[1024,2048]{1,0:T(8,128)(2,1)} %collective-permute-done.16.a_ref.a1_ref, bf16[1024,4096]{1,0:T(8,128)(2,1)} %get-tuple-element.66.b0_ref.a_ref, bf16[1024,4096]{1,0:T(8,128)(2,1)} %get-tuple-element.68.b1_ref.a_ref), custom_call_target="tpu_custom_call" | custom-call | flops 17179869184 | bytes 33554432 | tf_op jit(solution)/shard_map/grad_w_up/pallas_call | solution.py:351
  671.9 26.4 %grad_w_up.2.refs_0_ = bf16[2048,2048]{1,0:T(8,128)(2,1)} custom-call(bf16[1024,2048]{1,0:T(8,128)(2,1)} %get-tuple-element.117.a_ref.a0_ref, bf16[1024,2048]{1,0:T(8,128)(2,1)} %collective-permute-done.16.a_ref.a1_ref, bf16[1024,4096]{1,0:T(8,128)(2,1)} %get-tuple-element.66.b0_ref.a_ref, bf16[1024,4096]{1,0:T(8,128)(2,1)} %get-tuple-element.68.b1_ref.a_ref), custom_call_target="tpu_custom_call" | custom-call | flops 17179869184 | bytes 33554432 | tf_op jit(solution)/shard_map/grad_w_up/pallas_call | solution.py:351
  715.5 23.8 %grad_normed2.2.refs_0_ = bf16[1024,2048]{1,0:T(8,128)(2,1)} custom-call(bf16[1024,4096]{1,0:T(8,128)(2,1)} %get-tuple-element.68.b1_ref.a_ref, bf16[2048,4096]{1,0:T(8,128)(2,1)} %all-gather.6.cloned.1.call-done.b_ref, bf16[4,128,2048]{2,1,0:T(8,128)(2,1)} %get-tuple-element.69.refs_0_, bf16[4,128,2048]{2,1,0:T(8,128)(2,1)} %get-tuple-element.70.refs_1_, ...), custom_call_target="tpu_custom_call" | custom-call | flops 17179869184 | bytes 29360128 | tf_op jit(solution)/shard_map/grad_normed2/pallas_call | solution.py:313
  739.3 24.3 %grad_normed2.3.refs_0_.own_ref = f32[1024,2048]{1,0:T(8,128)} custom-call(bf16[1024,4096]{1,0:T(8,128)(2,1)} %get-tuple-element.66.b0_ref.a_ref, bf16[2048,4096]{1,0:T(8,128)(2,1)} %all-gather.6.cloned.1.call-done.b_ref, bf16[1024,2048]{1,0:T(8,128)(2,1)} %grad_normed2.2.refs_0_), custom_call_target="tpu_custom_call" | custom-call | flops 17179869184 | bytes 29360128 | tf_op jit(solution)/shard_map/grad_normed2/pallas_call | solution.py:313
  763.6 23.7 %mixed_out.2.refs_4_.refs_0_ = bf16[1024,2048]{1,0:T(8,128)(2,1)} custom-call(bf16[1024,4096]{1,0:T(8,128)(2,1)} %get-tuple-element.64.a1_ref.a_ref, bf16[4096,2048]{1,0:T(8,128)(2,1)} %all-gather.8.cloned.1.call-done.b_ref, f32[1024,2048]{1,0:T(8,128)} %grad_normed2.3.refs_0_.own_ref), custom_call_target="tpu_custom_call" | custom-call | flops 17179869184 | bytes 29360128 | tf_op jit(solution)/shard_map/mixed_out/pallas_call | solution.py:313
  800.0 17.1 %norm_backward.2 = (f32[1024,2048]{1,0:T(8,128)}, f32[8,2048]{1,0:T(8,128)S(1)}, f32[8,2048]{1,0:T(8,128)S(1)}, bf16[1024,2048]{1,0:T(8,128)(2,1)}, f32[8,2048]{1,0:T(8,128)S(1)}) custom-call(f32[1024,2048]{1,0:T(8,128)} %grad_normed2.3.refs_0_.own_ref, bf16[1024,2048]{1,0:T(8,128)(2,1)} %collective-permute-done.21.got_ref, ...), custom_call_target="tpu_custom_call" | custom-call | tf_op jit(solution)/shard_map/norm_backward/pallas_call | solution.py:420
  841.8 17.0 %grad_w_out.1.refs_0_ = bf16[2048,1024]{1,0:T(8,128)(2,1)} custom-call(bf16[1024,2048]{1,0:T(8,128)(2,1)} %get-tuple-element.75.a_ref.a0_ref, bf16[1024,2048]{1,0:T(8,128)(2,1)} %collective-permute-done.26.a_ref.a1_ref, bf16[1024,1024]{1,0:T(8,128)(2,1)} %copy-done.53, bf16[1024,1024]{1,0:T(8,128)(2,1)} %copy-done.49, ...), custom_call_target="tpu_custom_call" | custom-call | flops 8589934592 | bytes 20971520 | tf_op jit(solution)/shard_map/grad_w_out/pallas_call | solution.py:351
  880.6 19.5 %attention_backward.2 = (bf16[1024,1024]{1,0:T(8,128)(2,1)S(1)}, bf16[4,2,1024,128]{3,2,1,0:T(8,128)(2,1)S(1)}, bf16[4,2,1024,128]{3,2,1,0:T(8,128)(2,1)S(1)}) custom-call(s32[2,2,6]{2,1,0:T(2,128)S(1)} %stack.292.nums, bf16[1024,1024]{1,0:T(8,128)(2,1)S(1)} %copy-done.57, bf16[1024,1024]{1,0:T(8,128)(2,1)} %grad_attended.2.g_ref, ...), custom_call_target="tpu_custom_call" | custom-call | flops 17179869184 | bytes 8388608 | tf_op jit(solution)/shard_map/attention_backward/pallas_call | solution.py:215
  924.5 27.0 %attention_backward.3 = (bf16[1024,1024]{1,0:T(8,128)(2,1)S(1)}, bf16[4,2,1024,128]{3,2,1,0:T(8,128)(2,1)S(1)}, bf16[4,2,1024,128]{3,2,1,0:T(8,128)(2,1)S(1)}) custom-call(s32[2,2,6]{2,1,0:T(2,128)S(1)} %stack.293.nums, bf16[1024,1024]{1,0:T(8,128)(2,1)S(1)} %copy-done.55, bf16[1024,1024]{1,0:T(8,128)(2,1)S(1)} %copy-done.52, ...), custom_call_target="tpu_custom_call" | custom-call | flops 17179869184 | bytes 8388608 | tf_op jit(solution)/shard_map/attention_backward/pallas_call | solution.py:215
  955.0 17.0 %grad_w_query.1.refs_3_.refs_0_ = bf16[2048,1024]{1,0:T(8,128)(2,1)} custom-call(bf16[1024,2048]{1,0:T(8,128)(2,1)} %get-tuple-element.120.a0_ref, bf16[1024,2048]{1,0:T(8,128)(2,1)} %collective-permute-done.6.a1_ref, bf16[1024,1024]{1,0:T(8,128)(2,1)} %copy-done.10, bf16[1024,1024]{1,0:T(8,128)(2,1)} %copy-done.12, ...), custom_call_target="tpu_custom_call" | custom-call | flops 8589934592 | bytes 20971520 | tf_op jit(solution)/shard_map/grad_w_query/pallas_call | solution.py:351
  977.1 43.7 %reduce-scatter.6.cloned.1.call-done.refs_1_ = bf16[128,4096]{1,0:T(8,128)(2,1)} async-done(((bf16[512,4096]{1,0:T(8,128)(2,1)}), bf16[128,4096]{1,0:T(8,128)(2,1)}) %reduce-scatter.6.cloned.1.call-update) | async-done | bytes 1048592 | tf_op jit(solution)/shard_map/reduce_scatter | solution.py:634
  1027.2 24.6 %collective-permute-done.34 = bf16[2,1024,128]{2,1,0:T(8,128)(2,1)} collective-permute-done((bf16[2,1024,128]{2,1,0:T(8,128)(2,1)}, bf16[2,1024,128]{2,1,0:T(8,128)(2,1)}, u32[]{:S(2)}, u32[]{:S(2)}) %collective-permute-start.34) | collective-permute-done | bytes 524320 | tf_op jit(solution)/shard_map/ppermute | solution.py:896
  1068.6 25.8 %mixed_out.3.refs_4_.refs_0_ = bf16[1024,2048]{1,0:T(8,128)(2,1)} custom-call(bf16[1024,4096]{1,0:T(8,128)(2,1)} %get-tuple-element.63.a0_ref.a_ref, bf16[4096,2048]{1,0:T(8,128)(2,1)} %all-gather.8.cloned.1.call-done.b_ref, f32[1024,2048]{1,0:T(8,128)} %copy-done.60, f32[1,2048]{1,0:T(1,128)S(1)} %reshape_reshape.17.refs_1_, ...), custom_call_target="tpu_custom_call" | custom-call | flops 17179869184 | bytes 29360128 | tf_op jit(solution)/shard_map/mixed_out/pallas_call | solution.py:313
  (552 shorter events, 452.2 us)
Async XLA Ops:
  7.2 125.4 %all-gather.4.cloned.1.call-start = ((), (), s32[]{:S(2)}) async-start(), calls=%async_computation.3 | async-start | bytes 9469952 | tf_op jit(solution)/shard_map/all_gather | solution.py:786
  12.0 338.8 %all-gather.6.cloned.1.call-start = ((), (), s32[]{:S(2)}) async-start(), calls=%async_computation.4 | async-start | bytes 17825792 | tf_op jit(solution)/shard_map/all_gather | solution.py:786
  18.8 568.6 %all-gather.8.cloned.1.call-start = ((), (), s32[]{:S(2)}) async-start(), calls=%async_computation.5 | async-start | bytes 17825792 | tf_op jit(solution)/shard_map/all_gather | solution.py:786
  19.6 898.7 %reduce-scatter.4.cloned.1.call-start = ((), (), s32[]{:S(2)}) async-start(), calls=%async_computation.6 | async-start | bytes 5242880 | tf_op jit(solution)/shard_map/reduce_scatter | solution.py:634
  51.7 84.5 %collective-permute-start.6 = (bf16[1024,2048]{1,0:T(8,128)(2,1)}, bf16[1024,2048]{1,0:T(8,128)(2,1)}, u32[]{:S(2)}, u32[]{:S(2)}) collective-permute-start(bf16[1024,2048]{1,0:T(8,128)(2,1)} %get-tuple-element.120.a0_ref), channel_id=1, source_target_pairs={{0,1},{1,0},{2,3},{3,2},{4,5},{5,4},{6,7},{7,6},{8,9},{9,8},{10,11... | collective-permute-start | bytes 12582920 | tf_op jit(solution)/shard_map/ppermute | solution.py:435
  171.4 41.8 %collective-permute-start.7 = (bf16[2,1024,128]{2,1,0:T(8,128)(2,1)S(1)}, bf16[2,1024,128]{2,1,0:T(8,128)(2,1)S(1)}, u32[]{:S(2)}, u32[]{:S(2)}) collective-permute-start(bf16[2,1024,128]{2,1,0:T(8,128)(2,1)S(1)} %bitcast.283), channel_id=1, source_target_pairs={{0,1},{1,0},{2,3},{3,2},{4,5},{5,4},{6,7},{7,6},{8,9},{9,8},{10,11... | collective-permute-start | bytes 1572872 | tf_op jit(solution)/shard_map/ppermute | solution.py:435
  171.4 55.3 %collective-permute-start.9 = (bf16[2,1024,128]{2,1,0:T(8,128)(2,1)S(1)}, bf16[2,1024,128]{2,1,0:T(8,128)(2,1)S(1)}, u32[]{:S(2)}, u32[]{:S(2)}) collective-permute-start(bf16[2,1024,128]{2,1,0:T(8,128)(2,1)S(1)} %collective-permute-done.8), channel_id=1, source_target_pairs={{0,1},{1,0},{2,3},{3,2},{4,5},{5,4},{6,7},{7,6},{8,9},{9,8},{10,11... | collective-permute-start | bytes 1572872 | tf_op jit(solution)/shard_map/ppermute | solution.py:435
  188.5 38.2 %collective-permute-start.12 = (bf16[2,1024,128]{2,1,0:T(8,128)(2,1)S(1)}, bf16[2,1024,128]{2,1,0:T(8,128)(2,1)S(1)}, u32[]{:S(2)}, u32[]{:S(2)}) collective-permute-start(bf16[2,1024,128]{2,1,0:T(8,128)(2,1)S(1)} %collective-permute-done.10), channel_id=1, source_target_pairs={{0,2},{2,4},{4,6},{6,0},{1,3},{3,5},{5,7},{7,1},{8,10},{10,12},{12... | collective-permute-start | bytes 1572872 | tf_op jit(solution)/shard_map/ppermute | solution.py:807
  293.8 87.3 %collective-permute-start.16 = (bf16[1024,2048]{1,0:T(8,128)(2,1)}, bf16[1024,2048]{1,0:T(8,128)(2,1)}, u32[]{:S(2)}, u32[]{:S(2)}) collective-permute-start(bf16[1024,2048]{1,0:T(8,128)(2,1)} %get-tuple-element.117.a_ref.a0_ref), channel_id=1, source_target_pairs={{0,1},{1,0},{2,3},{3,2},{4,5},{5,4},{6,7},{7,6},{8,9},{9,8},{10,11... | collective-permute-start | bytes 12582920 | tf_op jit(solution)/shard_map/ppermute | solution.py:435
  305.5 105.8 %collective-permute-start.17 = (bf16[1024,2048]{1,0:T(8,128)(2,1)}, bf16[1024,2048]{1,0:T(8,128)(2,1)}, u32[]{:S(2)}, u32[]{:S(2)}) collective-permute-start(bf16[1024,2048]{1,0:T(8,128)(2,1)} %bitcast_select_fusion.b0_ref.a_ref.base_ref), channel_id=1, source_target_pairs={{0,1},{1,0},{2,3},{3,2},{4,5},{5,4},{6,7},{7,6},{8,9},{9,8},{10,11... | collective-permute-start | bytes 12582920 | tf_op jit(solution)/shard_map/ppermute | solution.py:435
  463.0 241.7 %collective-permute-start.18 = (bf16[2,4,128,2048]{3,2,1,0:T(8,128)(2,1)}, bf16[2,4,128,2048]{3,2,1,0:T(8,128)(2,1)}, u32[]{:S(2)}, u32[]{:S(2)}) collective-permute-start(bf16[2,4,128,2048]{3,2,1,0:T(8,128)(2,1)} %dynamic-slice_bitcast_fusion.1.refs_1_), channel_id=1, source_target_pairs={{0,16},{16,0},{1,17},{17,1},{2,18},{18,2},{3,19},{19,3},{4,20},{20... | collective-permute-start | bytes 12582920 | tf_op jit(solution)/shard_map/ppermute | solution.py:435
  469.3 235.4 %collective-permute-start.19 = (bf16[2,4,128,2048]{3,2,1,0:T(8,128)(2,1)}, bf16[2,4,128,2048]{3,2,1,0:T(8,128)(2,1)}, u32[]{:S(2)}, u32[]{:S(2)}) collective-permute-start(bf16[2,4,128,2048]{3,2,1,0:T(8,128)(2,1)} %dynamic-slice_bitcast_fusion.refs_2_), channel_id=1, source_target_pairs={{0,8},{8,0},{1,9},{9,1},{2,10},{10,2},{3,11},{11,3},{4,12},{12,4},... | collective-permute-start | bytes 12582920 | tf_op jit(solution)/shard_map/ppermute | solution.py:435
  666.6 124.4 %collective-permute-start.24 = (bf16[2,4,64,2048]{3,2,1,0:T(8,128)(2,1)}, bf16[2,4,64,2048]{3,2,1,0:T(8,128)(2,1)S(1)}, u32[]{:S(2)}, u32[]{:S(2)}) collective-permute-start(bf16[2,4,64,2048]{3,2,1,0:T(8,128)(2,1)} %dynamic-slice_bitcast_fusion.5.refs_2_), channel_id=1, source_target_pairs={{0,16},{16,0},{1,17},{17,1},{2,18},{18,2},{3,19},{19,3},{4,20},{20... | collective-permute-start | bytes 6291464 | tf_op jit(solution)/shard_map/ppermute | solution.py:435
  669.8 121.2 %collective-permute-start.25 = (bf16[2,4,64,2048]{3,2,1,0:T(8,128)(2,1)}, bf16[2,4,64,2048]{3,2,1,0:T(8,128)(2,1)}, u32[]{:S(2)}, u32[]{:S(2)}) collective-permute-start(bf16[2,4,64,2048]{3,2,1,0:T(8,128)(2,1)} %dynamic-slice_bitcast_fusion.4.refs_3_), channel_id=1, source_target_pairs={{0,8},{8,0},{1,9},{9,1},{2,10},{10,2},{3,11},{11,3},{4,12},{12,4},... | collective-permute-start | bytes 6291464 | tf_op jit(solution)/shard_map/ppermute | solution.py:435
  713.5 73.7 %collective-permute-start.22 = (bf16[4,128,2048]{2,1,0:T(8,128)(2,1)}, bf16[4,128,2048]{2,1,0:T(8,128)(2,1)S(1)}, u32[]{:S(2)}, u32[]{:S(2)}) collective-permute-start(bf16[4,128,2048]{2,1,0:T(8,128)(2,1)} %get-tuple-element.69.refs_0_), channel_id=1, source_target_pairs={{0,8},{8,0},{1,9},{9,1},{2,10},{10,2},{3,11},{11,3},{4,12},{12,4},... | collective-permute-start | bytes 6291464 | tf_op jit(solution)/shard_map/ppermute | solution.py:435
  713.5 73.7 %collective-permute-start.23 = (bf16[4,128,2048]{2,1,0:T(8,128)(2,1)}, bf16[4,128,2048]{2,1,0:T(8,128)(2,1)S(1)}, u32[]{:S(2)}, u32[]{:S(2)}) collective-permute-start(bf16[4,128,2048]{2,1,0:T(8,128)(2,1)} %get-tuple-element.70.refs_1_), channel_id=1, source_target_pairs={{0,16},{16,0},{1,17},{17,1},{2,18},{18,2},{3,19},{19,3},{4,20},{20... | collective-permute-start | bytes 6291464 | tf_op jit(solution)/shard_map/ppermute | solution.py:435
  739.3 60.5 %collective-permute-start.21 = (bf16[1024,2048]{1,0:T(8,128)(2,1)}, bf16[1024,2048]{1,0:T(8,128)(2,1)}, u32[]{:S(2)}, u32[]{:S(2)}) collective-permute-start(bf16[1024,2048]{1,0:T(8,128)(2,1)} %grad_normed2.2.refs_0_), channel_id=1, source_target_pairs={{0,1},{1,0},{2,3},{3,2},{4,5},{5,4},{6,7},{7,6},{8,9},{9,8},{10,11... | collective-permute-start | bytes 12582920 | tf_op jit(solution)/shard_map/ppermute | solution.py:435
  790.3 230.5 %reduce-scatter.6.cloned.1.call-start = ((), (), s32[]{:S(2)}) async-start(), calls=%async_computation.7 | async-start | bytes 5242880 | tf_op jit(solution)/shard_map/reduce_scatter | solution.py:634
  819.8 48.8 %collective-permute-start.27 = (bf16[2,4,64,2048]{3,2,1,0:T(8,128)(2,1)}, bf16[2,4,64,2048]{3,2,1,0:T(8,128)(2,1)S(1)}, u32[]{:S(2)}, u32[]{:S(2)}) collective-permute-start(bf16[2,4,64,2048]{3,2,1,0:T(8,128)(2,1)} %dynamic-slice_bitcast_fusion.3.refs_4_), channel_id=1, source_target_pairs={{0,16},{16,0},{1,17},{17,1},{2,18},{18,2},{3,19},{19,3},{4,20},{20... | collective-permute-start | bytes 6291464 | tf_op jit(solution)/shard_map/ppermute | solution.py:435
  820.1 48.8 %collective-permute-start.28 = (bf16[2,4,64,2048]{3,2,1,0:T(8,128)(2,1)}, bf16[2,4,64,2048]{3,2,1,0:T(8,128)(2,1)}, u32[]{:S(2)}, u32[]{:S(2)}) collective-permute-start(bf16[2,4,64,2048]{3,2,1,0:T(8,128)(2,1)} %dynamic-slice_bitcast_fusion.2.refs_5_), channel_id=1, source_target_pairs={{0,8},{8,0},{1,9},{9,1},{2,10},{10,2},{3,11},{11,3},{4,12},{12,4},... | collective-permute-start | bytes 6291464 | tf_op jit(solution)/shard_map/ppermute | solution.py:435
  822.5 78.9 %collective-permute-start.29 = (bf16[4,64,2048]{2,1,0:T(8,128)(2,1)}, bf16[4,64,2048]{2,1,0:T(8,128)(2,1)}, u32[]{:S(2)}, u32[]{:S(2)}) collective-permute-start(bf16[4,64,2048]{2,1,0:T(8,128)(2,1)} %copy-done.32), channel_id=1, source_target_pairs={{0,8},{8,0},{1,9},{9,1},{2,10},{10,2},{3,11},{11,3},{4,12},{12,4},... | collective-permute-start | bytes 3145736 | tf_op jit(solution)/shard_map/ppermute | solution.py:435
  822.6 78.8 %collective-permute-start.30 = (bf16[4,64,2048]{2,1,0:T(8,128)(2,1)}, bf16[4,64,2048]{2,1,0:T(8,128)(2,1)}, u32[]{:S(2)}, u32[]{:S(2)}) collective-permute-start(bf16[4,64,2048]{2,1,0:T(8,128)(2,1)} %copy-done.31), channel_id=1, source_target_pairs={{0,16},{16,0},{1,17},{17,1},{2,18},{18,2},{3,19},{19,3},{4,20},{20... | collective-permute-start | bytes 3145736 | tf_op jit(solution)/shard_map/ppermute | solution.py:435
  917.8 249.6 %reduce-scatter.8.cloned.1.call-start = ((), (), s32[]{:S(2)}) async-start(), calls=%async_computation.8 | async-start | bytes 1310720 | tf_op jit(solution)/shard_map/reduce_scatter | solution.py:634
  954.5 114.1 %collective-permute-start.20 = (bf16[1024,2048]{1,0:T(8,128)(2,1)}, bf16[1024,2048]{1,0:T(8,128)(2,1)}, u32[]{:S(2)}, u32[]{:S(2)}) collective-permute-start(bf16[1024,2048]{1,0:T(8,128)(2,1)} %mixed_out.2.refs_4_.refs_0_), channel_id=1, source_target_pairs={{0,1},{1,0},{2,3},{3,2},{4,5},{5,4},{6,7},{7,6},{8,9},{9,8},{10,11... | collective-permute-start | bytes 12582920 | tf_op jit(solution)/shard_map/ppermute | solution.py:435
  (153 other events, 2558.6 us)
Sparse Core Ops, SparseCore 0:
  12.1 120.4 all-gather.3
  135.4 215.4 all-gather.5
  353.6 233.8 all-gather.7
  790.4 75.1 reduce-scatter.3
  917.9 102.8 reduce-scatter.5
  1121.4 29.8 reduce-scatter.7

commit v3 on v2

--- a/solution.py
+++ b/solution.py
@@ -267,8 +267,12 @@
 
 
 def sum_finish(part, total, extras, outs):
-    total = total + extras[0][part, :] + extras[1][...] + extras[2][part, :].astype(F32)
+    total = total + extras[0][part, :] + extras[1][...] + extras[2][part, :].astype(F32) + extras[3][part, :]
     outs[0][part, :] = total.astype(BF16)
+
+
+def add_finish(part, total, extras, outs):
+    outs[0][part, :] = (total + extras[0][part, :]).astype(outs[0].dtype)
 
 
 def slope_finish(part, total, extras, outs):
@@ -299,25 +303,24 @@
         finish(part, dot(a_ref[part, :], b_ref[...]), extras, outs)
 
 
-def matmul(kind, a, b, outs, finish=store, extras=(), tn=512, chunk=256, deps=(), name="matmul"):
-    m, k = a.shape
+def matmul(
+    kind, a, b, outs, finish=store, extras=(), tn=512, chunk=256, deps=(), depth=None, a_part=0, b_part=0, extra_part=0, name="matmul"
+):
+    m, k = a.shape[0], depth or a.shape[1]
     n = b.shape[0] if kind == "nt" else b.shape[1]
     tn, chunk = min(tn, n), min(chunk, m)
-    tile = pl.BlockSpec((m, tn), lambda j: (0, j))
-    spec = {
-        "tile": tile,
-        "row": pl.BlockSpec((1, tn), lambda j: (0, j)),
-        "sums": pl.BlockSpec((8, tn), lambda j: (0, j)),
-    }
+    skip = extra_part * (n // tn)
+    given = {"tile": pl.BlockSpec((m, tn), lambda j: (0, j + skip)), "row": pl.BlockSpec((1, tn), lambda j: (0, j + skip))}
+    spec = {"tile": pl.BlockSpec((m, tn), lambda j: (0, j)), "sums": pl.BlockSpec((8, tn), lambda j: (0, j))}
     shape = {"tile": (m, n), "sums": (8, n)}
     res = pl.pallas_call(
         functools.partial(rows_kernel, kind, chunk, len(extras), len(deps), finish),
         grid=(n // tn,),
         in_specs=[
-            pl.BlockSpec((m, k), lambda j: (0, 0)),
-            pl.BlockSpec((tn, k), lambda j: (j, 0)) if kind == "nt" else pl.BlockSpec((k, tn), lambda j: (0, j)),
+            pl.BlockSpec((m, k), lambda j: (0, a_part)),
+            pl.BlockSpec((tn, k), lambda j: (j, b_part)) if kind == "nt" else pl.BlockSpec((k, tn), lambda j: (0, j)),
         ]
-        + [spec[kind_of] for _, kind_of in extras]
+        + [given[kind_of] for _, kind_of in extras]
         + [pl.BlockSpec(memory_space=pl.ANY)] * len(deps),
         out_specs=[spec[w] for _, w in outs],
         out_shape=[jax.ShapeDtypeStruct(shape[w], d) for d, w in outs],
@@ -341,13 +344,14 @@
         out[part, :] = (plain_dot(left[0, part, :], b0_ref[...]) + plain_dot(left[1, part, :], b1_ref[...])).astype(BF16)
 
 
-def over_tokens(a, b, tm=2048, tn=512, chunk=256, deps=(), b_cols=None, name="weight_gradient"):
-    k, m = a[0].shape
-    first, n = b_cols or (0, b[0].shape[1])
+def over_tokens(a, b, tm=2048, tn=512, chunk=256, deps=(), a_cols=None, name="weight_gradient"):
+    k = a[0].shape[0]
+    first, m = a_cols or (0, a[0].shape[1])
+    n = b[0].shape[1]
     tm, tn, chunk = min(tm, m), min(tn, n), min(chunk, m)
-    skip = first // tn
-    a_spec = pl.BlockSpec((k, tm), lambda i, j: (0, i))
-    b_spec = pl.BlockSpec((k, tn), lambda i, j: (0, j + skip))
+    skip = first // tm
+    a_spec = pl.BlockSpec((k, tm), lambda i, j: (0, i + skip))
+    b_spec = pl.BlockSpec((k, tn), lambda i, j: (0, j))
     return pl.pallas_call(
         functools.partial(tokens_kernel, chunk, len(deps)),
         grid=(m // tm, n // tn),
@@ -635,16 +639,17 @@
         return self.result.astype(F32)
 
 
-def pack_kernel(spot, gain1, bias1, query0, query1, out_bias, gain2, bias2, up0, up1, down_bias, packed):
+def pack_kernel(spot, gain1, bias1, query0, query1, out_bias, gain2, bias2, down_bias, *refs):
+    *units, packed = refs
     width = packed.shape[1]
     core = spot[0]
     packed[...] = jnp.zeros_like(packed)
     for n, ref in enumerate((gain1, bias1, out_bias, gain2, bias2, down_bias)):
         packed[n : n + 1, :] = jnp.sum(ref[...], axis=0, keepdims=True)
-    units = jnp.sum(up0[...] + up1[...], axis=0, keepdims=True)
-    count = units.shape[1] // width
+    count = len(units) // 2
     for n in range(count):
-        packed[pl.ds(8 + core * count + n, 1), :] = units[:, n * width : (n + 1) * width]
+        total = units[2 * n][...] + units[2 * n + 1][...]
+        packed[pl.ds(8 + core * count + n, 1), : total.shape[1]] = jnp.sum(total, axis=0, keepdims=True)
     columns = jnp.sum(query0[...], axis=0, keepdims=True) + jnp.sum(query1[...], axis=0, keepdims=True)
     half = width // 2
     for n in range(2):
@@ -654,7 +659,7 @@
 
 def pack(core, *arrays):
     width = arrays[0].shape[1]
-    units = arrays[7].shape[1] // width
+    units = (len(arrays) - 8) // 2
     return pl.pallas_call(
         pack_kernel,
         grid_spec=pltpu.PrefetchScalarGridSpec(
@@ -760,7 +765,7 @@
         full.append(packed[:, at : at + size].reshape(-1))
         at += size
     gain1, bias1, bias_qv, bias_out, gain2, bias2, bias_up, bias_down = full
-    bias_up = pick(bias_up.reshape(chips, 2, unit_block), core, 1).reshape(-1)
+    bias_up = jnp.swapaxes(pick(bias_up.reshape(chips, 2, 2, unit_block // 2), core, 1), 0, 1).reshape(-1)
     bias_qkv = jnp.where(
         core == 0,
         jnp.concatenate([bias_qv[:half_q], jnp.zeros((HD,), F32)]),
@@ -772,11 +777,11 @@
         jnp.concatenate([w_qkv[:, :half_q], w_qkv[:, width_q : width_q + HD], w_out_t[:, :half_q]], axis=1),
         jnp.concatenate([w_qkv[:, half_q:width_q], w_qkv[:, width_q + HD :], w_out_t[:, half_q:]], axis=1),
     )
-    up_parts = w_up.reshape(w_up.shape[0], chips, 2, unit_block)
+    up_parts = jnp.moveaxis(w_up.reshape(w_up.shape[0], chips, 2, 2, unit_block // 2), 3, 1)
     up_block = core_rows(
         core,
-        up_parts[:, :, 0].reshape(w_up.shape[0], -1),
-        up_parts[:, :, 1].reshape(w_up.shape[0], -1),
+        up_parts[:, :, :, 0].reshape(w_up.shape[0], -1),
+        up_parts[:, :, :, 1].reshape(w_up.shape[0], -1),
     )
     spot = jnp.stack([y, x, z]).astype(jnp.int32)
     by_hand = lax.axis_size("y") == 2
@@ -805,7 +810,8 @@
         values.append(jnp.where(core == 0, other_kv, own_kv))
         if s < chips_z - 1:
             own_kv = lax.ppermute(own_kv, "z", ring)
-    w_down_all = gather(w_down)
+    down_rows = w_down.shape[0] // 2
+    w_down_parts = [gather(w_down[:down_rows]), gather(w_down[down_rows:])]
     keys, values = jnp.stack(keys), jnp.stack(values)
     queries = [(plain_dot(rows, w_query) + bias_qkv[:half_q]).astype(BF16) for rows in normed1]
     tq_forward, tk_forward = min(512, local_len), min(512, chip_len)
@@ -831,33 +837,49 @@
         )
     upstream = jnp.where(valid, cotangent.reshape(own_count, width), 0)
     grad_down = both_cores(upstream)
-    down_total = over_tokens(active, grad_down, name="grad_w_down")
-
-    deps = ()
-    if by_hand:
-        down_sum = Sum(down_total, spot, chips_z)
-        deps = down_sum.sent
-    grad_up, unit_sums = [None, None], [None, None]
-    for n in (0, 1):
-        grad_up[n], unit_sums[n] = matmul(
-            "nt", grad_down[n], w_down_all, [(BF16, "tile"), (F32, "sums")], slope_finish, [(slope[n], "tile")],
-            deps=deps, name="grad_up",
-        )
-    cols = grad_up[0].shape[1] // 2
-    up_totals = [over_tokens(normed2, grad_up, b_cols=(n * cols, cols), name="grad_w_up") for n in (0, 1)]
-    if by_hand:
-        down_sum.first(up_totals[1])
-        up_sums = [Sum(total, spot, chips_z) for total in up_totals]
-        deps = down_sum.sent + up_sums[0].sent + up_sums[1].sent
-    mixed_other = matmul("nt", grad_up[1], w_up_all, [(BF16, "tile")], deps=deps, name="grad_normed2")
-    mixed_own = matmul("nt", grad_up[0], w_up_all, [(F32, "tile")], deps=(mixed_other,), name="grad_normed2")
-    down_other = matmul("nn", active[1], w_down_all, [(BF16, "tile")], deps=(mixed_own,), name="mixed_out")
-    deps = (down_other,)
-    if by_hand:
-        down_sum.second(down_other)
-        up_sums[0].first(down_other)
-        grad_w_down = down_sum.over_z()
-        deps += (down_sum.both,) + up_sums[0].sent
+    units = active[0].shape[1] // 2
+    down_totals = [over_tokens(active, grad_down, a_cols=(n * units, units), name="grad_w_down") for n in (0, 1)]
+    down_sums = [Sum(total, spot, chips_z) for total in down_totals] if by_hand else ()
+
+    grad_up, unit_sums, up_totals, up_sums = [None, None], [], [], []
+    grad_normed, down_out = [None, None], [None, None]
+    deps = tuple(array for one in down_sums for array in one.sent)
+    for part in (0, 1):
+        for n in (0, 1):
+            grad_up[n], sums = matmul(
+                "nt", grad_down[n], w_down_parts[part], [(BF16, "tile"), (F32, "sums")], slope_finish, [(slope[n], "tile")],
+                extra_part=part, deps=deps, name="grad_up",
+            )
+            unit_sums.append(sums)
+        up_totals.append(over_tokens(normed2, grad_up, name="grad_w_up"))
+        deps = (up_totals[-1],)
+        if by_hand:
+            up_sums.append(Sum(up_totals[-1], spot, chips_z))
+            deps += up_sums[-1].sent
+            if part == 1:
+                down_sums[0].second(up_totals[1], beside=down_sums[1:])
+                grad_w_down = down_sums[0].over_z()
+                up_sums[0].first(up_totals[1])
+                deps += (down_sums[0].both,) + up_sums[0].sent
+        for n in (1, 0):
+            grad_normed[n] = matmul(
+                "nt", grad_up[n], w_up_all, [(F32 if n == 0 or part == 0 else BF16, "tile")],
+                add_finish if part else store, [(grad_normed[n], "tile")] if part else (), depth=units, b_part=part,
+                deps=deps, name="grad_normed2",
+            )
+            deps = (grad_normed[n],)
+        for n in (1, 0)[: 2 - part]:
+            down_out[n] = matmul(
+                "nn", active[n], w_down_parts[part], [(BF16 if part else F32, "tile")], add_finish if part else store,
+                [(down_out[n], "tile")] if part else (), depth=units, a_part=part, deps=deps, name="mixed_out",
+            )
+            deps = (down_out[n],)
+        if by_hand and part == 0:
+            for one in down_sums:
+                one.first(down_out[0])
+            deps += tuple(array for one in down_sums for array in one.sent)
+    mixed_other, mixed_own = grad_normed[1], grad_normed[0]
+    down_other = down_out[1]
     grad_residual, gain2_sums, bias2_sums, branch_own, out_sums = norm_backward(
         mixed_own, swap(mixed_other, "core"), unit2, inverse2, gain2, upstream, True, deps
     )
@@ -877,7 +899,7 @@
             else:
                 up_sums[0].second(grad_keys[0], beside=up_sums[1:])
                 grad_w_up = up_sums[0].over_z()
-                deps = (up_sums[0].both, down_sum.result)
+                deps = (up_sums[0].both, down_sums[0].result)
         grad_query[n], grad_keys[n], grad_values[n] = attend_backward(
             queries[n], grad_attended[n], 0, attended[n], lse[n], keys, values, starts[n],
             tile_numbers(starts[n], positions[n], z, tq, tk), tq, tk, deps,
@@ -899,8 +921,9 @@
     kv_total = (contract_rows(normed1[0], grad_kv[0]) + contract_rows(normed1[1], grad_kv[1])).astype(BF16)
     qkv_total = jnp.concatenate([query_total, kv_total], axis=1)
     mixed_out = matmul(
-        "nn", active[0], w_down_all, [(BF16, "tile")], sum_finish,
-        [(residual, "tile"), (bias_down.reshape(1, -1), "row"), (swap(down_other, "core"), "tile")], deps=(query_total,), name="mixed_out",
+        "nn", active[0], w_down_parts[1], [(BF16, "tile")], sum_finish,
+        [(residual, "tile"), (bias_down.reshape(1, -1), "row"), (swap(down_other, "core"), "tile"), (down_out[0], "tile")],
+        depth=units, a_part=1, deps=(query_total,), name="mixed_out",
     )
     grad_qkv = [jnp.concatenate([grad_query[n], grad_kv[n]], axis=1) for n in (0, 1)]
     deps = (mixed_out,)
@@ -919,32 +942,34 @@
         qkv_sum.second()
         grad_w_qkv = qkv_sum.round_z(ring)
     qkv_sums = [jnp.sum(rows.astype(F32).reshape(-1, 8, rows.shape[1]), axis=0) for rows in grad_qkv]
-    down_sums = jnp.sum(upstream.astype(F32).reshape(-1, 8, width), axis=0)
+    upstream_sums = jnp.sum(upstream.astype(F32).reshape(-1, 8, width), axis=0)
 
     if not by_hand:
         grad_w_down, grad_w_up, grad_w_out, grad_w_qkv = (
             lax.psum_scatter(total, CHIPS, scatter_dimension=0, tiled=True).astype(F32)
-            for total in (down_total, jnp.concatenate(up_totals, axis=1), out_total, qkv_total)
+            for total in (jnp.concatenate(down_totals, axis=1), jnp.concatenate(up_totals, axis=1), out_total, qkv_total)
         )
     device = ((y * 2 + x) * chips_z + z) * 2 + core
     share = width // (2 * chips)
     sums = sum_small(
         pack(
-            core, gain1_sums, bias1_sums, *qkv_sums, out_sums, gain2_sums, bias2_sums, *unit_sums, down_sums,
+            core, gain1_sums, bias1_sums, *qkv_sums, out_sums, gain2_sums, bias2_sums, upstream_sums, *unit_sums,
         )
     )
     vectors = lax.dynamic_slice(sums, (0, device * share), (7, share))
     value_bias = lax.dynamic_slice(sums, (7, device * (HD // (2 * chips))), (1, HD // (2 * chips)))[0]
-    unit_bias = lax.dynamic_slice_in_dim(
-        sums[8:].reshape(2, -1), ((y * 2 + x) * chips_z + z) * unit_block, unit_block, 1
-    )
-    unit_bias = pick(unit_bias, core, 0)
+    half_block = unit_block // 2
+    unit_bias = lax.dynamic_slice(
+        sums, (8 + 2 * core, ((y * 2 + x) * chips_z + z) * half_block), (2, half_block)
+    ).reshape(-1)
+    grad_w_down = jnp.concatenate([grad_w_down[:, :width], grad_w_down[:, width:]], axis=0)
     pair = grad_w_qkv.reshape(2, -1, half_q + HD)
     own_qkv = join_columns(core, pick(pair, core, 0), swap(pick(pair, 1 - core, 0), "core"), half_q)
     own_out = own_rows(core, grad_w_out)
     own_out = jnp.concatenate([own_out[0], own_out[1]], axis=1).T
     own_up = own_rows(core, grad_w_up)
-    own_up = jnp.moveaxis(own_up.reshape(2, own_up.shape[1], chips, unit_block), 0, 2).reshape(own_up.shape[1], -1)
+    own_up = own_up.reshape(2, own_up.shape[1], 2, chips, half_block)
+    own_up = jnp.transpose(own_up, (1, 3, 0, 2, 4)).reshape(own_up.shape[1], -1)
     return (
         mixed_out.reshape(windows, local_len, width),
         grad_hidden.reshape(windows, local_len, width),

time: 1250 us -> 1190 us (0.952)
  waiting for transfers between devices: 435 us -> 338 us
  Pallas kernels: 524 us -> 569 us
    all_gather x3 -> x4, waiting for transfers between devices: 243 us -> 139 us  [gather(): return lax.all_gather(block, CHIPS, axis=0, tiled=True)]
    pallas_call x13 -> x19, Pallas kernels: 254 us -> 282 us  [matmul(): pl.pallas_call(functools.partial(rows_kernel, kind, chunk, len(extras), l...]
    unnamed x233 -> x278, local copies, waits for them, and re-layouts: 39.7 us -> 48.4 us
    pallas_call x5 -> x6, Pallas kernels: 133 us -> 140 us  [over_tokens(): pl.pallas_call(functools.partial(tokens_kernel, chunk, len(deps)), grid=(...]
    ppermute x38 -> x42, waiting for transfers between devices: 34 us -> 36 us  [swap(): return lax.ppermute(values, axis, PAIR)]
    ppermute x38 -> x42, starting transfers between devices: 35.9 us -> 37.6 us  [swap(): return lax.ppermute(values, axis, PAIR)]
    reshape x10 -> x12, local copies, waits for them, and re-layouts: 25.8 us -> 25.7 us  [cut(): lax.dynamic_slice(self.total, at, size)]
  transfers between devices with their start and end apart: 63 -> 68, of which waited for: 25 -> 27; matrix products, arithmetic and copies ran while one was open for 11% -> 11% of each run, Pallas kernels for 41% -> 46%
where the time goes in v3:
time: 1190 us; the launch traced here: 1180 us
  Pallas kernels  569 us (48%)
  waiting for transfers between devices  338 us (28%)
  local copies, waits for them, and re-layouts  98.7 us (8%)
  starting transfers between devices  60.7 us (5%)
  other arithmetic  52.8 us (4%)
  matrix products  38 us (3%)
  between operations  19.5 us (2%)
    pallas_call x19, Pallas kernels, matmul(): pl.pallas_call(functools.partial(rows_kernel, kind, chunk, len(extras), l...  282 us
    pallas_call x6, Pallas kernels, over_tokens(): pl.pallas_call(functools.partial(tokens_kernel, chunk, len(deps)), grid=(...  140 us
    all_gather x4, waiting for transfers between devices, gather(): return lax.all_gather(block, CHIPS, axis=0, tiled=True)  139 us
    ppermute x3, waiting for transfers between devices, body(): own_kv = lax.ppermute(own_kv, 'z', ring)  49 us
    unnamed x278, local copies, waits for them, and re-layouts  48.4 us
    pallas_call x2, Pallas kernels, attend_backward(): pl.pallas_call(functools.partial(backward_kernel, tq, tk, heads, len(deps...  46.9 us
    reduce_scatter x3, waiting for transfers between devices, over_z(): lax.psum_scatter(self.both, 'z', scatter_dimension=0, tiled=True)  44.3 us
    ppermute x42, starting transfers between devices, swap(): return lax.ppermute(values, axis, PAIR)  37.6 us
  transfers between devices with their start and end apart: 68, of which 27 were waited for; matrix products, arithmetic and copies ran while one was open for 11% of the time, Pallas kernels for 46%

profile of v3, /device:TPU:0, one launch (start us, length us, event | category | flops | bytes accessed | tf_op | source)
XLA Modules:
  0.0 1176.1 jit_solution(17214851959289342170)
XLA Ops:
  51.0 81.4 %all-gather.5.cloned.1.call-done.b_ref = bf16[2048,2176]{1,0:T(8,128)(2,1)} async-done(((bf16[128,2176]{1,0:T(8,128)(2,1)}), bf16[2048,2176]{1,0:T(8,128)(2,1)}) %all-gather.5.cloned.1.call-update) | async-done | bytes 8912912 | tf_op jit(solution)/shard_map/all_gather | solution.py:791
  142.2 21.4 %collective-permute-done.8 = bf16[2,1024,128]{2,1,0:T(8,128)(2,1)S(1)} collective-permute-done((bf16[2,1024,128]{2,1,0:T(8,128)(2,1)S(1)}, bf16[2,1024,128]{2,1,0:T(8,128)(2,1)S(1)}, u32[]{:S(2)}, u32[]{:S(2)}) %collective-permute-start.8) | collective-permute-done | bytes 524320 | tf_op jit(solution)/shard_map/ppermute | solution.py:812
  171.7 16.6 %collective-permute-done.10 = bf16[2,1024,128]{2,1,0:T(8,128)(2,1)S(1)} collective-permute-done((bf16[2,1024,128]{2,1,0:T(8,128)(2,1)S(1)}, bf16[2,1024,128]{2,1,0:T(8,128)(2,1)S(1)}, u32[]{:S(2)}, u32[]{:S(2)}) %collective-permute-start.10) | collective-permute-done | bytes 524320 | tf_op jit(solution)/shard_map/ppermute | solution.py:812
  216.8 15.5 %attention_forward.2 = (bf16[1024,1024]{1,0:T(8,128)(2,1)S(1)}, f32[8,1024]{1,0:T(8,128)S(1)}) custom-call(s32[2,1,6]{2,1,0:T(1,128)S(1)} %stack.284.nums, bf16[1024,1024]{1,0:T(8,128)(2,1)S(1)} %add_convert_fusion.3.q_ref, bf16[4,2,1024,128]{3,2,1,0:T(8,128)(2,1)S(1)} %pad_maximum_fusion.3.k_ref, bf16[4,2,1024,128]{3,2,1,0:T(8,128)(2,1)S(1)} %pad_maximum_fusion.4.v_ref, ...), custom_call_target="tpu_custom_call" | custom-call | flops 8589934592 | bytes 4194304 | tf_op jit(solution)/shard_map/attention_forward/pallas_call | solution.py:93
  252.8 18.0 %attention_forward.3 = (bf16[1024,1024]{1,0:T(8,128)(2,1)S(1)}, f32[8,1024]{1,0:T(8,128)S(1)}) custom-call(s32[2,1,6]{2,1,0:T(1,128)S(1)} %stack.268.nums, bf16[1024,1024]{1,0:T(8,128)(2,1)S(1)} %add_convert_fusion.4.q_ref, bf16[4,2,1024,128]{3,2,1,0:T(8,128)(2,1)S(1)} %copy-done.30, bf16[4,2,1024,128]{3,2,1,0:T(8,128)(2,1)S(1)} %pad_maximum_fusion.4.v_ref, ...), custom_call_target="tpu_custom_call" | custom-call | flops 8589934592 | bytes 4194304 | tf_op jit(solution)/shard_map/attention_forward/pallas_call | solution.py:93
  300.4 47.3 %all-gather.7.cloned.1.call-done.b_ref = bf16[2048,4096]{1,0:T(8,128)(2,1)} async-done(((bf16[128,4096]{1,0:T(8,128)(2,1)}), bf16[2048,4096]{1,0:T(8,128)(2,1)}) %all-gather.7.cloned.1.call-update) | async-done | bytes 16777232 | tf_op jit(solution)/shard_map/all_gather | solution.py:791
  347.7 30.2 %upward.2 = (bf16[1024,4096]{1,0:T(8,128)(2,1)}, bf16[1024,4096]{1,0:T(8,128)(2,1)}) custom-call(bf16[1024,2048]{1,0:T(8,128)(2,1)} %get-tuple-element.133.a_ref.a0_ref, bf16[2048,4096]{1,0:T(8,128)(2,1)} %all-gather.7.cloned.1.call-done.b_ref, f32[1,4096]{1,0:T(1,128)S(1)} %bitcast.290), custom_call_target="tpu_custom_call" | custom-call | flops 17179869184 | bytes 29360128 | tf_op jit(solution)/shard_map/upward/pallas_call | solution.py:316
  377.9 30.5 %upward.3 = (bf16[1024,4096]{1,0:T(8,128)(2,1)}, bf16[1024,4096]{1,0:T(8,128)(2,1)}) custom-call(bf16[1024,2048]{1,0:T(8,128)(2,1)} %collective-permute-done.16.a_ref.a1_ref, bf16[2048,4096]{1,0:T(8,128)(2,1)} %all-gather.7.cloned.1.call-done.b_ref, f32[1,4096]{1,0:T(1,128)S(1)} %bitcast.291), custom_call_target="tpu_custom_call" | custom-call | flops 17179869184 | bytes 29360128 | tf_op jit(solution)/shard_map/upward/pallas_call | solution.py:316
  408.4 27.1 %grad_w_down.3 = bf16[2048,2048]{1,0:T(8,128)(2,1)} custom-call(bf16[1024,4096]{1,0:T(8,128)(2,1)} %get-tuple-element.71.a0_ref.a_ref, bf16[1024,4096]{1,0:T(8,128)(2,1)} %get-tuple-element.72.a1_ref.a_ref, bf16[1024,2048]{1,0:T(8,128)(2,1)} %bitcast_select_fusion.b0_ref.a_ref.base_ref, bf16[1024,2048]{1,0:T(8,128)(2,1)} %collective-permute-done.17.b1_ref.a_ref), custom_call_target="tpu_custom_call" | custom-call | flops 17179869184 | bytes 33554432 | tf_op jit(solution)/shard_map/grad_w_down/pallas_call | solution.py:355
  443.3 26.6 %grad_w_down.2 = bf16[2048,2048]{1,0:T(8,128)(2,1)} custom-call(bf16[1024,4096]{1,0:T(8,128)(2,1)} %get-tuple-element.71.a0_ref.a_ref, bf16[1024,4096]{1,0:T(8,128)(2,1)} %get-tuple-element.72.a1_ref.a_ref, bf16[1024,2048]{1,0:T(8,128)(2,1)} %bitcast_select_fusion.b0_ref.a_ref.base_ref, bf16[1024,2048]{1,0:T(8,128)(2,1)} %collective-permute-done.17.b1_ref.a_ref), custom_call_target="tpu_custom_call" | custom-call | flops 17179869184 | bytes 33554432 | tf_op jit(solution)/shard_map/grad_w_down/pallas_call | solution.py:355
  478.9 14.8 %grad_up.5 = (bf16[1024,2048]{1,0:T(8,128)(2,1)}, f32[8,2048]{1,0:T(8,128)S(1)}) custom-call(bf16[1024,2048]{1,0:T(8,128)(2,1)} %collective-permute-done.17.b1_ref.a_ref, bf16[2048,2048]{1,0:T(8,128)(2,1)} %all-gather.11.cloned.1.call-done.b_ref, bf16[1024,4096]{1,0:T(8,128)(2,1)} %get-tuple-element.75.refs_0_, ...), custom_call_target="tpu_custom_call" | custom-call | flops 8589934592 | bytes 16777216 | tf_op jit(solution)/shard_map/grad_up/pallas_call | solution.py:316
  493.7 14.8 %grad_up.4 = (bf16[1024,2048]{1,0:T(8,128)(2,1)}, f32[8,2048]{1,0:T(8,128)S(1)}) custom-call(bf16[1024,2048]{1,0:T(8,128)(2,1)} %bitcast_select_fusion.b0_ref.a_ref.base_ref, bf16[2048,2048]{1,0:T(8,128)(2,1)} %all-gather.11.cloned.1.call-done.b_ref, bf16[1024,4096]{1,0:T(8,128)(2,1)} %get-tuple-element.73.refs_0_, ...), custom_call_target="tpu_custom_call" | custom-call | flops 8589934592 | bytes 16777216 | tf_op jit(solution)/shard_map/grad_up/pallas_call | solution.py:316
  508.4 26.1 %grad_w_up.2.refs_0_ = bf16[2048,2048]{1,0:T(8,128)(2,1)} custom-call(bf16[1024,2048]{1,0:T(8,128)(2,1)} %get-tuple-element.133.a_ref.a0_ref, bf16[1024,2048]{1,0:T(8,128)(2,1)} %collective-permute-done.16.a_ref.a1_ref, bf16[1024,2048]{1,0:T(8,128)(2,1)} %get-tuple-element.74.b0_ref.a_ref, bf16[1024,2048]{1,0:T(8,128)(2,1)} %get-tuple-element.76.b1_ref.a_ref), custom_call_target="tpu_custom_call" | custom-call | flops 17179869184 | bytes 33554432 | tf_op jit(solution)/shard_map/grad_w_up/pallas_call | solution.py:355
  658.7 26.0 %grad_w_up.3.refs_8_.refs_0_.refs_1_ = bf16[2048,2048]{1,0:T(8,128)(2,1)} custom-call(bf16[1024,2048]{1,0:T(8,128)(2,1)} %get-tuple-element.133.a_ref.a0_ref, bf16[1024,2048]{1,0:T(8,128)(2,1)} %collective-permute-done.16.a_ref.a1_ref, bf16[1024,2048]{1,0:T(8,128)(2,1)} %get-tuple-element.81.b0_ref.a_ref, bf16[1024,2048]{1,0:T(8,128)(2,1)} %get-tuple-element.82.b1_ref.a_ref), custom_call_target="tpu_custom_call" | custom-call | flops 17179869184 | bytes 33554432 | tf_op jit(solution)/shard_map/grad_w_up/pallas_call | solution.py:355
  704.3 14.9 %grad_normed2.6.refs_1_ = bf16[1024,2048]{1,0:T(8,128)(2,1)} custom-call(bf16[1024,2048]{1,0:T(8,128)(2,1)} %get-tuple-element.82.b1_ref.a_ref, bf16[2048,4096]{1,0:T(8,128)(2,1)} %all-gather.7.cloned.1.call-done.b_ref, f32[1024,2048]{1,0:T(8,128)} %grad_normed2.4.refs_0_, bf16[2048,2048]{1,0:T(8,128)(2,1)} %grad_w_up.3.refs_8_.refs_0_.refs_1_, ...), custom_call_target="tpu_custom_call" | custom-call | flops 8589934592 | bytes 16777216 | tf_op jit(solution)/shard_map/grad_normed2/pallas_call | solution.py:316
  719.4 16.4 %grad_normed2.7.refs_1_.own_ref = f32[1024,2048]{1,0:T(8,128)} custom-call(bf16[1024,2048]{1,0:T(8,128)(2,1)} %get-tuple-element.81.b0_ref.a_ref, bf16[2048,4096]{1,0:T(8,128)(2,1)} %all-gather.7.cloned.1.call-done.b_ref, f32[1024,2048]{1,0:T(8,128)} %grad_normed2.5.refs_0_, bf16[1024,2048]{1,0:T(8,128)(2,1)} %grad_normed2.6.refs_1_), custom_call_target="tpu_custom_call" | custom-call | flops 8589934592 | bytes 16777216 | tf_op jit(solution)/shard_map/grad_normed2/pallas_call | solution.py:316
  750.4 16.7 %norm_backward.2 = (f32[1024,2048]{1,0:T(8,128)}, f32[8,2048]{1,0:T(8,128)S(1)}, f32[8,2048]{1,0:T(8,128)S(1)}, bf16[1024,2048]{1,0:T(8,128)(2,1)}, f32[8,2048]{1,0:T(8,128)S(1)}) custom-call(f32[1024,2048]{1,0:T(8,128)} %grad_normed2.7.refs_1_.own_ref, bf16[1024,2048]{1,0:T(8,128)(2,1)} %collective-permute-done.29.got_ref, ...), custom_call_target="tpu_custom_call" | custom-call | tf_op jit(solution)/shard_map/norm_backward/pallas_call | solution.py:424
  791.8 17.2 %grad_w_out.1.refs_0_ = bf16[2048,1024]{1,0:T(8,128)(2,1)} custom-call(bf16[1024,2048]{1,0:T(8,128)(2,1)} %get-tuple-element.89.a_ref.a0_ref, bf16[1024,2048]{1,0:T(8,128)(2,1)} %collective-permute-done.30.a_ref.a1_ref, bf16[1024,1024]{1,0:T(8,128)(2,1)} %copy-done.70, bf16[1024,1024]{1,0:T(8,128)(2,1)} %copy-done.66, ...), custom_call_target="tpu_custom_call" | custom-call | flops 8589934592 | bytes 20971520 | tf_op jit(solution)/shard_map/grad_w_out/pallas_call | solution.py:355
  829.1 19.5 %attention_backward.2 = (bf16[1024,1024]{1,0:T(8,128)(2,1)S(1)}, bf16[4,2,1024,128]{3,2,1,0:T(8,128)(2,1)S(1)}, bf16[4,2,1024,128]{3,2,1,0:T(8,128)(2,1)S(1)}) custom-call(s32[2,2,6]{2,1,0:T(2,128)S(1)} %stack.292.nums, bf16[1024,1024]{1,0:T(8,128)(2,1)S(1)} %copy-done.74, bf16[1024,1024]{1,0:T(8,128)(2,1)} %grad_attended.2.g_ref, ...), custom_call_target="tpu_custom_call" | custom-call | flops 17179869184 | bytes 8388608 | tf_op jit(solution)/shard_map/attention_backward/pallas_call | solution.py:215
  874.1 27.4 %attention_backward.3 = (bf16[1024,1024]{1,0:T(8,128)(2,1)S(1)}, bf16[4,2,1024,128]{3,2,1,0:T(8,128)(2,1)S(1)}, bf16[4,2,1024,128]{3,2,1,0:T(8,128)(2,1)S(1)}) custom-call(s32[2,2,6]{2,1,0:T(2,128)S(1)} %stack.293.nums, bf16[1024,1024]{1,0:T(8,128)(2,1)S(1)} %copy-done.72, bf16[1024,1024]{1,0:T(8,128)(2,1)S(1)} %copy-done.69, ...), custom_call_target="tpu_custom_call" | custom-call | flops 17179869184 | bytes 8388608 | tf_op jit(solution)/shard_map/attention_backward/pallas_call | solution.py:215
  904.8 17.2 %grad_w_query.1.refs_4_.refs_0_ = bf16[2048,1024]{1,0:T(8,128)(2,1)} custom-call(bf16[1024,2048]{1,0:T(8,128)(2,1)} %get-tuple-element.136.a0_ref, bf16[1024,2048]{1,0:T(8,128)(2,1)} %collective-permute-done.6.a1_ref, bf16[1024,1024]{1,0:T(8,128)(2,1)} %copy-done.12, bf16[1024,1024]{1,0:T(8,128)(2,1)} %copy-done.14, bf16[4,2,1024,128]{3,2,1,0:T(8,128)(2,1)} %copy-done.88), custom_call_target="tpu_custom_call" | custom-call | flops 8589934592 | bytes 20971520 | tf_op jit(solution)/shard_map/grad_w_query/pallas_call | solution.py:355
  927.2 44.3 %reduce-scatter.6.cloned.1.call-done.refs_1_ = bf16[128,4096]{1,0:T(8,128)(2,1)} async-done(((bf16[512,4096]{1,0:T(8,128)(2,1)}), bf16[128,4096]{1,0:T(8,128)(2,1)}) %reduce-scatter.6.cloned.1.call-update) | async-done | bytes 1048592 | tf_op jit(solution)/shard_map/reduce_scatter | solution.py:638
  977.9 24.7 %collective-permute-done.38 = bf16[2,1024,128]{2,1,0:T(8,128)(2,1)} collective-permute-done((bf16[2,1024,128]{2,1,0:T(8,128)(2,1)}, bf16[2,1024,128]{2,1,0:T(8,128)(2,1)}, u32[]{:S(2)}, u32[]{:S(2)}) %collective-permute-start.38) | collective-permute-done | bytes 524320 | tf_op jit(solution)/shard_map/ppermute | solution.py:918
  1018.4 17.4 %mixed_out.7.refs_4_.refs_0_ = bf16[1024,2048]{1,0:T(8,128)(2,1)} custom-call(bf16[1024,4096]{1,0:T(8,128)(2,1)} %get-tuple-element.71.a0_ref.a_ref, bf16[2048,2048]{1,0:T(8,128)(2,1)} %all-gather.9.cloned.1.call-done.b_ref, f32[1024,2048]{1,0:T(8,128)} %copy-done.75, f32[1,2048]{1,0:T(1,128)S(1)} %reshape_reshape.17.refs_1_, ...), custom_call_target="tpu_custom_call" | custom-call | flops 8589934592 | bytes 16777216 | tf_op jit(solution)/shard_map/mixed_out/pallas_call | solution.py:316
  (621 shorter events, 544.8 us)
Async XLA Ops:
  7.2 125.2 %all-gather.5.cloned.1.call-start = ((), (), s32[]{:S(2)}) async-start(), calls=%async_computation.3 | async-start | bytes 9469952 | tf_op jit(solution)/shard_map/all_gather | solution.py:791
  12.0 335.7 %all-gather.7.cloned.1.call-start = ((), (), s32[]{:S(2)}) async-start(), calls=%async_computation.4 | async-start | bytes 17825792 | tf_op jit(solution)/shard_map/all_gather | solution.py:791
  17.3 461.6 %all-gather.11.cloned.1.call-start = ((), (), s32[]{:S(2)}) async-start(), calls=%async_computation.6 | async-start | bytes 8912896 | tf_op jit(solution)/shard_map/all_gather | solution.py:791
  49.6 86.5 %collective-permute-start.6 = (bf16[1024,2048]{1,0:T(8,128)(2,1)}, bf16[1024,2048]{1,0:T(8,128)(2,1)}, u32[]{:S(2)}, u32[]{:S(2)}) collective-permute-start(bf16[1024,2048]{1,0:T(8,128)(2,1)} %get-tuple-element.136.a0_ref), channel_id=1, source_target_pairs={{0,1},{1,0},{2,3},{3,2},{4,5},{5,4},{6,7},{7,6},{8,9},{9,8},{10,11... | collective-permute-start | bytes 12582920 | tf_op jit(solution)/shard_map/ppermute | solution.py:439
  50.8 578.0 %all-gather.9.cloned.1.call-start = ((), (), s32[]{:S(2)}) async-start(), calls=%async_computation.5 | async-start | bytes 8912896 | tf_op jit(solution)/shard_map/all_gather | solution.py:791
  288.6 89.3 %collective-permute-start.16 = (bf16[1024,2048]{1,0:T(8,128)(2,1)}, bf16[1024,2048]{1,0:T(8,128)(2,1)}, u32[]{:S(2)}, u32[]{:S(2)}) collective-permute-start(bf16[1024,2048]{1,0:T(8,128)(2,1)} %get-tuple-element.133.a_ref.a0_ref), channel_id=1, source_target_pairs={{0,1},{1,0},{2,3},{3,2},{4,5},{5,4},{6,7},{7,6},{8,9},{9,8},{10,11... | collective-permute-start | bytes 12582920 | tf_op jit(solution)/shard_map/ppermute | solution.py:439
  295.3 572.5 %reduce-scatter.4.cloned.1.call-start = ((), (), s32[]{:S(2)}) async-start(), calls=%async_computation.7 | async-start | bytes 5242880 | tf_op jit(solution)/shard_map/reduce_scatter | solution.py:638
  300.2 108.1 %collective-permute-start.17 = (bf16[1024,2048]{1,0:T(8,128)(2,1)}, bf16[1024,2048]{1,0:T(8,128)(2,1)}, u32[]{:S(2)}, u32[]{:S(2)}) collective-permute-start(bf16[1024,2048]{1,0:T(8,128)(2,1)} %bitcast_select_fusion.b0_ref.a_ref.base_ref), channel_id=1, source_target_pairs={{0,1},{1,0},{2,3},{3,2},{4,5},{5,4},{6,7},{7,6},{8,9},{9,8},{10,11... | collective-permute-start | bytes 12582920 | tf_op jit(solution)/shard_map/ppermute | solution.py:439
  438.6 158.9 %collective-permute-start.21 = (bf16[2,4,64,2048]{3,2,1,0:T(8,128)(2,1)}, bf16[2,4,64,2048]{3,2,1,0:T(8,128)(2,1)S(1)}, u32[]{:S(2)}, u32[]{:S(2)}) collective-permute-start(bf16[2,4,64,2048]{3,2,1,0:T(8,128)(2,1)} %dynamic-slice_bitcast_fusion.4.refs_4_), channel_id=1, source_target_pairs={{0,8},{8,0},{1,9},{9,1},{2,10},{10,2},{3,11},{11,3},{4,12},{12,4},... | collective-permute-start | bytes 6291464 | tf_op jit(solution)/shard_map/ppermute | solution.py:439
  443.2 156.2 %collective-permute-start.20 = (bf16[2,4,64,2048]{3,2,1,0:T(8,128)(2,1)}, bf16[2,4,64,2048]{3,2,1,0:T(8,128)(2,1)}, u32[]{:S(2)}, u32[]{:S(2)}) collective-permute-start(bf16[2,4,64,2048]{3,2,1,0:T(8,128)(2,1)} %dynamic-slice_bitcast_fusion.5.refs_3_), channel_id=1, source_target_pairs={{0,16},{16,0},{1,17},{17,1},{2,18},{18,2},{3,19},{19,3},{4,20},{20... | collective-permute-start | bytes 6291464 | tf_op jit(solution)/shard_map/ppermute | solution.py:439
  473.1 136.9 %collective-permute-start.19 = (bf16[2,4,64,2048]{3,2,1,0:T(8,128)(2,1)}, bf16[2,4,64,2048]{3,2,1,0:T(8,128)(2,1)}, u32[]{:S(2)}, u32[]{:S(2)}) collective-permute-start(bf16[2,4,64,2048]{3,2,1,0:T(8,128)(2,1)} %dynamic-slice_bitcast_fusion.6.refs_2_), channel_id=1, source_target_pairs={{0,8},{8,0},{1,9},{9,1},{2,10},{10,2},{3,11},{11,3},{4,12},{12,4},... | collective-permute-start | bytes 6291464 | tf_op jit(solution)/shard_map/ppermute | solution.py:439
  478.1 132.6 %collective-permute-start.18 = (bf16[2,4,64,2048]{3,2,1,0:T(8,128)(2,1)}, bf16[2,4,64,2048]{3,2,1,0:T(8,128)(2,1)}, u32[]{:S(2)}, u32[]{:S(2)}) collective-permute-start(bf16[2,4,64,2048]{3,2,1,0:T(8,128)(2,1)} %dynamic-slice_bitcast_fusion.7.refs_1_), channel_id=1, source_target_pairs={{0,16},{16,0},{1,17},{17,1},{2,18},{18,2},{3,19},{19,3},{4,20},{20... | collective-permute-start | bytes 6291464 | tf_op jit(solution)/shard_map/ppermute | solution.py:439
  537.7 119.5 %collective-permute-start.27 = (bf16[2,4,64,2048]{3,2,1,0:T(8,128)(2,1)}, bf16[2,4,64,2048]{3,2,1,0:T(8,128)(2,1)}, u32[]{:S(2)}, u32[]{:S(2)}) collective-permute-start(bf16[2,4,64,2048]{3,2,1,0:T(8,128)(2,1)} %dynamic-slice_bitcast_fusion.2.refs_2_), channel_id=1, source_target_pairs={{0,8},{8,0},{1,9},{9,1},{2,10},{10,2},{3,11},{11,3},{4,12},{12,4},... | collective-permute-start | bytes 6291464 | tf_op jit(solution)/shard_map/ppermute | solution.py:439
  598.9 85.9 %collective-permute-start.26 = (bf16[2,4,64,2048]{3,2,1,0:T(8,128)(2,1)}, bf16[2,4,64,2048]{3,2,1,0:T(8,128)(2,1)}, u32[]{:S(2)}, u32[]{:S(2)}) collective-permute-start(bf16[2,4,64,2048]{3,2,1,0:T(8,128)(2,1)} %dynamic-slice_bitcast_fusion.3.refs_1_), channel_id=1, source_target_pairs={{0,16},{16,0},{1,17},{17,1},{2,18},{18,2},{3,19},{19,3},{4,20},{20... | collective-permute-start | bytes 6291464 | tf_op jit(solution)/shard_map/ppermute | solution.py:439
  608.2 88.1 %collective-permute-start.24 = (bf16[4,64,2048]{2,1,0:T(8,128)(2,1)S(1)}, bf16[4,64,2048]{2,1,0:T(8,128)(2,1)}, u32[]{:S(2)}, u32[]{:S(2)}) collective-permute-start(bf16[4,64,2048]{2,1,0:T(8,128)(2,1)S(1)} %get-tuple-element.79.refs_4_), channel_id=1, source_target_pairs={{0,8},{8,0},{1,9},{9,1},{2,10},{10,2},{3,11},{11,3},{4,12},{12,4},... | collective-permute-start | bytes 3145736 | tf_op jit(solution)/shard_map/ppermute | solution.py:439
  609.9 86.3 %collective-permute-start.25 = (bf16[4,64,2048]{2,1,0:T(8,128)(2,1)S(1)}, bf16[4,64,2048]{2,1,0:T(8,128)(2,1)}, u32[]{:S(2)}, u32[]{:S(2)}) collective-permute-start(bf16[4,64,2048]{2,1,0:T(8,128)(2,1)S(1)} %get-tuple-element.80.refs_5_), channel_id=1, source_target_pairs={{0,16},{16,0},{1,17},{17,1},{2,18},{18,2},{3,19},{19,3},{4,20},{20... | collective-permute-start | bytes 3145736 | tf_op jit(solution)/shard_map/ppermute | solution.py:439
  617.8 78.4 %collective-permute-start.22 = (bf16[4,64,2048]{2,1,0:T(8,128)(2,1)S(1)}, bf16[4,64,2048]{2,1,0:T(8,128)(2,1)}, u32[]{:S(2)}, u32[]{:S(2)}) collective-permute-start(bf16[4,64,2048]{2,1,0:T(8,128)(2,1)S(1)} %get-tuple-element.77.refs_2_), channel_id=1, source_target_pairs={{0,8},{8,0},{1,9},{9,1},{2,10},{10,2},{3,11},{11,3},{4,12},{12,4},... | collective-permute-start | bytes 3145736 | tf_op jit(solution)/shard_map/ppermute | solution.py:439
  719.3 252.2 %reduce-scatter.6.cloned.1.call-start = ((), (), s32[]{:S(2)}) async-start(), calls=%async_computation.8 | async-start | bytes 5242880 | tf_op jit(solution)/shard_map/reduce_scatter | solution.py:638
  769.9 48.8 %collective-permute-start.32 = (bf16[2,4,64,2048]{3,2,1,0:T(8,128)(2,1)}, bf16[2,4,64,2048]{3,2,1,0:T(8,128)(2,1)S(1)}, u32[]{:S(2)}, u32[]{:S(2)}) collective-permute-start(bf16[2,4,64,2048]{3,2,1,0:T(8,128)(2,1)} %dynamic-slice_bitcast_fusion.refs_3_), channel_id=1, source_target_pairs={{0,8},{8,0},{1,9},{9,1},{2,10},{10,2},{3,11},{11,3},{4,12},{12,4},... | collective-permute-start | bytes 6291464 | tf_op jit(solution)/shard_map/ppermute | solution.py:439
  770.0 48.9 %collective-permute-start.31 = (bf16[2,4,64,2048]{3,2,1,0:T(8,128)(2,1)}, bf16[2,4,64,2048]{3,2,1,0:T(8,128)(2,1)}, u32[]{:S(2)}, u32[]{:S(2)}) collective-permute-start(bf16[2,4,64,2048]{3,2,1,0:T(8,128)(2,1)} %dynamic-slice_bitcast_fusion.1.refs_2_), channel_id=1, source_target_pairs={{0,16},{16,0},{1,17},{17,1},{2,18},{18,2},{3,19},{19,3},{4,20},{20... | collective-permute-start | bytes 6291464 | tf_op jit(solution)/shard_map/ppermute | solution.py:439
  770.7 79.4 %collective-permute-start.33 = (bf16[4,64,2048]{2,1,0:T(8,128)(2,1)}, bf16[4,64,2048]{2,1,0:T(8,128)(2,1)S(1)}, u32[]{:S(2)}, u32[]{:S(2)}) collective-permute-start(bf16[4,64,2048]{2,1,0:T(8,128)(2,1)} %copy-done.42), channel_id=1, source_target_pairs={{0,8},{8,0},{1,9},{9,1},{2,10},{10,2},{3,11},{11,3},{4,12},{12,4},... | collective-permute-start | bytes 3145736 | tf_op jit(solution)/shard_map/ppermute | solution.py:439
  772.5 77.5 %collective-permute-start.34 = (bf16[4,64,2048]{2,1,0:T(8,128)(2,1)}, bf16[4,64,2048]{2,1,0:T(8,128)(2,1)}, u32[]{:S(2)}, u32[]{:S(2)}) collective-permute-start(bf16[4,64,2048]{2,1,0:T(8,128)(2,1)} %copy-done.41), channel_id=1, source_target_pairs={{0,16},{16,0},{1,17},{17,1},{2,18},{18,2},{3,19},{19,3},{4,20},{20... | collective-permute-start | bytes 3145736 | tf_op jit(solution)/shard_map/ppermute | solution.py:439
  867.4 235.7 %reduce-scatter.8.cloned.1.call-start = ((), (), s32[]{:S(2)}) async-start(), calls=%async_computation.9 | async-start | bytes 1310720 | tf_op jit(solution)/shard_map/reduce_scatter | solution.py:638
  903.5 114.9 %collective-permute-start.28 = (bf16[1024,2048]{1,0:T(8,128)(2,1)}, bf16[1024,2048]{1,0:T(8,128)(2,1)}, u32[]{:S(2)}, u32[]{:S(2)}) collective-permute-start(bf16[1024,2048]{1,0:T(8,128)(2,1)} %mixed_out.6.refs_0_), channel_id=1, source_target_pairs={{0,1},{1,0},{2,3},{3,2},{4,5},{5,4},{6,7},{7,6},{8,9},{9,8},{10,11... | collective-permute-start | bytes 12582920 | tf_op jit(solution)/shard_map/ppermute | solution.py:439
  (180 other events, 2835.1 us)
Sparse Core Ops, SparseCore 0:
  12.1 120.2 all-gather.4
  135.2 212.4 all-gather.6
  351.1 114.3 all-gather.10
  468.2 160.5 all-gather.8
  719.4 74.1 reduce-scatter.3
  867.6 103.8 reduce-scatter.5
  1059.8 29.1 reduce-scatter.7

commit v4 on v3

--- a/solution.py
+++ b/solution.py
@@ -17,6 +17,13 @@
 PAIR = [(0, 1), (1, 0)]
 BF16 = jnp.bfloat16
 F32 = jnp.float32
+COST_SCALE = 8
+
+
+def estimate(flops, bytes_accessed, transcendentals):
+    return pl.CostEstimate(
+        flops=flops // COST_SCALE, bytes_accessed=bytes_accessed // COST_SCALE, transcendentals=transcendentals // COST_SCALE
+    )
 
 
 def key_place(j, tk, nums, w, i, chips_z, chip_len):
@@ -117,7 +124,7 @@
             jax.ShapeDtypeStruct((heads, rows), F32),
         ],
         compiler_params=pltpu.CompilerParams(vmem_limit_bytes=40 * 2**20),
-        cost_estimate=pl.CostEstimate(
+        cost_estimate=estimate(
             flops=2 * rows * width * chip_len * chips_z, bytes_accessed=4 * rows * width,
             transcendentals=rows * heads * chip_len * chips_z // 4,
         ),
@@ -243,7 +250,7 @@
         ),
         out_shape=[jax.ShapeDtypeStruct((rows, width), BF16), key_shape, key_shape],
         compiler_params=pltpu.CompilerParams(vmem_limit_bytes=40 * 2**20),
-        cost_estimate=pl.CostEstimate(
+        cost_estimate=estimate(
             flops=4 * rows * width * chip_len * chips_z, bytes_accessed=8 * rows * width,
             transcendentals=rows * heads * chip_len * chips_z // 4,
         ),
@@ -325,16 +332,16 @@
         out_specs=[spec[w] for _, w in outs],
         out_shape=[jax.ShapeDtypeStruct(shape[w], d) for d, w in outs],
         compiler_params=pltpu.CompilerParams(vmem_limit_bytes=52 * 2**20),
-        cost_estimate=pl.CostEstimate(flops=2 * m * n * k, bytes_accessed=2 * (m * k + n * k + m * n), transcendentals=0),
+        cost_estimate=estimate(flops=2 * m * n * k, bytes_accessed=2 * (m * k + n * k + m * n), transcendentals=0),
         name=name,
     )(a, b, *[array for array, _ in extras], *deps)
     return res[0] if len(outs) == 1 else res
 
 
-def tokens_kernel(chunk, dep_count, a0_ref, a1_ref, b0_ref, b1_ref, *refs):
-    out, left = refs[dep_count:]
-
-    @pl.when(pl.program_id(1) == 0)
+def tokens_kernel(chunk, chips_z, dep_count, spot, a0_ref, a1_ref, b0_ref, b1_ref, *refs):
+    out, first, second, left = refs[dep_count:]
+
+    @pl.when(pl.program_id(0) == 0)
     def _():
         left[0] = jnp.transpose(a0_ref[...])
         left[1] = jnp.transpose(a1_ref[...])
@@ -342,27 +349,41 @@
     for r in range(0, left.shape[1], chunk):
         part = pl.ds(r, chunk)
         out[part, :] = (plain_dot(left[0, part, :], b0_ref[...]) + plain_dot(left[1, part, :], b1_ref[...])).astype(BF16)
-
-
-def over_tokens(a, b, tm=2048, tn=512, chunk=256, deps=(), a_cols=None, name="weight_gradient"):
+    half = first.shape[2]
+    y, x = spot[0], spot[1]
+    for n in range(2):
+        for z in range(chips_z):
+            for sent, plane, part in ((first, (1 - y) * 2 + n, 0), (second, n * 2 + 1 - x, 1)):
+                row = ((plane * chips_z + z) * 2 + part) * half
+                sent[n, z] = out[pl.ds(pl.multiple_of(row, half), half), :]
+
+
+def over_tokens(a, b, spot, chips_z, tn=512, chunk=256, deps=(), a_cols=None, name="weight_gradient"):
     k = a[0].shape[0]
     first, m = a_cols or (0, a[0].shape[1])
     n = b[0].shape[1]
-    tm, tn, chunk = min(tm, m), min(tn, n), min(chunk, m)
-    skip = first // tm
-    a_spec = pl.BlockSpec((k, tm), lambda i, j: (0, i + skip))
-    b_spec = pl.BlockSpec((k, tn), lambda i, j: (0, j))
-    return pl.pallas_call(
-        functools.partial(tokens_kernel, chunk, len(deps)),
-        grid=(m // tm, n // tn),
-        in_specs=[a_spec, a_spec, b_spec, b_spec] + [pl.BlockSpec(memory_space=pl.ANY)] * len(deps),
-        out_specs=pl.BlockSpec((tm, tn), lambda i, j: (i, j)),
-        scratch_shapes=[pltpu.VMEM((2, tm, k), BF16)],
-        out_shape=jax.ShapeDtypeStruct((m, n), BF16),
-        compiler_params=pltpu.CompilerParams(vmem_limit_bytes=52 * 2**20),
-        cost_estimate=pl.CostEstimate(flops=4 * m * n * k, bytes_accessed=4 * (m * k + n * k + m * n), transcendentals=0),
+    tn, chunk = min(tn, n), min(chunk, m)
+    skip = first // m
+    half = max(m // (8 * chips_z), 16)
+    a_spec = pl.BlockSpec((k, m), lambda j, spot: (0, skip))
+    b_spec = pl.BlockSpec((k, tn), lambda j, spot: (0, j))
+    sent_spec = pl.BlockSpec((2, chips_z, half, tn), lambda j, spot: (0, 0, 0, j))
+    sent_shape = jax.ShapeDtypeStruct((2, chips_z, half, n), BF16)
+    total, *sent = pl.pallas_call(
+        functools.partial(tokens_kernel, chunk, chips_z, len(deps)),
+        grid_spec=pltpu.PrefetchScalarGridSpec(
+            num_scalar_prefetch=1,
+            grid=(n // tn,),
+            in_specs=[a_spec, a_spec, b_spec, b_spec] + [pl.BlockSpec(memory_space=pl.ANY)] * len(deps),
+            out_specs=[pl.BlockSpec((m, tn), lambda j, spot: (0, j)), sent_spec, sent_spec],
+            scratch_shapes=[pltpu.VMEM((2, m, k), BF16)],
+        ),
+        out_shape=[jax.ShapeDtypeStruct((m, n), BF16), sent_shape, sent_shape],
+        compiler_params=pltpu.CompilerParams(vmem_limit_bytes=56 * 2**20),
+        cost_estimate=estimate(flops=4 * m * n * k, bytes_accessed=4 * (m * k + n * k + m * n), transcendentals=0),
         name=name,
-    )(*a, *b, *deps)
+    )(spot, *a, *b, *deps)
+    return total, tuple(sent)
 
 
 def contract_rows(left_op, right_op):
@@ -471,6 +492,21 @@
         out_shape=jax.ShapeDtypeStruct(value.shape, value.dtype),
         name="hold",
     )(value, *deps)
+
+
+def add_kernel(first, second, *refs):
+    refs[-1][...] = (first[...].astype(F32) + second[...].astype(F32)).astype(BF16)
+
+
+def add_after(first, second, *deps):
+    whole = pl.BlockSpec(first.shape, lambda: (0,) * first.ndim)
+    return pl.pallas_call(
+        add_kernel,
+        in_specs=[whole] * 2 + [pl.BlockSpec(memory_space=pl.ANY)] * len(deps),
+        out_specs=whole,
+        out_shape=jax.ShapeDtypeStruct(first.shape, BF16),
+        name="add_after",
+    )(first, second, *deps)
 
 
 def place_kernel(moves_of, whole_count, half, dep_count, spot, *refs):
@@ -571,16 +607,11 @@
 
 
 class Sum:
-    def __init__(self, total, spot, chips_z):
+    def __init__(self, total, sent, spot, chips_z):
         self.cols = total.shape[1]
         self.half = total.shape[0] // (8 * chips_z)
         self.total, self.spot, self.chips_z = total.reshape(2, 2, chips_z, 2, self.half, self.cols), spot, chips_z
-        self.sent = (self.cut(0, 1 - spot[0], 0), self.cut(1, 1 - spot[1], 1))
-
-    def cut(self, dim, index, part):
-        at, size = [0, 0, 0, part, 0, 0], [2, 2, self.chips_z, 1, self.half, self.cols]
-        at[dim], size[dim] = index, 1
-        return lax.dynamic_slice(self.total, at, size).reshape(2, self.chips_z, self.half, self.cols)
+        self.sent = sent
 
     def first(self, *deps):
         got = (swap(self.sent[0], "y"), swap(self.sent[1], "x"))
@@ -688,6 +719,16 @@
         for step, pairs in doubling(axis):
             vector = in_order((index // step) % 2, vector, lax.ppermute(vector, axis, pairs))
     return vector.reshape(-1, vector.shape[-1])
+
+
+def gather_rows(block):
+    rows = block[None]
+    for axis in reversed(CHIPS):
+        index = lax.axis_index(axis)
+        for step, pairs in doubling(axis):
+            rows = in_order((index // step) % 2, rows, lax.ppermute(rows, axis, pairs))
+            rows = rows.reshape(-1, *block.shape)
+    return rows.reshape(-1, block.shape[1])
 
 
 def sum_small(vector):
@@ -799,7 +840,7 @@
     tokens = hidden_in.reshape(own_count, width).astype(F32)
     unit1, inverse1 = normalise(tokens)
     normed1 = both_cores((unit1 * gain1 + bias1).astype(BF16))
-    w_query, w_kv = near_all[:, :half_q], near_all[:, half_q : half_q + HD]
+    w_query, w_kv = near_all[:, :half_q], gather_rows(near_block[:, half_q : half_q + HD])
     own_kv = [(plain_dot(rows, w_kv) + bias_qkv[half_q:]).astype(BF16) for rows in normed1]
     own_kv = [rows.reshape(windows, local_len, HD) for rows in own_kv]
     own_kv = jnp.swapaxes(in_order(core, *own_kv), 0, 1).reshape(windows, chip_len, HD)
@@ -838,8 +879,11 @@
     upstream = jnp.where(valid, cotangent.reshape(own_count, width), 0)
     grad_down = both_cores(upstream)
     units = active[0].shape[1] // 2
-    down_totals = [over_tokens(active, grad_down, a_cols=(n * units, units), name="grad_w_down") for n in (0, 1)]
-    down_sums = [Sum(total, spot, chips_z) for total in down_totals] if by_hand else ()
+    down_totals = [
+        over_tokens(active, grad_down, spot, chips_z, a_cols=(n * units, units), name="grad_w_down") for n in (0, 1)
+    ]
+    down_sums = [Sum(*total, spot, chips_z) for total in down_totals] if by_hand else ()
+    down_totals = [total for total, _ in down_totals]
 
     grad_up, unit_sums, up_totals, up_sums = [None, None], [], [], []
     grad_normed, down_out = [None, None], [None, None]
@@ -851,16 +895,16 @@
                 extra_part=part, deps=deps, name="grad_up",
             )
             unit_sums.append(sums)
-        up_totals.append(over_tokens(normed2, grad_up, name="grad_w_up"))
+        total, sent = over_tokens(normed2, grad_up, spot, chips_z, name="grad_w_up")
+        up_totals.append(total)
         deps = (up_totals[-1],)
         if by_hand:
-            up_sums.append(Sum(up_totals[-1], spot, chips_z))
+            up_sums.append(Sum(total, sent, spot, chips_z))
             deps += up_sums[-1].sent
             if part == 1:
                 down_sums[0].second(up_totals[1], beside=down_sums[1:])
                 grad_w_down = down_sums[0].over_z()
-                up_sums[0].first(up_totals[1])
-                deps += (down_sums[0].both,) + up_sums[0].sent
+                deps += (down_sums[0].both,)
         for n in (1, 0):
             grad_normed[n] = matmul(
                 "nt", grad_up[n], w_up_all, [(F32 if n == 0 or part == 0 else BF16, "tile")],
@@ -885,18 +929,18 @@
     )
     branch = both_cores(branch_own)
 
-    grad_attended = [matmul("nn", branch[n], w_out_all, [(BF16, "tile")], name="grad_attended") for n in (0, 1)]
-    out_total = over_tokens(branch, attended, deps=(grad_attended[1],), name="grad_w_out")
-    if by_hand:
-        out_sum = Sum(out_total, spot, chips_z)
-        up_sums[1].first(out_total)
+    grad_attended, deps = [], ()
+    for n in (0, 1):
+        grad_attended.append(matmul("nn", branch[n], w_out_all, [(BF16, "tile")], deps=deps, name="grad_attended"))
+        if by_hand and n == 0:
+            for one in up_sums:
+                one.first(grad_attended[0])
+                deps += one.sent
     grad_query, grad_keys, grad_values = [None, None], [None, None], [None, None]
     for n in (0, 1):
         deps = ()
         if by_hand:
-            if n == 0:
-                deps = out_sum.sent + up_sums[1].sent
-            else:
+            if n == 1:
                 up_sums[0].second(grad_keys[0], beside=up_sums[1:])
                 grad_w_up = up_sums[0].over_z()
                 deps = (up_sums[0].both, down_sums[0].result)
@@ -904,34 +948,37 @@
             queries[n], grad_attended[n], 0, attended[n], lse[n], keys, values, starts[n],
             tile_numbers(starts[n], positions[n], z, tq, tk), tq, tk, deps,
         )
-    if by_hand:
-        out_sum.first(grad_keys[1])
     grad_keys = grad_keys[0].astype(F32) + grad_keys[1].astype(F32)
     grad_values = grad_values[0].astype(F32) + grad_values[1].astype(F32)
     kv_sent = jnp.where(core == 0, grad_values, grad_keys).astype(BF16)
-    query_total = over_tokens(
-        normed1, grad_query, deps=(kv_sent,), name="grad_w_query"
-    )
+    query_total, query_sent = over_tokens(normed1, grad_query, spot, chips_z, deps=(kv_sent,), name="grad_w_query")
     grad_kv = (jnp.where(core == 0, grad_keys, grad_values) + swap(kv_sent, "core").astype(F32)).astype(BF16)
     running = hold(grad_kv[1 % chips_z], query_total, *((up_sums[0].result,) if by_hand else ()))
+    out_total, sent = over_tokens(branch, attended, spot, chips_z, deps=(running,), name="grad_w_out")
+    if by_hand:
+        out_sum = Sum(out_total, sent, spot, chips_z)
+    deps = (out_total,)
     for s in range(2, chips_z + 1):
-        running = (grad_kv[s % chips_z].astype(F32) + lax.ppermute(running, "z", ring).astype(F32)).astype(BF16)
+        running = add_after(grad_kv[s % chips_z], lax.ppermute(running, "z", ring), *deps)
+        if s == 2:
+            mixed_out = matmul(
+                "nn", active[0], w_down_parts[1], [(BF16, "tile")], sum_finish,
+                [(residual, "tile"), (bias_down.reshape(1, -1), "row"), (swap(down_other, "core"), "tile"), (down_out[0], "tile")],
+                depth=units, a_part=1, deps=(running, *sent), name="mixed_out",
+            )
+            deps = (mixed_out,)
     grad_kv = jnp.swapaxes(running.reshape(windows, 2, local_len, HD), 0, 1)
     grad_kv = in_order(core, grad_kv[0], grad_kv[1]).reshape(2, own_count, HD)
     kv_total = (contract_rows(normed1[0], grad_kv[0]) + contract_rows(normed1[1], grad_kv[1])).astype(BF16)
     qkv_total = jnp.concatenate([query_total, kv_total], axis=1)
-    mixed_out = matmul(
-        "nn", active[0], w_down_parts[1], [(BF16, "tile")], sum_finish,
-        [(residual, "tile"), (bias_down.reshape(1, -1), "row"), (swap(down_other, "core"), "tile"), (down_out[0], "tile")],
-        depth=units, a_part=1, deps=(query_total,), name="mixed_out",
-    )
     grad_qkv = [jnp.concatenate([grad_query[n], grad_kv[n]], axis=1) for n in (0, 1)]
     deps = (mixed_out,)
     if by_hand:
-        out_sum.second(mixed_out)
-        grad_w_out = out_sum.over_z()
-        qkv_sum = Sum(qkv_total, spot, chips_z)
-        deps += qkv_sum.sent + (out_sum.both,)
+        parts = kv_total.reshape(2, 2, chips_z, 2, -1, HD)
+        kv_parts = (pick(parts[:, :, :, 0], 1 - y, 0), pick(parts[:, :, :, 1], 1 - x, 1))
+        sent = tuple(jnp.concatenate(pair, axis=3) for pair in zip(query_sent, kv_parts))
+        qkv_sum = Sum(qkv_total, sent, spot, chips_z)
+        deps += qkv_sum.sent
     first_other = matmul("nt", grad_qkv[1], near_all, [(BF16, "tile")], deps=deps, name="grad_normed1")
     first_own = matmul("nt", grad_qkv[0], near_all, [(F32, "tile")], deps=(first_other,), name="grad_normed1")
     grad_hidden, gain1_sums, bias1_sums = norm_backward(
@@ -939,7 +986,10 @@
     )
     if by_hand:
         qkv_sum.first(gain1_sums)
-        qkv_sum.second()
+        out_sum.first(gain1_sums)
+        qkv_sum.second(out_sum.sent[0])
+        out_sum.second(qkv_sum.both)
+        grad_w_out = out_sum.over_z()
         grad_w_qkv = qkv_sum.round_z(ring)
     qkv_sums = [jnp.sum(rows.astype(F32).reshape(-1, 8, rows.shape[1]), axis=0) for rows in grad_qkv]
     upstream_sums = jnp.sum(upstream.astype(F32).reshape(-1, 8, width), axis=0)

time: 1190 us -> 1200 us (level)
  local copies, waits for them, and re-layouts: 98.7 us -> 81.9 us
  Pallas kernels: 569 us -> 585 us
  waiting for transfers between devices: 338 us -> 324 us
  starting transfers between devices: 60.7 us -> 72.9 us
    all_gather x4, waiting for transfers between devices: 139 us -> 87 us  [gather(): return lax.all_gather(block, CHIPS, axis=0, tiled=True)]
    ppermute x3 -> x7, waiting for transfers between devices: 29.7 us -> 60.4 us  [the longest x3 40.2 us: body(): lax.ppermute(running, 'z', ring)]
    reshape x12 -> x0, local copies, waits for them, and re-layouts: 25.7 us -> none  [cut(): lax.dynamic_slice(self.total, at, size)]
    ppermute x3, waiting for transfers between devices: 49 us -> 68.1 us  [body(): own_kv = lax.ppermute(own_kv, 'z', ring)]
    reduce_scatter x3, waiting for transfers between devices: 44.3 us -> 26.8 us  [over_z(): lax.psum_scatter(self.both, 'z', scatter_dimension=0, tiled=True)]
    ppermute x42, waiting for transfers between devices: 36 us -> 52.8 us  [swap(): return lax.ppermute(values, axis, PAIR)]
    pallas_call x6 -> x9, Pallas kernels: 140 us -> 155 us  [the longest x6 149 us: over_tokens(): pl.pallas_call(functools.partial(tokens_kernel, chunk, chips_z, len(deps)...]
    ppermute x3 -> x7, starting transfers between devices: 1.59 us -> 15.7 us  [the longest x3 8.29 us: body(): lax.ppermute(running, 'z', ring)]
  transfers between devices with their start and end apart: 68 -> 72, of which waited for: 27 -> 29; matrix products, arithmetic and copies ran while one was open for 11% -> 9% of each run, Pallas kernels for 46% -> 48%
where the time goes in v4:
time: 1200 us; the launch traced here: 1180 us
  Pallas kernels  585 us (49%)
  waiting for transfers between devices  324 us (27%)
  local copies, waits for them, and re-layouts  81.9 us (7%)
  starting transfers between devices  72.9 us (6%)
  other arithmetic  57.2 us (5%)
  matrix products  37.3 us (3%)
  between operations  19.4 us (2%)
    pallas_call x19, Pallas kernels, matmul(): pl.pallas_call(functools.partial(rows_kernel, kind, chunk, len(extras), l...  283 us
    pallas_call x6, Pallas kernels, over_tokens(): pl.pallas_call(functools.partial(tokens_kernel, chunk, chips_z, len(deps)...  149 us
    all_gather x4, waiting for transfers between devices, gather(): return lax.all_gather(block, CHIPS, axis=0, tiled=True)  87 us
    ppermute x3, waiting for transfers between devices, body(): own_kv = lax.ppermute(own_kv, 'z', ring)  68.1 us
    unnamed x300, local copies, waits for them, and re-layouts  54 us
    ppermute x42, waiting for transfers between devices, swap(): return lax.ppermute(values, axis, PAIR)  52.8 us
    pallas_call x2, Pallas kernels, attend_backward(): pl.pallas_call(functools.partial(backward_kernel, tq, tk, heads, len(deps...  49.1 us
    ppermute x3, waiting for transfers between devices, body(): lax.ppermute(running, 'z', ring)  40.2 us
  transfers between devices with their start and end apart: 72, of which 29 were waited for; matrix products, arithmetic and copies ran while one was open for 9% of the time, Pallas kernels for 48%

profile of v4, /device:TPU:0, one launch (start us, length us, event | category | flops | bytes accessed | tf_op | source)
XLA Modules:
  0.0 1177.9 jit_solution(11437002194393657549)
XLA Ops:
  89.8 26.6 %collective-permute-done.12 = bf16[2,1024,128]{2,1,0:T(8,128)(2,1)S(1)} collective-permute-done((bf16[2,1024,128]{2,1,0:T(8,128)(2,1)S(1)}, bf16[2,1024,128]{2,1,0:T(8,128)(2,1)S(1)}, u32[]{:S(2)}, u32[]{:S(2)}) %collective-permute-start.12) | collective-permute-done | bytes 524320 | tf_op jit(solution)/shard_map/ppermute | solution.py:853
  120.8 33.3 %collective-permute-done.14 = bf16[2,1024,128]{2,1,0:T(8,128)(2,1)S(1)} collective-permute-done((bf16[2,1024,128]{2,1,0:T(8,128)(2,1)S(1)}, bf16[2,1024,128]{2,1,0:T(8,128)(2,1)S(1)}, u32[]{:S(2)}, u32[]{:S(2)}) %collective-permute-start.14) | collective-permute-done | bytes 524320 | tf_op jit(solution)/shard_map/ppermute | solution.py:853
  182.7 15.5 %attention_forward.2 = (bf16[1024,1024]{1,0:T(8,128)(2,1)S(1)}, f32[8,1024]{1,0:T(8,128)S(1)}) custom-call(s32[2,1,6]{2,1,0:T(1,128)S(1)} %stack.345.nums, bf16[1024,1024]{1,0:T(8,128)(2,1)S(1)} %add_convert_fusion.3.q_ref, bf16[4,2,1024,128]{3,2,1,0:T(8,128)(2,1)S(1)} %copy-done.2, bf16[4,2,1024,128]{3,2,1,0:T(8,128)(2,1)S(1)} %pad_maximum_fusion.4.v_ref, ...), custom_call_target="tpu_custom_call" | custom-call | flops 1073741824 | bytes 524288 | tf_op jit(solution)/shard_map/attention_forward/pallas_call | solution.py:100
  260.0 87.0 %all-gather.7.cloned.1.call-done.b_ref = bf16[2048,4096]{1,0:T(8,128)(2,1)} async-done(((bf16[128,4096]{1,0:T(8,128)(2,1)}), bf16[2048,4096]{1,0:T(8,128)(2,1)}) %all-gather.7.cloned.1.call-update) | async-done | bytes 16777232 | tf_op jit(solution)/shard_map/all_gather | solution.py:832
  347.0 30.2 %upward.2 = (bf16[1024,4096]{1,0:T(8,128)(2,1)}, bf16[1024,4096]{1,0:T(8,128)(2,1)}) custom-call(bf16[1024,2048]{1,0:T(8,128)(2,1)} %get-tuple-element.169.a_ref.a0_ref, bf16[2048,4096]{1,0:T(8,128)(2,1)} %all-gather.7.cloned.1.call-done.b_ref, f32[1,4096]{1,0:T(1,128)S(1)} %bitcast.271), custom_call_target="tpu_custom_call" | custom-call | flops 2147483648 | bytes 3670016 | tf_op jit(solution)/shard_map/upward/pallas_call | solution.py:323
  377.1 30.6 %upward.3 = (bf16[1024,4096]{1,0:T(8,128)(2,1)}, bf16[1024,4096]{1,0:T(8,128)(2,1)}) custom-call(bf16[1024,2048]{1,0:T(8,128)(2,1)} %collective-permute-done.20.a_ref.a1_ref, bf16[2048,4096]{1,0:T(8,128)(2,1)} %all-gather.7.cloned.1.call-done.b_ref, f32[1,4096]{1,0:T(1,128)S(1)} %bitcast.272), custom_call_target="tpu_custom_call" | custom-call | flops 2147483648 | bytes 3670016 | tf_op jit(solution)/shard_map/upward/pallas_call | solution.py:323
  407.8 28.3 %grad_w_down.3 = (bf16[2048,2048]{1,0:T(8,128)(2,1)}, bf16[2,4,64,2048]{3,2,1,0:T(8,128)(2,1)}, bf16[2,4,64,2048]{3,2,1,0:T(8,128)(2,1)}) custom-call(s32[3]{0:T(128)} %pad_add_fusion.spot, bf16[1024,4096]{1,0:T(8,128)(2,1)} %get-tuple-element.89.a0_ref.a_ref, bf16[1024,4096]{1,0:T(8,128)(2,1)} %get-tuple-element.90.a1_ref.a_ref, ...), custom_call_target="tpu_custom_call" | custom-call | flops 2147483648 | bytes 4194304 | tf_op jit(solution)/shard_map/grad_w_down/pallas_call | solution.py:372
  437.6 27.7 %grad_w_down.2 = (bf16[2048,2048]{1,0:T(8,128)(2,1)}, bf16[2,4,64,2048]{3,2,1,0:T(8,128)(2,1)}, bf16[2,4,64,2048]{3,2,1,0:T(8,128)(2,1)}) custom-call(s32[3]{0:T(128)} %pad_add_fusion.spot, bf16[1024,4096]{1,0:T(8,128)(2,1)} %get-tuple-element.89.a0_ref.a_ref, bf16[1024,4096]{1,0:T(8,128)(2,1)} %get-tuple-element.90.a1_ref.a_ref, ...), custom_call_target="tpu_custom_call" | custom-call | flops 2147483648 | bytes 4194304 | tf_op jit(solution)/shard_map/grad_w_down/pallas_call | solution.py:372
  467.8 14.8 %grad_up.5 = (bf16[1024,2048]{1,0:T(8,128)(2,1)}, f32[8,2048]{1,0:T(8,128)S(1)}) custom-call(bf16[1024,2048]{1,0:T(8,128)(2,1)} %collective-permute-done.21.b1_ref.a_ref, bf16[2048,2048]{1,0:T(8,128)(2,1)} %all-gather.11.cloned.1.call-done.b_ref, bf16[1024,4096]{1,0:T(8,128)(2,1)} %get-tuple-element.97.refs_0_, ...), custom_call_target="tpu_custom_call" | custom-call | flops 1073741824 | bytes 2097152 | tf_op jit(solution)/shard_map/grad_up/pallas_call | solution.py:323
  482.6 14.8 %grad_up.4 = (bf16[1024,2048]{1,0:T(8,128)(2,1)}, f32[8,2048]{1,0:T(8,128)S(1)}) custom-call(bf16[1024,2048]{1,0:T(8,128)(2,1)} %bitcast_select_fusion.b0_ref.a_ref.base_ref, bf16[2048,2048]{1,0:T(8,128)(2,1)} %all-gather.11.cloned.1.call-done.b_ref, bf16[1024,4096]{1,0:T(8,128)(2,1)} %get-tuple-element.91.refs_0_, ...), custom_call_target="tpu_custom_call" | custom-call | flops 1073741824 | bytes 2097152 | tf_op jit(solution)/shard_map/grad_up/pallas_call | solution.py:323
  497.4 27.9 %grad_w_up.2 = (bf16[2048,2048]{1,0:T(8,128)(2,1)}, bf16[2,4,64,2048]{3,2,1,0:T(8,128)(2,1)}, bf16[2,4,64,2048]{3,2,1,0:T(8,128)(2,1)}) custom-call(s32[3]{0:T(128)} %pad_add_fusion.spot, bf16[1024,2048]{1,0:T(8,128)(2,1)} %get-tuple-element.169.a_ref.a0_ref, bf16[1024,2048]{1,0:T(8,128)(2,1)} %collective-permute-done.20.a_ref.a1_ref, ...), custom_call_target="tpu_custom_call" | custom-call | flops 2147483648 | bytes 4194304 | tf_op jit(solution)/shard_map/grad_w_up/pallas_call | solution.py:372
  631.2 27.8 %grad_w_up.3 = (bf16[2048,2048]{1,0:T(8,128)(2,1)}, bf16[2,4,64,2048]{3,2,1,0:T(8,128)(2,1)}, bf16[2,4,64,2048]{3,2,1,0:T(8,128)(2,1)}) custom-call(s32[3]{0:T(128)} %pad_add_fusion.spot, bf16[1024,2048]{1,0:T(8,128)(2,1)} %get-tuple-element.169.a_ref.a0_ref, bf16[1024,2048]{1,0:T(8,128)(2,1)} %collective-permute-done.20.a_ref.a1_ref, ...), custom_call_target="tpu_custom_call" | custom-call | flops 2147483648 | bytes 4194304 | tf_op jit(solution)/shard_map/grad_w_up/pallas_call | solution.py:372
  668.0 16.1 %grad_normed2.6.refs_1_ = bf16[1024,2048]{1,0:T(8,128)(2,1)} custom-call(bf16[1024,2048]{1,0:T(8,128)(2,1)} %get-tuple-element.109.b1_ref.a_ref, bf16[2048,4096]{1,0:T(8,128)(2,1)} %all-gather.7.cloned.1.call-done.b_ref, f32[1024,2048]{1,0:T(8,128)} %grad_normed2.4.refs_0_, bf16[2048,2048]{1,0:T(8,128)(2,1)} %get-tuple-element.110.refs_8_.refs_1_, ...), custom_call_target="tpu_custom_call" | custom-call | flops 1073741824 | bytes 2097152 | tf_op jit(solution)/shard_map/grad_normed2/pallas_call | solution.py:323
  689.2 16.0 %grad_normed2.7.refs_1_.own_ref = f32[1024,2048]{1,0:T(8,128)} custom-call(bf16[1024,2048]{1,0:T(8,128)(2,1)} %get-tuple-element.108.b0_ref.a_ref, bf16[2048,4096]{1,0:T(8,128)(2,1)} %all-gather.7.cloned.1.call-done.b_ref, f32[1024,2048]{1,0:T(8,128)} %grad_normed2.5.refs_0_, bf16[1024,2048]{1,0:T(8,128)(2,1)} %grad_normed2.6.refs_1_), custom_call_target="tpu_custom_call" | custom-call | flops 1073741824 | bytes 2097152 | tf_op jit(solution)/shard_map/grad_normed2/pallas_call | solution.py:323
  705.2 14.3 %mixed_out.6.refs_0_ = bf16[1024,2048]{1,0:T(8,128)(2,1)} custom-call(bf16[1024,4096]{1,0:T(8,128)(2,1)} %get-tuple-element.90.a1_ref.a_ref, bf16[2048,2048]{1,0:T(8,128)(2,1)} %all-gather.9.cloned.1.call-done.b_ref, f32[1024,2048]{1,0:T(8,128)} %mixed_out.4.refs_0_, f32[1024,2048]{1,0:T(8,128)} %grad_normed2.7.refs_1_.own_ref), custom_call_target="tpu_custom_call" | custom-call | flops 1073741824 | bytes 2097152 | tf_op jit(solution)/shard_map/mixed_out/pallas_call | solution.py:323
  719.7 16.7 %norm_backward.2 = (f32[1024,2048]{1,0:T(8,128)}, f32[8,2048]{1,0:T(8,128)S(1)}, f32[8,2048]{1,0:T(8,128)S(1)}, bf16[1024,2048]{1,0:T(8,128)(2,1)S(1)}, f32[8,2048]{1,0:T(8,128)S(1)}) custom-call(f32[1024,2048]{1,0:T(8,128)} %grad_normed2.7.refs_1_.own_ref, bf16[1024,2048]{1,0:T(8,128)(2,1)} %collective-permute-done.31.got_ref, ...), custom_call_target="tpu_custom_call" | custom-call | tf_op jit(solution)/shard_map/norm_backward/pallas_call | solution.py:445
  757.3 20.4 %collective-permute-done.33.got_one = bf16[2,4,64,2048]{3,2,1,0:T(8,128)(2,1)S(1)} collective-permute-done((bf16[2,4,64,2048]{3,2,1,0:T(8,128)(2,1)}, bf16[2,4,64,2048]{3,2,1,0:T(8,128)(2,1)S(1)}, u32[]{:S(2)}, u32[]{:S(2)}) %collective-permute-start.33) | collective-permute-done | bytes 2097184 | tf_op jit(solution)/shard_map/ppermute | solution.py:460
  792.8 19.1 %attention_backward.2 = (bf16[1024,1024]{1,0:T(8,128)(2,1)S(1)}, bf16[4,2,1024,128]{3,2,1,0:T(8,128)(2,1)S(1)}, bf16[4,2,1024,128]{3,2,1,0:T(8,128)(2,1)S(1)}) custom-call(s32[2,2,6]{2,1,0:T(2,128)S(1)} %stack.353.nums, bf16[1024,1024]{1,0:T(8,128)(2,1)S(1)} %copy-done.29, bf16[1024,1024]{1,0:T(8,128)(2,1)S(1)} %copy-done.11, ...), custom_call_target="tpu_custom_call" | custom-call | flops 2147483648 | bytes 1048576 | tf_op jit(solution)/shard_map/attention_backward/pallas_call | solution.py:222
  850.5 30.1 %attention_backward.3 = (bf16[1024,1024]{1,0:T(8,128)(2,1)S(1)}, bf16[4,2,1024,128]{3,2,1,0:T(8,128)(2,1)S(1)}, bf16[4,2,1024,128]{3,2,1,0:T(8,128)(2,1)S(1)}) custom-call(s32[2,2,6]{2,1,0:T(2,128)S(1)} %stack.354.nums, bf16[1024,1024]{1,0:T(8,128)(2,1)S(1)} %copy-done.25, bf16[1024,1024]{1,0:T(8,128)(2,1)S(1)} %copy-done.23, ...), custom_call_target="tpu_custom_call" | custom-call | flops 2147483648 | bytes 1048576 | tf_op jit(solution)/shard_map/attention_backward/pallas_call | solution.py:222
  883.9 18.5 %grad_w_query.1 = (bf16[2048,1024]{1,0:T(8,128)(2,1)}, bf16[2,4,64,1024]{3,2,1,0:T(8,128)(2,1)}, bf16[2,4,64,1024]{3,2,1,0:T(8,128)(2,1)}) custom-call(s32[3]{0:T(128)} %pad_add_fusion.spot, bf16[1024,2048]{1,0:T(8,128)(2,1)} %get-tuple-element.172.a0_ref, bf16[1024,2048]{1,0:T(8,128)(2,1)} %collective-permute-done.10.a1_ref, bf16[1024,1024]{1,0:T(8,128)(2,1)} %copy-done.16, ...), custom_call_target="tpu_custom_call" | custom-call | flops 1073741824 | bytes 2621440 | tf_op jit(solution)/shard_map/grad_w_query/pallas_call | solution.py:372
  907.4 26.8 %reduce-scatter.6.cloned.1.call-done.refs_1_ = bf16[128,4096]{1,0:T(8,128)(2,1)} async-done(((bf16[512,4096]{1,0:T(8,128)(2,1)}), bf16[128,4096]{1,0:T(8,128)(2,1)}) %reduce-scatter.6.cloned.1.call-update) | async-done | bytes 1048592 | tf_op jit(solution)/shard_map/reduce_scatter | solution.py:669
  937.6 18.5 %grad_w_out.1 = (bf16[2048,1024]{1,0:T(8,128)(2,1)}, bf16[2,4,64,1024]{3,2,1,0:T(8,128)(2,1)}, bf16[2,4,64,1024]{3,2,1,0:T(8,128)(2,1)}) custom-call(s32[3]{0:T(128)} %pad_add_fusion.spot, bf16[1024,2048]{1,0:T(8,128)(2,1)} %copy-done.20, bf16[1024,2048]{1,0:T(8,128)(2,1)} %collective-permute-done.32.a_ref.a1_ref, bf16[1024,1024]{1,0:T(8,128)(2,1)} %copy-done.26, ...), custom_call_target="tpu_custom_call" | custom-call | flops 1073741824 | bytes 2621440 | tf_op jit(solution)/shard_map/grad_w_out/pallas_call | solution.py:372
  956.1 28.5 %collective-permute-done.42.second = bf16[2,1024,128]{2,1,0:T(8,128)(2,1)S(1)} collective-permute-done((bf16[2,1024,128]{2,1,0:T(8,128)(2,1)}, bf16[2,1024,128]{2,1,0:T(8,128)(2,1)S(1)}, u32[]{:S(2)}, u32[]{:S(2)}) %collective-permute-start.42) | collective-permute-done | bytes 524320 | tf_op jit(solution)/shard_map/ppermute | solution.py:962
  988.6 17.4 %mixed_out.7.refs_0_ = bf16[1024,2048]{1,0:T(8,128)(2,1)} custom-call(bf16[1024,4096]{1,0:T(8,128)(2,1)} %get-tuple-element.89.a0_ref.a_ref, bf16[2048,2048]{1,0:T(8,128)(2,1)} %all-gather.9.cloned.1.call-done.b_ref, f32[1024,2048]{1,0:T(8,128)} %copy-done.75, f32[1,2048]{1,0:T(1,128)S(1)} %reshape_reshape.18.refs_1_, ...), custom_call_target="tpu_custom_call" | custom-call | flops 1073741824 | bytes 2097152 | tf_op jit(solution)/shard_map/mixed_out/pallas_call | solution.py:323
  (650 shorter events, 551.9 us)
Async XLA Ops:
  7.2 162.6 %all-gather.5.cloned.1.call-start = ((), (), s32[]{:S(2)}) async-start(), calls=%async_computation.3 | async-start | bytes 9469952 | tf_op jit(solution)/shard_map/all_gather | solution.py:832
  12.0 335.0 %all-gather.7.cloned.1.call-start = ((), (), s32[]{:S(2)}) async-start(), calls=%async_computation.4 | async-start | bytes 17825792 | tf_op jit(solution)/shard_map/all_gather | solution.py:832
  18.2 449.6 %all-gather.11.cloned.1.call-start = ((), (), s32[]{:S(2)}) async-start(), calls=%async_computation.6 | async-start | bytes 8912896 | tf_op jit(solution)/shard_map/all_gather | solution.py:832
  19.3 583.6 %all-gather.9.cloned.1.call-start = ((), (), s32[]{:S(2)}) async-start(), calls=%async_computation.5 | async-start | bytes 8912896 | tf_op jit(solution)/shard_map/all_gather | solution.py:832
  89.4 756.6 %reduce-scatter.4.cloned.1.call-start = ((), (), s32[]{:S(2)}) async-start(), calls=%async_computation.7 | async-start | bytes 5242880 | tf_op jit(solution)/shard_map/reduce_scatter | solution.py:669
  248.1 129.1 %collective-permute-start.20 = (bf16[1024,2048]{1,0:T(8,128)(2,1)}, bf16[1024,2048]{1,0:T(8,128)(2,1)}, u32[]{:S(2)}, u32[]{:S(2)}) collective-permute-start(bf16[1024,2048]{1,0:T(8,128)(2,1)} %get-tuple-element.169.a_ref.a0_ref), channel_id=1, source_target_pairs={{0,1},{1,0},{2,3},{3,2},{4,5},{5,4},{6,7},{7,6},{8,9},{9,8},{10,11... | collective-permute-start | bytes 12582920 | tf_op jit(solution)/shard_map/ppermute | solution.py:460
  259.3 148.5 %collective-permute-start.21 = (bf16[1024,2048]{1,0:T(8,128)(2,1)}, bf16[1024,2048]{1,0:T(8,128)(2,1)}, u32[]{:S(2)}, u32[]{:S(2)}) collective-permute-start(bf16[1024,2048]{1,0:T(8,128)(2,1)} %bitcast_select_fusion.b0_ref.a_ref.base_ref), channel_id=1, source_target_pairs={{0,1},{1,0},{2,3},{3,2},{4,5},{5,4},{6,7},{7,6},{8,9},{9,8},{10,11... | collective-permute-start | bytes 12582920 | tf_op jit(solution)/shard_map/ppermute | solution.py:460
  436.1 144.5 %collective-permute-start.24 = (bf16[2,4,64,2048]{3,2,1,0:T(8,128)(2,1)}, bf16[2,4,64,2048]{3,2,1,0:T(8,128)(2,1)S(1)}, u32[]{:S(2)}, u32[]{:S(2)}) collective-permute-start(bf16[2,4,64,2048]{3,2,1,0:T(8,128)(2,1)} %get-tuple-element.94.refs_3_), channel_id=1, source_target_pairs={{0,16},{16,0},{1,17},{17,1},{2,18},{18,2},{3,19},{19,3},{4,20},{20... | collective-permute-start | bytes 6291464 | tf_op jit(solution)/shard_map/ppermute | solution.py:460
  437.6 144.4 %collective-permute-start.25 = (bf16[2,4,64,2048]{3,2,1,0:T(8,128)(2,1)}, bf16[2,4,64,2048]{3,2,1,0:T(8,128)(2,1)}, u32[]{:S(2)}, u32[]{:S(2)}) collective-permute-start(bf16[2,4,64,2048]{3,2,1,0:T(8,128)(2,1)} %get-tuple-element.95.refs_4_), channel_id=1, source_target_pairs={{0,8},{8,0},{1,9},{9,1},{2,10},{10,2},{3,11},{11,3},{4,12},{12,4},... | collective-permute-start | bytes 6291464 | tf_op jit(solution)/shard_map/ppermute | solution.py:460
  465.3 128.0 %collective-permute-start.22 = (bf16[2,4,64,2048]{3,2,1,0:T(8,128)(2,1)}, bf16[2,4,64,2048]{3,2,1,0:T(8,128)(2,1)}, u32[]{:S(2)}, u32[]{:S(2)}) collective-permute-start(bf16[2,4,64,2048]{3,2,1,0:T(8,128)(2,1)} %get-tuple-element.92.refs_1_), channel_id=1, source_target_pairs={{0,16},{16,0},{1,17},{17,1},{2,18},{18,2},{3,19},{19,3},{4,20},{20... | collective-permute-start | bytes 6291464 | tf_op jit(solution)/shard_map/ppermute | solution.py:460
  467.3 126.1 %collective-permute-start.23 = (bf16[2,4,64,2048]{3,2,1,0:T(8,128)(2,1)}, bf16[2,4,64,2048]{3,2,1,0:T(8,128)(2,1)}, u32[]{:S(2)}, u32[]{:S(2)}) collective-permute-start(bf16[2,4,64,2048]{3,2,1,0:T(8,128)(2,1)} %get-tuple-element.93.refs_2_), channel_id=1, source_target_pairs={{0,8},{8,0},{1,9},{9,1},{2,10},{10,2},{3,11},{11,3},{4,12},{12,4},... | collective-permute-start | bytes 6291464 | tf_op jit(solution)/shard_map/ppermute | solution.py:460
  591.8 67.3 %collective-permute-start.28 = (bf16[4,64,2048]{2,1,0:T(8,128)(2,1)S(1)}, bf16[4,64,2048]{2,1,0:T(8,128)(2,1)}, u32[]{:S(2)}, u32[]{:S(2)}) collective-permute-start(bf16[4,64,2048]{2,1,0:T(8,128)(2,1)S(1)} %get-tuple-element.106.refs_4_), channel_id=1, source_target_pairs={{0,8},{8,0},{1,9},{9,1},{2,10},{10,2},{3,11},{11,3},{4,12},{12,4},... | collective-permute-start | bytes 3145736 | tf_op jit(solution)/shard_map/ppermute | solution.py:460
  593.0 66.1 %collective-permute-start.29 = (bf16[4,64,2048]{2,1,0:T(8,128)(2,1)S(1)}, bf16[4,64,2048]{2,1,0:T(8,128)(2,1)}, u32[]{:S(2)}, u32[]{:S(2)}) collective-permute-start(bf16[4,64,2048]{2,1,0:T(8,128)(2,1)S(1)} %get-tuple-element.107.refs_5_), channel_id=1, source_target_pairs={{0,16},{16,0},{1,17},{17,1},{2,18},{18,2},{3,19},{19,3},{4,20},{20... | collective-permute-start | bytes 3145736 | tf_op jit(solution)/shard_map/ppermute | solution.py:460
  600.3 58.8 %collective-permute-start.26 = (bf16[4,64,2048]{2,1,0:T(8,128)(2,1)}, bf16[4,64,2048]{2,1,0:T(8,128)(2,1)}, u32[]{:S(2)}, u32[]{:S(2)}) collective-permute-start(bf16[4,64,2048]{2,1,0:T(8,128)(2,1)} %get-tuple-element.103.refs_2_), channel_id=1, source_target_pairs={{0,8},{8,0},{1,9},{9,1},{2,10},{10,2},{3,11},{11,3},{4,12},{12,4},... | collective-permute-start | bytes 3145736 | tf_op jit(solution)/shard_map/ppermute | solution.py:460
  602.3 56.8 %collective-permute-start.27 = (bf16[4,64,2048]{2,1,0:T(8,128)(2,1)S(1)}, bf16[4,64,2048]{2,1,0:T(8,128)(2,1)}, u32[]{:S(2)}, u32[]{:S(2)}) collective-permute-start(bf16[4,64,2048]{2,1,0:T(8,128)(2,1)S(1)} %get-tuple-element.104.refs_3_), channel_id=1, source_target_pairs={{0,16},{16,0},{1,17},{17,1},{2,18},{18,2},{3,19},{19,3},{4,20},{20... | collective-permute-start | bytes 3145736 | tf_op jit(solution)/shard_map/ppermute | solution.py:460
  667.9 266.3 %reduce-scatter.6.cloned.1.call-start = ((), (), s32[]{:S(2)}) async-start(), calls=%async_computation.8 | async-start | bytes 5242880 | tf_op jit(solution)/shard_map/reduce_scatter | solution.py:669
  684.1 62.9 %collective-permute-start.35 = (bf16[2,4,64,2048]{3,2,1,0:T(8,128)(2,1)}, bf16[2,4,64,2048]{3,2,1,0:T(8,128)(2,1)}, u32[]{:S(2)}, u32[]{:S(2)}) collective-permute-start(bf16[2,4,64,2048]{3,2,1,0:T(8,128)(2,1)} %get-tuple-element.111.refs_2_), channel_id=1, source_target_pairs={{0,16},{16,0},{1,17},{17,1},{2,18},{18,2},{3,19},{19,3},{4,20},{20... | collective-permute-start | bytes 6291464 | tf_op jit(solution)/shard_map/ppermute | solution.py:460
  685.3 61.7 %collective-permute-start.36 = (bf16[2,4,64,2048]{3,2,1,0:T(8,128)(2,1)}, bf16[2,4,64,2048]{3,2,1,0:T(8,128)(2,1)}, u32[]{:S(2)}, u32[]{:S(2)}) collective-permute-start(bf16[2,4,64,2048]{3,2,1,0:T(8,128)(2,1)} %get-tuple-element.112.refs_3_), channel_id=1, source_target_pairs={{0,8},{8,0},{1,9},{9,1},{2,10},{10,2},{3,11},{11,3},{4,12},{12,4},... | collective-permute-start | bytes 6291464 | tf_op jit(solution)/shard_map/ppermute | solution.py:460
  685.3 92.3 %collective-permute-start.33 = (bf16[2,4,64,2048]{3,2,1,0:T(8,128)(2,1)}, bf16[2,4,64,2048]{3,2,1,0:T(8,128)(2,1)S(1)}, u32[]{:S(2)}, u32[]{:S(2)}) collective-permute-start(bf16[2,4,64,2048]{3,2,1,0:T(8,128)(2,1)} %get-tuple-element.100.refs_1_), channel_id=1, source_target_pairs={{0,16},{16,0},{1,17},{17,1},{2,18},{18,2},{3,19},{19,3},{4,20},{20... | collective-permute-start | bytes 6291464 | tf_op jit(solution)/shard_map/ppermute | solution.py:460
  686.8 92.2 %collective-permute-start.34 = (bf16[2,4,64,2048]{3,2,1,0:T(8,128)(2,1)}, bf16[2,4,64,2048]{3,2,1,0:T(8,128)(2,1)}, u32[]{:S(2)}, u32[]{:S(2)}) collective-permute-start(bf16[2,4,64,2048]{3,2,1,0:T(8,128)(2,1)} %get-tuple-element.101.refs_2_), channel_id=1, source_target_pairs={{0,8},{8,0},{1,9},{9,1},{2,10},{10,2},{3,11},{11,3},{4,12},{12,4},... | collective-permute-start | bytes 6291464 | tf_op jit(solution)/shard_map/ppermute | solution.py:460
  756.1 57.1 %collective-permute-start.39 = (bf16[4,64,2048]{2,1,0:T(8,128)(2,1)S(1)}, bf16[4,64,2048]{2,1,0:T(8,128)(2,1)}, u32[]{:S(2)}, u32[]{:S(2)}) collective-permute-start(bf16[4,64,2048]{2,1,0:T(8,128)(2,1)S(1)} %get-tuple-element.122.refs_2_), channel_id=1, source_target_pairs={{0,8},{8,0},{1,9},{9,1},{2,10},{10,2},{3,11},{11,3},{4,12},{12,4},... | collective-permute-start | bytes 3145736 | tf_op jit(solution)/shard_map/ppermute | solution.py:460
  756.7 56.5 %collective-permute-start.40 = (bf16[4,64,2048]{2,1,0:T(8,128)(2,1)}, bf16[4,64,2048]{2,1,0:T(8,128)(2,1)}, u32[]{:S(2)}, u32[]{:S(2)}) collective-permute-start(bf16[4,64,2048]{2,1,0:T(8,128)(2,1)} %get-tuple-element.123.refs_3_), channel_id=1, source_target_pairs={{0,16},{16,0},{1,17},{17,1},{2,18},{18,2},{3,19},{19,3},{4,20},{20... | collective-permute-start | bytes 3145736 | tf_op jit(solution)/shard_map/ppermute | solution.py:460
  828.6 335.9 %reduce-scatter.8.cloned.1.call-start = ((), (), s32[]{:S(2)}) async-start(), calls=%async_computation.9 | async-start | bytes 1310720 | tf_op jit(solution)/shard_map/reduce_scatter | solution.py:669
  830.6 156.9 %collective-permute-start.30 = (bf16[1024,2048]{1,0:T(8,128)(2,1)}, bf16[1024,2048]{1,0:T(8,128)(2,1)}, u32[]{:S(2)}, u32[]{:S(2)}) collective-permute-start(bf16[1024,2048]{1,0:T(8,128)(2,1)} %mixed_out.6.refs_0_), channel_id=1, source_target_pairs={{0,1},{1,0},{2,3},{3,2},{4,5},{5,4},{6,7},{7,6},{8,9},{9,8},{10,11... | collective-permute-start | bytes 12582920 | tf_op jit(solution)/shard_map/ppermute | solution.py:460
  (195 other events, 2707.2 us)
Sparse Core Ops, SparseCore 0:
  12.1 141.1 all-gather.4
  156.0 190.9 all-gather.6
  350.4 116.3 all-gather.10
  469.4 131.1 all-gather.8
  668.0 74.0 reduce-scatter.3
  828.7 105.4 reduce-scatter.5
  1127.6 36.4 reduce-scatter.7
